TPU v7x, 128 devices: a whole 4x4x4 slice. The times are simulated.
128 devices in a mesh: frame: 8 (over x_lo, z), space: 16 (over y, x_hi, core).
Axes of the slice: x: 4 (x_hi: 2, x_lo: 2; x = x_hi * 2 + x_lo), y: 4, z: 4, core: 2. Of those that a mesh axis runs over, the one named last changes fastest.
Arguments:
- latents: float32 [8, 1024, 128], P('frame', 'space'), may hold values from -6 to 6
- fresh_noise: float32 [2, 1024, 128], P(None, 'space'), may hold values from -6 to 6
- level_index: int32 [8], replicated, may hold values from 0 to 47, as said below
- plan: int32 [48], replicated, may hold values from 1 to 999, as said below
- frame_ids: int32 [10], replicated, may hold values from 5003 to 5030, as said below
- in_weight: bfloat16 [128, 3072], replicated, may hold values from -0.5 to 0.5
- cond_gain: float32 [2, 3072], replicated, may hold values from 0.1 to 1.9
- norm_gain: float32 [3072], replicated, may hold values from 0.1 to 1.9
- qkv_weight: bfloat16 [3, 3072, 3072], P(None, None, 'space'), may hold values from -0.109375 to 0.109375
- qk_gain: float32 [2, 64], replicated, may hold values from 0.5 to 4
- out_weight: bfloat16 [3072, 3072], replicated, may hold values from -0.109375 to 0.109375
- final_gain: float32 [3072], replicated, may hold values from 0.1 to 1.9
- final_weight: bfloat16 [3072, 128], replicated, may hold values from -0.109375 to 0.109375
Outputs:
- estimates: float32 [2, 8, 1024, 128], P(None, 'frame', 'space')
- queue: float32 [8, 1024, 128], P('frame', 'space')
Inputs may be any that keep to these rules, and one draw needn't show every extreme that they name: `level_index`: strictly rising along the slots, from 0 in the first slot to 47 in the last. `plan`: strictly rising, from 1 to 999. `frame_ids`: strictly rising, in steps of 1 to 3, the last one 5000 + 3 * 10.
All inputs are finite; a program needn't handle non-finite values.
Results may differ from a plain program's by a relative error of at most 0.0095.
Values may be sent and summed in bfloat16 or wider, within the bound.
No kernel may reach another device: no remote copies, remote signals or barrier semaphores. Data moves between devices by JAX's collectives and lax.ppermute only.
A program may use at most 128 MiB of HBM per device.

v0:
```python
import math

import jax
import jax.numpy as jnp
from jax import lax
from jax.sharding import PartitionSpec as P

HEAD = 64
STEPS = 2


def passed_along(x, axis, by):
    peers = lax.axis_size(axis)
    pairs = [(i, i + by) for i in range(peers) if 0 <= i + by < peers]
    return lax.ppermute(x, axis, pairs)


def waves(stamp, width):
    half = width // 2
    freqs = jnp.exp(-math.log(10000.0) * jnp.arange(half, dtype=jnp.float32) / half)
    angle = stamp * freqs
    return jnp.concatenate([jnp.cos(angle), jnp.sin(angle)])


def rms_scale(values, gain):
    return values * lax.rsqrt(jnp.mean(values * values, axis=-1, keepdims=True) + 1e-06) * gain


def embed(latent_b, stamp, frame_id, in_weight, cond_gain, norm_gain):
    width = in_weight.shape[1]
    hidden = jnp.dot(latent_b, in_weight, preferred_element_type=jnp.float32)
    hidden = hidden + cond_gain[0] * waves(stamp, width) + cond_gain[1] * waves(frame_id, width)
    return (hidden, rms_scale(hidden, norm_gain).astype(jnp.bfloat16))


def project_heads(normed, weight, gain_row, factor):
    rows = normed.shape[0]
    raw = jnp.dot(normed, weight, preferred_element_type=jnp.float32).reshape(rows, -1, HEAD)
    return (rms_scale(raw, gain_row) * factor).astype(jnp.bfloat16)


def keys_values(normed, qkv_weight, qk_gain):
    rows = normed.shape[0]
    key = project_heads(normed, qkv_weight[1], qk_gain[1], 1.0)
    value = jnp.dot(normed, qkv_weight[2], preferred_element_type=jnp.float32)
    return (key, value.astype(jnp.bfloat16).reshape(rows, -1, HEAD))


def attend(query, key, value, bias):
    rows = query.shape[0]
    size = min(512, rows)
    blocks = query.reshape(rows // size, size, query.shape[1], query.shape[2])

    def one_block(block):
        scores = jnp.einsum("qhd,khd->hqk", block, key, preferred_element_type=jnp.float32) + bias
        weights = jax.nn.softmax(scores, axis=-1).astype(jnp.bfloat16)
        return jnp.einsum(
            "hqk,khd->qhd", weights, value, preferred_element_type=jnp.float32
        ).astype(jnp.bfloat16)

    return lax.map(one_block, blocks).reshape(rows, -1)


def pick(table, where):
    return jnp.sum(jnp.where(jnp.arange(table.shape[0]) == where, table, 0))


def shards(
    latents,
    fresh_noise,
    level_index,
    plan,
    frame_ids,
    in_weight,
    cond_gain,
    norm_gain,
    qkv_weight,
    qk_gain,
    out_weight,
    final_gain,
    final_weight,
):
    slot = lax.axis_index("frame")
    count = lax.axis_size("frame")
    place = lax.axis_index("space")
    before = jnp.maximum(slot - 1, 0)
    stamp_now = pick(plan, pick(level_index, slot)).astype(jnp.float32)
    stamp_prev = pick(plan, pick(level_index, before)).astype(jnp.float32)
    sigma = stamp_now / 1000.0
    sigma_next = jnp.where(slot > 0, stamp_prev / 1000.0, jnp.float32(0.0))
    scale = 1.0 / math.sqrt(HEAD)
    state = latents[0]
    tok_rows = state.shape[0]
    results = []
    for step in range(STEPS):
        latent_b = state.astype(jnp.bfloat16)
        id_now = pick(frame_ids, slot + step).astype(jnp.float32)
        id_prev = pick(frame_ids, before + step).astype(jnp.float32)
        prev_b = passed_along(latent_b, "frame", 1)
        whole, prev_whole = (
            lax.all_gather(latent_b, "space", axis=0, tiled=True),
            lax.all_gather(prev_b, "space", axis=0, tiled=True),
        )
        hidden, normed = embed(whole, stamp_now, id_now, in_weight, cond_gain, norm_gain)
        query = project_heads(normed, qkv_weight[0], qk_gain[0], scale)
        key, value = keys_values(normed, qkv_weight, qk_gain)
        unused, prev_normed = embed(
            prev_whole, stamp_prev, id_prev, in_weight, cond_gain, norm_gain
        )
        prev_key, prev_value = keys_values(prev_normed, qkv_weight, qk_gain)
        group_rows = key.shape[0]
        key_all = jnp.concatenate([key, prev_key], axis=0)
        value_all = jnp.concatenate([value, prev_value], axis=0)
        later = jnp.arange(2 * group_rows) >= group_rows
        bias = jnp.where(jnp.logical_and(later, slot == 0), jnp.float32(-1e30), jnp.float32(0.0))
        attended = attend(query, key_all, value_all, bias)
        regrouped = lax.all_to_all(attended, "space", split_axis=0, concat_axis=1, tiled=True)
        own_hidden = lax.dynamic_slice_in_dim(hidden, place * tok_rows, tok_rows, 0)
        mixed = own_hidden + jnp.dot(regrouped, out_weight, preferred_element_type=jnp.float32)
        velocity = jnp.dot(
            rms_scale(mixed, final_gain).astype(jnp.bfloat16),
            final_weight,
            preferred_element_type=jnp.float32,
        )
        results.append(state - sigma * velocity)
        renewed = state + (sigma_next - sigma) * velocity
        moved = passed_along(renewed.astype(jnp.bfloat16), "frame", -1).astype(renewed.dtype)
        state = jnp.where(slot == count - 1, fresh_noise[step], moved)
    estimates = jnp.stack(results)[:, None]
    return (estimates, state[None])


def solution(mesh):
    in_specs = (
        P("frame", "space", None),
        P(None, "space", None),
        P(),
        P(),
        P(),
        P(),
        P(),
        P(),
        P(None, None, "space"),
        P(),
        P(),
        P(),
        P(),
    )
    out_specs = (P(None, "frame", "space", None), P("frame", "space", None))
    return jax.shard_map(shards, mesh=mesh, in_specs=in_specs, out_specs=out_specs, check_vma=False)
```

profile of v0, /device:TPU:0, one launch (start us, length us, event | category | flops | bytes accessed | tf_op | source)
XLA Modules:
  0.0 316.2 jit_solution(13860814906823973382)
XLA Ops:
  0.6 0.8 bitcast_convert_fusion
  1.5 3.9 %collective-permute-start = (bf16[64,128]{1,0:T(8,128)(2,1)S(1)}, bf16[64,128]{1,0:T(8,128)(2,1)S(1)}, u32[]{:S(2)}, u32[]{:S(2)}) collective-permute-start(bf16[64,128]{1,0:T(8,128)(2,1)S(1)} %bitcast_convert_fusion), channel_id=1, source_target_pairs={{0,16},{16,32},{32,48},{48,64},{64,80},{80,96},{96,112},{1,17},{17... | collective-permute-start | bytes 49160 | tf_op jit(solution)/shard_map/ppermute | solution.py:15
  5.4 25.5 %all_gather.12 = bf16[1024,128]{1,0:T(8,128)(2,1)S(1)} all-gather(bf16[64,128]{1,0:T(8,128)(2,1)S(1)} %bitcast_convert_fusion), channel_id=1, replica_groups=mesh['frame'=8,'space'=16] {'space'}, dimensions={0}, use_global_device_ids=true | all-gather | bytes 278528 | tf_op jit(solution)/shard_map/all_gather | solution.py:101
  30.8 1.4 fusion.93
  32.2 2.7 fusion.94
  36.5 1.4 fusion.97
  41.3 0.9 maximum_multiply_fusion.5
  42.3 5.7 %multiply_reduce_fusion.3 = (f32[1024]{0:T(1024)S(1)}, f32[1024,3072]{1,0:T(8,128)}) fusion(f32[3072]{0:T(1024)S(1)} %bitcast.212, f32[3072]{0:T(1024)S(1)} %bitcast.205, bf16[1024,128]{1,0:T(8,128)(2,1)S(1)} %all_gather.12, bf16[128,3072]{1,0:T(8,128)(2,1)S(1)} %copy-done), kind=kOutput, calls=%fused_computation.54 | convolution fusion | flops 817888256 | bytes 13660160 | tf_op jit(solution)/shard_map/dot_general | solution.py:31
  48.1 20.5 %all_gather.13 = bf16[1024,128]{1,0:T(8,128)(2,1)S(1)} all-gather(bf16[64,128]{1,0:T(8,128)(2,1)S(1)} %collective-permute-done), channel_id=1, replica_groups=mesh['frame'=8,'space'=16] {'space'}, dimensions={0}, use_global_device_ids=true | all-gather | bytes 278528 | tf_op jit(solution)/shard_map/all_gather | solution.py:102
  68.7 7.2 %multiply_reduce_fusion.2 = (f32[1024]{0:T(1024)S(1)}, f32[1024,3072]{1,0:T(8,128)}) fusion(f32[3072]{0:T(1024)S(1)} %bitcast.209, f32[3072]{0:T(1024)S(1)} %bitcast.195, bf16[1024,128]{1,0:T(8,128)(2,1)S(1)} %all_gather.13, bf16[128,3072]{1,0:T(8,128)(2,1)S(1)} %copy-done), kind=kOutput, calls=%fused_computation.51 | convolution fusion | flops 817888256 | bytes 13660160 | tf_op jit(solution)/shard_map/dot_general | solution.py:31
  75.9 1.7 copy-done.2
  77.6 10.5 %multiply_convert_fusion.2 = (bf16[1024,3072]{1,0:T(8,128)(2,1)}, bf16[1024,3072]{1,0:T(8,128)(2,1)S(1)}) fusion(f32[1024,3072]{1,0:T(8,128)} %get-tuple-element.199, f32[1024]{0:T(1024)S(1)} %add_rsqrt_fusion.8, f32[3072]{0:T(1024)S(1)} %bitcast.210, f32[3072]{0:T(1024)S(1)} %bitcast.196, f32[3072]{0:T(1024)S(1)} %copy-done.16, ...), kind=kLoop, calls=%fused_computation.50 | loop fusion | flops 25165824 | bytes 37793792 | tf_op jit(solution)/shard_map/convert_element_type | solution.py:33
  88.1 2.2 convolution_convert_fusion.3
  90.9 2.2 convolution_convert_fusion.2
  93.1 2.2 multiply_reduce_fusion.9
  95.4 2.2 multiply_reduce_fusion.10
  97.6 2.2 multiply_reduce_fusion.11
  101.4 31.6 %while.22 = (s32[]{:T(128)}, bf16[2,512,3,64]{1,3,2,0:T(8,128)(2,1)S(1)}, bf16[2,512,3,64]{1,3,2,0:T(8,128)(2,1)}, bf16[2048,3,64]{0,2,1:T(8,128)(2,1)S(1)}, bf1...) while((s32[]{:T(128)}, bf16[2,512,3,64]{1,3,2,0:T(8,128)(2,1)S(1)}, ...), condition=%wide.region_14.15_spmd.clone, body=%wide.region_11.14_spmd.clone.sunk | while | flops 821141504 | bytes 27163216 | solution.py:61
  101.6 9.0 %fusion.155 = (f32[3,512]{1,0:T(4,128)S(1)}, f32[3,512,2048]{2,1,0:T(8,128)}) fusion(f32[2048]{0:T(1024)S(1)} %fusion.154, bf16[2048,3,64]{0,2,1:T(8,128)(2,1)S(1)} %get-tuple-element.333, bf16[2,512,3,64]{1,3,2,0:T(8,128)(2,1)} %get-tuple-element.332, s32[]{:T(128)} %get-tuple-element.323), kind=kOutput, calls=%fused_computation.171.clone.1 | convolution fusion | flops 412092416 | bytes 13580800 | tf_op jit(solution)/shard_map/while/body/eval_jaxpr/sub | solution.py:56
  110.6 6.7 %fusion.156 = bf16[2,512,3,64]{1,3,2,0:T(8,128)(2,1)S(1)} fusion(bf16[2,512,3,64]{1,3,2,0:T(8,128)(2,1)S(1)} %get-tuple-element.324, s32[]{:T(128)} %get-tuple-element.323, bf16[2048,3,64]{0,2,1:T(8,128)(2,1)S(1)} %get-tuple-element.334, f32[3,512,2048]{2,1,0:T(8,128)} %get-tuple-element.306, f32[3,512]{1,0:T(4,128)S(1)} %get-tuple-element.307), kind=kOutput, calls=%fused_computation.12.clone.1 | convolution fusion | flops 409042944 | bytes 13574148 | tf_op jit(solution)/shard_map/while/body/eval_jaxpr/hqk,khd->qhd/dot_general | solution.py:57
  117.3 9.0 %fusion.155 = (f32[3,512]{1,0:T(4,128)S(1)}, f32[3,512,2048]{2,1,0:T(8,128)}) fusion(f32[2048]{0:T(1024)S(1)} %fusion.154, bf16[2048,3,64]{0,2,1:T(8,128)(2,1)S(1)} %get-tuple-element.333, bf16[2,512,3,64]{1,3,2,0:T(8,128)(2,1)} %get-tuple-element.332, s32[]{:T(128)} %get-tuple-element.323), kind=kOutput, calls=%fused_computation.171.clone.1 | convolution fusion | flops 412092416 | bytes 13580800 | tf_op jit(solution)/shard_map/while/body/eval_jaxpr/sub | solution.py:56
  126.3 6.7 %fusion.156 = bf16[2,512,3,64]{1,3,2,0:T(8,128)(2,1)S(1)} fusion(bf16[2,512,3,64]{1,3,2,0:T(8,128)(2,1)S(1)} %get-tuple-element.324, s32[]{:T(128)} %get-tuple-element.323, bf16[2048,3,64]{0,2,1:T(8,128)(2,1)S(1)} %get-tuple-element.334, f32[3,512,2048]{2,1,0:T(8,128)} %get-tuple-element.306, f32[3,512]{1,0:T(4,128)S(1)} %get-tuple-element.307), kind=kOutput, calls=%fused_computation.12.clone.1 | convolution fusion | flops 409042944 | bytes 13574148 | tf_op jit(solution)/shard_map/while/body/eval_jaxpr/hqk,khd->qhd/dot_general | solution.py:57
  133.7 1.4 reshape.226
  135.0 4.6 %all-to-all-start = ((bf16[16,64,192]{2,1,0:T(8,128)(2,1)}), bf16[16,64,192]{2,1,0:T(8,128)(2,1)S(1)}, u32[]{:S(2)}, u32[]{:S(2)}) async-start(bf16[16,64,192]{2,1,0:T(8,128)(2,1)} %reshape.226), calls=%async_computation | async-start | bytes 1048576 | tf_op jit(solution)/shard_map/all_to_all | solution.py:117
  139.6 12.3 %all-to-all-done = bf16[16,64,192]{2,1,0:T(8,128)(2,1)S(1)} async-done(((bf16[16,64,192]{2,1,0:T(8,128)(2,1)}), bf16[16,64,192]{2,1,0:T(8,128)(2,1)S(1)}, u32[]{:S(2)}, u32[]{:S(2)}) %all-to-all-start) | async-done | bytes 393248 | tf_op jit(solution)/shard_map/all_to_all | solution.py:117
  152.9 10.1 %multiply_reduce_fusion.8 = (f32[64]{0:T(128)S(1)}, f32[64,3072]{1,0:T(8,128)S(1)}) fusion(bf16[64,3072]{1,0:T(8,128)(2,1)S(1)} %all_to_all.31, bf16[3072,3072]{1,0:T(8,128)(2,1)} %param.27, f32[1024,3072]{1,0:T(8,128)} %get-tuple-element.201, s32[]{:T(128)S(6)} %select_n.55), kind=kOutput, calls=%fused_computation.91 | convolution fusion | flops 1208549376 | bytes 20840708 | tf_op jit(solution)/shard_map/dot_general | solution.py:119
  163.3 1.3 collective-permute-start.1
  164.6 4.3 %collective-permute-done.1 = bf16[64,128]{1,0:T(8,128)(2,1)S(1)} collective-permute-done((bf16[64,128]{1,0:T(8,128)(2,1)S(1)}, bf16[64,128]{1,0:T(8,128)(2,1)S(1)}, u32[]{:S(2)}, u32[]{:S(2)}) %collective-permute-start.1) | collective-permute-done | bytes 16416 | tf_op jit(solution)/shard_map/ppermute | solution.py:15
  169.0 20.8 %all_gather.14 = bf16[1024,128]{1,0:T(8,128)(2,1)S(1)} all-gather(bf16[64,128]{1,0:T(8,128)(2,1)S(1)} %fusion.89), channel_id=1, replica_groups=mesh['frame'=8,'space'=16] {'space'}, dimensions={0}, use_global_device_ids=true | all-gather | bytes 278528 | tf_op jit(solution)/shard_map/all_gather | solution.py:101
  189.8 3.8 %collective-permute-start.2 = (bf16[64,128]{1,0:T(8,128)(2,1)S(1)}, bf16[64,128]{1,0:T(8,128)(2,1)S(1)}, u32[]{:S(2)}, u32[]{:S(2)}) collective-permute-start(bf16[64,128]{1,0:T(8,128)(2,1)S(1)} %fusion.89), channel_id=1, source_target_pairs={{0,16},{16,32},{32,48},{48,64},{64,80},{80,96},{96,112},{1,17},{17... | collective-permute-start | bytes 49160 | tf_op jit(solution)/shard_map/ppermute | solution.py:15
  193.6 2.1 multiply_reduce_fusion.1
  195.7 23.1 %all_gather.15 = bf16[1024,128]{1,0:T(8,128)(2,1)S(1)} all-gather(bf16[64,128]{1,0:T(8,128)(2,1)S(1)} %collective-permute-done.2), channel_id=1, replica_groups=mesh['frame'=8,'space'=16] {'space'}, dimensions={0}, use_global_device_ids=true | all-gather | bytes 278528 | tf_op jit(solution)/shard_map/all_gather | solution.py:102
  218.8 5.5 %multiply_reduce_fusion = (f32[1024]{0:T(1024)S(1)}, f32[1024,3072]{1,0:T(8,128)}) fusion(f32[3072]{0:T(1024)S(1)} %bitcast.207, f32[3072]{0:T(1024)S(1)} %bitcast.197, bf16[1024,128]{1,0:T(8,128)(2,1)S(1)} %all_gather.15, bf16[128,3072]{1,0:T(8,128)(2,1)S(1)} %copy-done), kind=kOutput, calls=%fused_computation.45 | convolution fusion | flops 817888256 | bytes 13660160 | tf_op jit(solution)/shard_map/dot_general | solution.py:31
  224.3 10.5 %multiply_convert_fusion = (bf16[1024,3072]{1,0:T(8,128)(2,1)}, bf16[1024,3072]{1,0:T(8,128)(2,1)S(1)}) fusion(f32[1024,3072]{1,0:T(8,128)} %get-tuple-element.211, f32[1024]{0:T(1024)S(1)} %add_rsqrt_fusion.6, f32[3072]{0:T(1024)S(1)} %bitcast.208, f32[3072]{0:T(1024)S(1)} %bitcast.198, f32[3072]{0:T(1024)S(1)} %copy-done.16, ...), kind=kLoop, calls=%fused_computation.44 | loop fusion | flops 25165824 | bytes 37793792 | tf_op jit(solution)/shard_map/convert_element_type | solution.py:33
  234.8 5.1 %convolution_convert_fusion = bf16[1024,192]{0,1:T(8,128)(2,1)S(1)} fusion(bf16[1024,3072]{1,0:T(8,128)(2,1)} %get-tuple-element.188, bf16[3,3072,192]{1,2,0:T(8,128)(2,1)S(1)} %copy-done.9), kind=kOutput, calls=%fused_computation.70 | convolution fusion | flops 1208156160 | bytes 7864320 | tf_op jit(solution)/shard_map/dot_general | solution.py:45
  240.0 2.3 multiply_reduce_fusion.5
  242.3 2.2 convolution_convert_fusion.1
  244.5 2.2 multiply_reduce_fusion.6
  246.7 2.2 multiply_reduce_fusion.7
  250.5 31.5 %while.23 = (s32[]{:T(128)}, bf16[2,512,3,64]{1,3,2,0:T(8,128)(2,1)S(1)}, bf16[2,512,3,64]{1,3,2,0:T(8,128)(2,1)}, bf16[2048,3,64]{0,2,1:T(8,128)(2,1)S(1)}, bf1...) while((s32[]{:T(128)}, bf16[2,512,3,64]{1,3,2,0:T(8,128)(2,1)S(1)}, ...), condition=%wide.region_26.27_spmd.clone, body=%wide.region_23.26_spmd.clone.sunk | while | flops 821141504 | bytes 27163216 | solution.py:61
  250.7 9.0 %fusion.161 = (f32[3,512]{1,0:T(4,128)S(1)}, f32[3,512,2048]{2,1,0:T(8,128)}) fusion(f32[2048]{0:T(1024)S(1)} %fusion.160, bf16[2048,3,64]{0,2,1:T(8,128)(2,1)S(1)} %get-tuple-element.354, bf16[2,512,3,64]{1,3,2,0:T(8,128)(2,1)} %get-tuple-element.353, s32[]{:T(128)} %get-tuple-element.344), kind=kOutput, calls=%fused_computation.172.clone.1 | convolution fusion | flops 412092416 | bytes 13580800 | tf_op jit(solution)/shard_map/while/body/eval_jaxpr/sub | solution.py:56
  259.7 6.7 %fusion.162 = bf16[2,512,3,64]{1,3,2,0:T(8,128)(2,1)S(1)} fusion(bf16[2,512,3,64]{1,3,2,0:T(8,128)(2,1)S(1)} %get-tuple-element.345, s32[]{:T(128)} %get-tuple-element.344, bf16[2048,3,64]{0,2,1:T(8,128)(2,1)S(1)} %get-tuple-element.355, f32[3,512,2048]{2,1,0:T(8,128)} %get-tuple-element.314, f32[3,512]{1,0:T(4,128)S(1)} %get-tuple-element.315), kind=kOutput, calls=%fused_computation.33.clone.1 | convolution fusion | flops 409042944 | bytes 13574148 | tf_op jit(solution)/shard_map/while/body/eval_jaxpr/hqk,khd->qhd/dot_general | solution.py:57
  266.4 9.0 %fusion.161 = (f32[3,512]{1,0:T(4,128)S(1)}, f32[3,512,2048]{2,1,0:T(8,128)}) fusion(f32[2048]{0:T(1024)S(1)} %fusion.160, bf16[2048,3,64]{0,2,1:T(8,128)(2,1)S(1)} %get-tuple-element.354, bf16[2,512,3,64]{1,3,2,0:T(8,128)(2,1)} %get-tuple-element.353, s32[]{:T(128)} %get-tuple-element.344), kind=kOutput, calls=%fused_computation.172.clone.1 | convolution fusion | flops 412092416 | bytes 13580800 | tf_op jit(solution)/shard_map/while/body/eval_jaxpr/sub | solution.py:56
  275.4 6.7 %fusion.162 = bf16[2,512,3,64]{1,3,2,0:T(8,128)(2,1)S(1)} fusion(bf16[2,512,3,64]{1,3,2,0:T(8,128)(2,1)S(1)} %get-tuple-element.345, s32[]{:T(128)} %get-tuple-element.344, bf16[2048,3,64]{0,2,1:T(8,128)(2,1)S(1)} %get-tuple-element.355, f32[3,512,2048]{2,1,0:T(8,128)} %get-tuple-element.314, f32[3,512]{1,0:T(4,128)S(1)} %get-tuple-element.315), kind=kOutput, calls=%fused_computation.33.clone.1 | convolution fusion | flops 409042944 | bytes 13574148 | tf_op jit(solution)/shard_map/while/body/eval_jaxpr/hqk,khd->qhd/dot_general | solution.py:57
  283.4 15.0 %all_to_all.38 = bf16[16,64,192]{2,1,0:T(8,128)(2,1)S(1)} all-to-all(bf16[16,64,192]{2,1,0:T(8,128)(2,1)S(1)} %reshape.227), channel_id=1, replica_groups=mesh['frame'=8,'space'=16] {'space'}, dimensions={0} | all-to-all | bytes 786432 | tf_op jit(solution)/shard_map/all_to_all | solution.py:117
  299.3 10.1 %multiply_reduce_fusion.4 = (f32[64]{0:T(128)S(1)}, f32[64,3072]{1,0:T(8,128)S(1)}) fusion(bf16[64,3072]{1,0:T(8,128)(2,1)S(1)} %all_to_all.35, bf16[3072,3072]{1,0:T(8,128)(2,1)} %param.27, f32[1024,3072]{1,0:T(8,128)} %copy-done.3, s32[]{:T(128)S(6)} %select_n.55), kind=kOutput, calls=%fused_computation.83 | convolution fusion | flops 1208549376 | bytes 20840708 | tf_op jit(solution)/shard_map/dot_general | solution.py:119
  309.7 1.3 collective-permute-start.3
  311.7 3.7 %collective-permute-done.3 = bf16[64,128]{1,0:T(8,128)(2,1)S(1)} collective-permute-done((bf16[64,128]{1,0:T(8,128)(2,1)S(1)}, bf16[64,128]{1,0:T(8,128)(2,1)S(1)}, u32[]{:S(2)}, u32[]{:S(2)}) %collective-permute-start.3) | collective-permute-done | bytes 16416 | tf_op jit(solution)/shard_map/ppermute | solution.py:15
  (87 shorter events, 10.8 us)
Async XLA Ops:
  0.6 41.6 %copy-start = (bf16[128,3072]{1,0:T(8,128)(2,1)S(1)}, bf16[128,3072]{1,0:T(8,128)(2,1)}, u32[]{:S(2)}) copy-start(bf16[128,3072]{1,0:T(8,128)(2,1)} %param.22) | copy-start | bytes 2359300
  1.5 46.7 %collective-permute-start = (bf16[64,128]{1,0:T(8,128)(2,1)S(1)}, bf16[64,128]{1,0:T(8,128)(2,1)S(1)}, u32[]{:S(2)}, u32[]{:S(2)}) collective-permute-start(bf16[64,128]{1,0:T(8,128)(2,1)S(1)} %bitcast_convert_fusion), channel_id=1, source_target_pairs={{0,16},{16,32},{32,48},{48,64},{64,80},{80,96},{96,112},{1,17},{17... | collective-permute-start | bytes 49160 | tf_op jit(solution)/shard_map/ppermute | solution.py:15
  42.2 5.7 %copy-start.7 = (bf16[3,3072,192]{1,2,0:T(8,128)(2,1)S(1)}, bf16[3,3072,192]{1,2,0:T(8,128)(2,1)}, u32[]{:S(2)}) copy-start(bf16[3,3072,192]{1,2,0:T(8,128)(2,1)} %param.25) | copy-start | bytes 10616836
  42.2 5.8 %copy-start.18 = (f32[2,64]{1,0:T(2,128)S(1)}, f32[2,64]{1,0:T(2,128)}, u32[]{:S(2)}) copy-start(f32[2,64]{1,0:T(2,128)} %param.26) | copy-start | bytes 1540
  48.1 47.2 %copy-start.12 = (bf16[1,3072,192]{1,2,0:T(8,128)(2,1)}, bf16[1,3072,192]{1,2,0:T(8,128)(2,1)S(1)}, u32[]{:S(2)}) copy-start(bf16[1,3072,192]{1,2,0:T(8,128)(2,1)S(1)} %get-tuple-element.176) | copy-start | bytes 3538948
  48.1 49.5 %copy-start.10 = (bf16[1,3072,192]{1,2,0:T(8,128)(2,1)}, bf16[1,3072,192]{1,2,0:T(8,128)(2,1)S(1)}, u32[]{:S(2)}) copy-start(bf16[1,3072,192]{1,2,0:T(8,128)(2,1)S(1)} %get-tuple-element.177) | copy-start | bytes 3538948
  68.7 8.9 %copy-start.2 = (f32[1024,3072]{1,0:T(8,128)S(1)}, f32[1024,3072]{1,0:T(8,128)}, u32[]{:S(2)}) copy-start(f32[1024,3072]{1,0:T(8,128)} %get-tuple-element.201) | copy-start | bytes 37748740
  68.7 8.9 %copy-start.16 = (f32[3072]{0:T(1024)S(1)}, f32[3072]{0:T(1024)}, u32[]{:S(2)}) copy-start(f32[3072]{0:T(1024)} %param.24) | copy-start | bytes 36868
  77.6 10.5 %copy-start.8 = (bf16[3,3072,192]{1,2,0:T(8,128)(2,1)S(1)}, bf16[3,3072,192]{1,2,0:T(8,128)(2,1)}, u32[]{:S(2)}) copy-start(bf16[3,3072,192]{1,2,0:T(8,128)(2,1)} %param.25) | copy-start | bytes 10616836
  88.1 2.8 copy-start.4
  135.0 16.9 %all-to-all-start = ((bf16[16,64,192]{2,1,0:T(8,128)(2,1)}), bf16[16,64,192]{2,1,0:T(8,128)(2,1)S(1)}, u32[]{:S(2)}, u32[]{:S(2)}) async-start(bf16[16,64,192]{2,1,0:T(8,128)(2,1)} %reshape.226), calls=%async_computation | async-start | bytes 1048576 | tf_op jit(solution)/shard_map/all_to_all | solution.py:117
  152.8 10.1 %copy-start.6 = (bf16[3072,128]{1,0:T(8,128)(2,1)S(1)}, bf16[3072,128]{1,0:T(8,128)(2,1)}, u32[]{:S(2)}) copy-start(bf16[3072,128]{1,0:T(8,128)(2,1)} %param.29) | copy-start | bytes 2359300
  152.8 10.1 %copy-start.14 = (f32[1,64,128]{2,1,0:T(8,128)S(1)}, f32[1,64,128]{2,1,0:T(8,128)}, u32[]{:S(2)}) copy-start(f32[1,64,128]{2,1,0:T(8,128)} %param.17) | copy-start | bytes 98308
  152.9 10.1 %copy-start.17 = (f32[3072]{0:T(1024)S(1)}, f32[3072]{0:T(1024)}, u32[]{:S(2)}) copy-start(f32[3072]{0:T(1024)} %param.28) | copy-start | bytes 36868
  152.9 16.1 %copy-start.15 = (f32[2,64,128]{2,1,0:T(8,128)S(1)}, f32[2,64,128]{2,1,0:T(8,128)}, u32[]{:S(2)}) copy-start(f32[2,64,128]{2,1,0:T(8,128)} %param.18) | copy-start | bytes 196612
  163.3 5.6 %collective-permute-start.1 = (bf16[64,128]{1,0:T(8,128)(2,1)S(1)}, bf16[64,128]{1,0:T(8,128)(2,1)S(1)}, u32[]{:S(2)}, u32[]{:S(2)}) collective-permute-start(bf16[64,128]{1,0:T(8,128)(2,1)S(1)} %get-tuple-element.181), channel_id=1, source_target_pairs={{16,0},{32,16},{48,32},{64,48},{80,64},{96,80},{112,96},{17,1},{33... | collective-permute-start | bytes 49160 | tf_op jit(solution)/shard_map/ppermute | solution.py:15
  189.8 5.9 %collective-permute-start.2 = (bf16[64,128]{1,0:T(8,128)(2,1)S(1)}, bf16[64,128]{1,0:T(8,128)(2,1)S(1)}, u32[]{:S(2)}, u32[]{:S(2)}) collective-permute-start(bf16[64,128]{1,0:T(8,128)(2,1)S(1)} %fusion.89), channel_id=1, source_target_pairs={{0,16},{16,32},{32,48},{48,64},{64,80},{80,96},{96,112},{1,17},{17... | collective-permute-start | bytes 49160 | tf_op jit(solution)/shard_map/ppermute | solution.py:15
  195.7 28.7 %copy-start.3 = (f32[1024,3072]{1,0:T(8,128)}, f32[1024,3072]{1,0:T(8,128)S(1)}, u32[]{:S(2)}) copy-start(f32[1024,3072]{1,0:T(8,128)S(1)} %get-tuple-element.213) | copy-start | bytes 37748740
  224.3 10.5 %copy-start.9 = (bf16[3,3072,192]{1,2,0:T(8,128)(2,1)S(1)}, bf16[3,3072,192]{1,2,0:T(8,128)(2,1)}, u32[]{:S(2)}) copy-start(bf16[3,3072,192]{1,2,0:T(8,128)(2,1)} %param.25) | copy-start | bytes 10616836
  234.8 5.2 %copy-start.5 = (bf16[1024,3072]{1,0:T(8,128)(2,1)S(1)}, bf16[1024,3072]{1,0:T(8,128)(2,1)}, u32[]{:S(2)}) copy-start(bf16[1024,3072]{1,0:T(8,128)(2,1)} %get-tuple-element.188) | copy-start | bytes 18874372
  234.8 5.2 %copy-start.13 = (bf16[1,3072,192]{1,2,0:T(8,128)(2,1)S(1)}, bf16[1,3072,192]{1,2,0:T(8,128)(2,1)}, u32[]{:S(2)}) copy-start(bf16[1,3072,192]{1,2,0:T(8,128)(2,1)} %copy-done.12) | copy-start | bytes 3538948
  244.5 2.3 copy-start.11
  299.3 16.7 %copy-start.1 = (bf16[128,3072]{1,0:T(8,128)(2,1)S(1)}, bf16[128,3072]{1,0:T(8,128)(2,1)}, u32[]{:S(2)}) copy-start(bf16[128,3072]{1,0:T(8,128)(2,1)} %param.22) | copy-start | bytes 2359300
  309.7 5.6 %collective-permute-start.3 = (bf16[64,128]{1,0:T(8,128)(2,1)S(1)}, bf16[64,128]{1,0:T(8,128)(2,1)S(1)}, u32[]{:S(2)}, u32[]{:S(2)}) collective-permute-start(bf16[64,128]{1,0:T(8,128)(2,1)S(1)} %get-tuple-element.178), channel_id=1, source_target_pairs={{16,0},{32,16},{48,32},{64,48},{80,64},{96,80},{112,96},{17,1},{33... | collective-permute-start | bytes 49160 | tf_op jit(solution)/shard_map/ppermute | solution.py:15
where the time goes:
time: 322 us; the launch traced here: 316 us
  matrix products  129 us (40%)
  blocking collectives  105 us (33%)
  other arithmetic  32 us (10%)
  waiting for transfers between devices  20.4 us (6%)
  starting transfers between devices  14.9 us (5%)
  local copies, waits for them, and re-layouts  9.33 us (3%)
  between operations  5.18 us (2%)
    all_gather x2, blocking collectives, shards(): lax.all_gather(latent_b, 'space', axis=0, tiled=True)  46.3 us
    all_gather x2, blocking collectives, shards(): lax.all_gather(prev_b, 'space', axis=0, tiled=True)  43.6 us
    sub x4, matrix products, one_block(): weights = jax.nn.softmax(scores, axis=-1).astype(jnp.bfloat16)  35.9 us
    dot_general x4, matrix products, one_block(): jnp.einsum('hqk,khd->qhd', weights, value, preferred_element_type=jnp.flo...  26.6 us
    convert_element_type x2, other arithmetic, embed(): return (hidden, rms_scale(hidden, norm_gain).astype(jnp.bfloat16))  21 us
    dot_general x4, matrix products, embed(): hidden = jnp.dot(latent_b, in_weight, preferred_element_type=jnp.float32)  20.5 us
    dot_general x2, matrix products, shards(): jnp.dot(regrouped, out_weight, preferred_element_type=jnp.float32)  20.2 us
    all_to_all x1, blocking collectives, shards(): lax.all_to_all(attended, 'space', split_axis=0, concat_axis=1, tiled=True)  15 us
  transfers between devices with their start and end apart: 5, of which 3 were waited for; matrix products, arithmetic and copies ran while one was open for 5% of the time, Pallas kernels for 0%

commit v1 on v0

v1 whole, which is shorter than its diff:
```python
import functools
import math

import jax
import jax.numpy as jnp
from jax import lax
from jax.experimental import pallas as pl
from jax.experimental.pallas import tpu as pltpu
from jax.sharding import Mesh
from jax.sharding import PartitionSpec as P

HEAD = 64
STEPS = 2
FEAT = 128
WIDE = 256
CHIPS = 8
TOK = 64
COLS = 192
PACK = 48
PAY = 3 * COLS + PACK + 2 * TOK
HEADS = CHIPS * 3
GROUPS = HEADS // 4
KEYS = 2048
ONE = 136
EPS = 1e-06
SAFE = 60.0

BF = jnp.bfloat16
F32 = jnp.float32
VMEM = pl.BlockSpec(memory_space=pltpu.VMEM)
SMEM = pl.BlockSpec(memory_space=pltpu.SMEM)
ANY = pl.BlockSpec(memory_space=pl.ANY)


def dot(a, b):
    return jnp.dot(a, b, preferred_element_type=F32)


def dot_t(a, b):
    return lax.dot_general(a, b, (((1,), (1,)), ((), ())), preferred_element_type=F32)


def halves(x):
    high = x.astype(BF)
    return high, (x - high.astype(F32)).astype(BF)


def lanes(shape):
    return lax.broadcasted_iota(jnp.int32, shape, len(shape) - 1)


def rows(shape):
    return lax.broadcasted_iota(jnp.int32, shape, len(shape) - 2)


def fold_kernel(qkv_ref, in_ref, cond_ref, gain_ref, x_ref, prev_ref, pay_ref, gram_hi_ref, gram_lo_ref):
    gain = gain_ref[...]
    cond = cond_ref[...]
    embed = in_ref[...]
    emb_hi, emb_lo = halves(embed.astype(F32) * gain)
    cg_hi, cg_lo = halves(jnp.concatenate([cond, jnp.zeros_like(cond)], axis=0) * gain)
    left = jnp.concatenate([emb_hi, emb_lo, cg_hi, cg_lo], axis=0)
    packed = jnp.zeros((PACK, FEAT), F32)
    for j in range(3):
        full = dot(left, qkv_ref[j])
        mat = full[0:128] + full[128:256]
        bias = full[256:264] + full[272:280]
        high = bias.astype(BF).astype(F32)
        bias = jnp.where(rows(bias.shape) < 4, high, bias - high)
        mat_t = jnp.transpose(mat).astype(BF)
        bias = jnp.concatenate([bias, jnp.zeros((120, COLS), F32)], axis=0)
        bias_t = jnp.transpose(bias)
        for i in range(4):
            part = bias_t[PACK * i : PACK * (i + 1)]
            shift = 8 * (4 * j + i)
            packed = packed + (pltpu.roll(part, shift, 1) if shift else part)
        for chip in range(CHIPS):
            pay_ref[chip, COLS * j : COLS * (j + 1)] = mat_t
    packed = packed.astype(BF)
    for chip in range(CHIPS):
        pay_ref[chip, 3 * COLS : 3 * COLS + PACK] = packed
        pay_ref[chip, 3 * COLS + PACK : PAY - TOK] = x_ref[...]
        pay_ref[chip, PAY - TOK : PAY] = prev_ref[...]
    c_hi, c_lo = halves(cond)
    four = rows(cond.shape) < 4
    c_hi = jnp.where(four, c_hi.astype(F32), 0.0).astype(BF)
    c_lo = jnp.where(four, c_lo.astype(F32), 0.0).astype(BF)
    none = jnp.zeros((120, embed.shape[1]), BF)
    l_hi = jnp.concatenate([embed, jnp.concatenate([c_hi, none], axis=0)], axis=0)
    l_lo = jnp.concatenate([jnp.zeros_like(embed), jnp.concatenate([c_lo, none], axis=0)], axis=0)
    gram = dot_t(l_hi, l_hi) + dot_t(l_hi, l_lo) + dot_t(l_lo, l_hi)
    g_hi, g_lo = halves(gram)
    gram_hi_ref[...] = g_hi
    gram_lo_ref[...] = g_lo


def fold(qkv, in_weight, cond, gain, x, prev):
    return pl.pallas_call(
        fold_kernel,
        out_shape=(
            jax.ShapeDtypeStruct((CHIPS, PAY, FEAT), BF),
            jax.ShapeDtypeStruct((WIDE, WIDE), BF),
            jax.ShapeDtypeStruct((WIDE, WIDE), BF),
        ),
        in_specs=[VMEM] * 6,
        out_specs=(VMEM,) * 3,
        compiler_params=pltpu.CompilerParams(vmem_limit_bytes=40 * 2**20),
        name="fold",
    )(qkv, in_weight, cond, gain, x, prev)


def attend_kernel(
    step,
    place_ref,
    safe_ref,
    pay_ref,
    mine_ref,
    other_ref,
    gram_hi_ref,
    gram_lo_ref,
    qk_ref,
    out_w_ref,
    part_ref,
    part_other_ref,
    xk_ref,
    xkt_ref,
    val_ref,
    aq_ref,
    ak_ref,
    av_ref,
    rk_ref,
    p_ref,
    s_ref,
    acc_ref,
    w_ref,
    sem,
):
    chip, core = place_ref[0], place_ref[1]
    copies = []
    for m in range(CHIPS):
        begin = pl.multiple_of((2 * m + core) * COLS, COLS)
        copies.append(pltpu.make_async_copy(out_w_ref.at[pl.ds(begin, COLS)], w_ref.at[pl.ds(m * COLS, COLS)], sem))
    for copy in copies:
        copy.start()

    half = CHIPS * TOK
    for group in range(2):
        for side, ref in enumerate((mine_ref, other_ref)):
            base = (2 * group + side) * half
            block = ref[:, TOK * group : TOK * (group + 1), :].reshape(half, FEAT)
            xk_ref[base : base + half, 0:FEAT] = block
        lane = lanes((KEYS // 2, FEAT))
        mark = jnp.logical_or(lane == 2 * step + group, lane == 4 + 2 * step + group)
        xk_ref[group * KEYS // 2 : (group + 1) * KEYS // 2, FEAT:WIDE] = mark.astype(F32).astype(BF)
    xkt_ref[0:FEAT, :] = jnp.transpose(xk_ref[:, 0:FEAT])
    row = rows((FEAT, KEYS))
    group = (lanes((FEAT, KEYS)) >= KEYS // 2).astype(jnp.int32)
    mark = jnp.logical_or(row == 2 * step + group, row == 4 + 2 * step + group)
    xkt_ref[FEAT:WIDE, :] = mark.astype(F32).astype(BF)

    xkt = xkt_ref[...]
    square = dot(gram_hi_ref[...], xkt) + dot(gram_lo_ref[...], xkt)
    m_row = jnp.sum(square * xkt.astype(F32), axis=0, keepdims=True) * (1.0 / 3072.0) + EPS
    r_col = jnp.transpose(jnp.broadcast_to(lax.rsqrt(m_row), (8, KEYS)))[:, 0:1]
    val = xk_ref[...].astype(F32) * r_col
    val_ref[...] = jnp.where(lanes((KEYS, WIDE)) == ONE, 1.0, val).astype(BF)

    lane = lanes((PACK, FEAT))
    for m in range(CHIPS):
        packed = pay_ref[m, 3 * COLS : 3 * COLS + PACK, :].astype(F32)
        for j, ref in enumerate((aq_ref, ak_ref, av_ref)):
            ref[m * COLS : (m + 1) * COLS, 0:FEAT] = pay_ref[m, j * COLS : (j + 1) * COLS, :]
            for i in range(4):
                shift = 8 * (4 * j + i)
                part = pltpu.roll(packed, FEAT - shift, 1) if shift else packed
                part = jnp.where(lane < 8, part, 0.0)
                ref[m * COLS + i * PACK : m * COLS + (i + 1) * PACK, FEAT:WIDE] = part.astype(BF)

    xq = jnp.concatenate([mine_ref[chip, 0:TOK, :], other_ref[chip, 0:TOK, :]], axis=0)
    lane = lanes((2 * TOK, FEAT))
    mark = jnp.logical_or(lane == 2 * step, lane == 4 + 2 * step)
    xq = jnp.concatenate([xq, mark.astype(F32).astype(BF)], axis=1)
    square = dot(xq, gram_hi_ref[...]) + dot(xq, gram_lo_ref[...])
    m_q = jnp.sum(square * xq.astype(F32), axis=1, keepdims=True) * (1.0 / 3072.0) + EPS
    ones = (rows((WIDE, WIDE)) // HEAD == lanes((WIDE, WIDE)) // HEAD).astype(F32).astype(BF)
    head_of = lanes((2 * TOK, WIDE)) // HEAD

    def one_group(g, fast):
        begin = pl.multiple_of(g * WIDE, WIDE)
        ak = ak_ref[pl.ds(begin, WIDE), :]
        u = dot(ak, xkt_ref[...])
        u = jnp.sum((u * u).reshape(4, HEAD, KEYS), axis=1)
        rk = lax.rsqrt(u * (1.0 / HEAD) + EPS * m_row)
        q = dot_t(xq, aq_ref[pl.ds(begin, WIDE), :])
        sq_hi, sq_lo = halves(q * q)
        mean = (dot(sq_hi, ones) + dot(sq_lo, ones)) * (1.0 / HEAD)
        q = q * lax.rsqrt(mean + EPS * m_q) * qk_ref[...]
        q = jnp.concatenate([jnp.where(head_of == h, q, 0.0) for h in range(4)], axis=0)
        carried = dot(q.astype(BF), ak).astype(BF)
        if fast:
            for h in range(4):
                s = dot(carried[128 * h : 128 * (h + 1)], xkt_ref[...])
                p_ref[128 * h : 128 * (h + 1), :] = jnp.exp2(s * rk[h : h + 1]).astype(BF)
        else:
            for h in range(4):
                s_ref[...] = dot(carried[128 * h : 128 * (h + 1)], xkt_ref[...]) * rk[h : h + 1]
                s = s_ref[...]
                s = s - jnp.max(s, axis=1, keepdims=True)
                p_ref[128 * h : 128 * (h + 1), :] = jnp.exp2(s).astype(BF)
        z = dot(p_ref[...], val_ref[...])
        z = (z * (1.0 / z[:, ONE : ONE + 1])).astype(BF)
        o = dot_t(z, av_ref[pl.ds(begin, WIDE), :])
        picked = jnp.where(head_of == 0, o[0:128], 0.0)
        for h in range(1, 4):
            picked = jnp.where(head_of == h, o[128 * h : 128 * (h + 1)], picked)
        acc_ref[g] = picked.astype(BF)

    @pl.when(safe_ref[0] == 1)
    def _():
        def body(g, carry):
            one_group(g, True)
            return carry

        lax.fori_loop(0, GROUPS, body, 0)

    @pl.when(safe_ref[0] != 1)
    def _():
        def body(g, carry):
            one_group(g, False)
            return carry

        lax.fori_loop(0, GROUPS, body, 0)

    for copy in copies:
        copy.wait()
    o = jnp.concatenate([acc_ref[g] for g in range(GROUPS)], axis=1)
    y = dot(o, w_ref[...])
    part_ref[...] = y[0:TOK]
    part_other_ref[...] = y[TOK:]


def attend(step, place, safe, pay, mine, other, gram_hi, gram_lo, qk, out_weight):
    width = out_weight.shape[1]
    part = jax.ShapeDtypeStruct((TOK, width), F32)
    half = HEADS * HEAD
    return pl.pallas_call(
        functools.partial(attend_kernel, step),
        out_shape=(part, part),
        in_specs=[SMEM, SMEM] + [VMEM] * 6 + [ANY],
        out_specs=(VMEM, VMEM),
        scratch_shapes=[
            pltpu.VMEM((KEYS, WIDE), BF),
            pltpu.VMEM((WIDE, KEYS), BF),
            pltpu.VMEM((KEYS, WIDE), BF),
            pltpu.VMEM((half, WIDE), BF),
            pltpu.VMEM((half, WIDE), BF),
            pltpu.VMEM((half, WIDE), BF),
            pltpu.VMEM((HEADS, KEYS), F32),
            pltpu.VMEM((512, KEYS), BF),
            pltpu.VMEM((128, KEYS), F32),
            pltpu.VMEM((GROUPS, 2 * TOK, WIDE), BF),
            pltpu.VMEM((half, width), BF),
            pltpu.SemaphoreType.DMA,
        ],
        compiler_params=pltpu.CompilerParams(vmem_limit_bytes=56 * 2**20),
        name="attend",
    )(place, safe, pay, mine, other, gram_hi, gram_lo, qk, out_weight)


def finish_kernel(step, sig_ref, state_ref, in_ref, cond_ref, part_ref, got_ref, gain_ref, final_ref, est_ref, new_ref):
    state = state_ref[...]
    y = dot(state.astype(BF), in_ref[...]) + cond_ref[2 * step : 2 * step + 1, :]
    y = y + part_ref[...] + got_ref[...]
    scale = lax.rsqrt(jnp.mean(y * y, axis=1, keepdims=True) + EPS)
    velocity = dot((y * scale * gain_ref[...]).astype(BF), final_ref[...])
    est_ref[...] = state - sig_ref[0] * velocity
    new_ref[...] = state + sig_ref[1] * velocity


def finish(step, sig, state, in_weight, cond, part, got, gain, final_weight):
    out = jax.ShapeDtypeStruct(state.shape, F32)
    return pl.pallas_call(
        functools.partial(finish_kernel, step),
        out_shape=(out, out),
        in_specs=[SMEM] + [VMEM] * 7,
        out_specs=(VMEM, VMEM),
        compiler_params=pltpu.CompilerParams(vmem_limit_bytes=32 * 2**20),
        name="finish",
    )(sig, state, in_weight, cond, part, got, gain, final_weight)


def passed_along(x, by):
    peers = lax.axis_size("frame")
    pairs = [(i, i + by) for i in range(peers) if 0 <= i + by < peers]
    return lax.ppermute(x, "frame", pairs)


def swapped(x):
    return lax.ppermute(x, "core", [(0, 1), (1, 0)])


def spread(x):
    return lax.all_to_all(x, ("y", "far"), 0, 0, tiled=True)


def waves(stamp, width):
    half = width // 2
    freqs = jnp.exp(-math.log(10000.0) * jnp.arange(half, dtype=F32) / half)
    angle = stamp * freqs
    return jnp.concatenate([jnp.cos(angle), jnp.sin(angle)])


def pick(table, where):
    return jnp.sum(jnp.where(jnp.arange(table.shape[0]) == where, table, 0))


def shards(
    latents,
    fresh_noise,
    level_index,
    plan,
    frame_ids,
    in_weight,
    cond_gain,
    norm_gain,
    qkv_weight,
    qk_gain,
    out_weight,
    final_gain,
    final_weight,
):
    slot = lax.axis_index("frame")
    count = lax.axis_size("frame")
    width = in_weight.shape[1]
    state = latents[0]
    x = state.astype(BF)
    prev = jnp.where(slot == 0, x, passed_along(x, 1))

    before = jnp.maximum(slot - 1, 0)
    stamp_now = pick(plan, pick(level_index, slot)).astype(F32)
    stamp_prev = pick(plan, pick(level_index, before)).astype(F32)
    sigma = stamp_now / 1000.0
    sigma_next = jnp.where(slot > 0, stamp_prev / 1000.0, jnp.float32(0.0))
    sig = jnp.stack([sigma, sigma_next - sigma])
    wave_now = cond_gain[0] * waves(stamp_now, width)
    wave_prev = cond_gain[0] * waves(stamp_prev, width)
    conds = []
    for step in range(STEPS):
        id_now = pick(frame_ids, slot + step).astype(F32)
        id_prev = pick(frame_ids, before + step).astype(F32)
        conds.append(wave_now + cond_gain[1] * waves(id_now, width))
        conds.append(wave_prev + cond_gain[1] * waves(id_prev, width))
    cond = jnp.stack(conds + conds)

    product = qk_gain[0] * qk_gain[1]
    safe = (HEAD**0.5 * jnp.max(jnp.abs(product)) <= SAFE).astype(jnp.int32)[None]
    qk = jnp.tile(product * (math.log2(math.e) / math.sqrt(HEAD)), 4)[None]
    place = jnp.stack([lax.axis_index(("y", "far")), lax.axis_index("core")]).astype(jnp.int32)

    sent, gram_hi, gram_lo = fold(qkv_weight, in_weight, cond, norm_gain[None], x, prev)
    pay = spread(sent)
    mine = pay[:, PAY - 2 * TOK :, :]
    results = []
    for step in range(STEPS):
        other = swapped(mine)
        part, part_other = attend(step, place, safe, pay, mine, other, gram_hi, gram_lo, qk, out_weight)
        got = swapped(part_other)
        estimate, renewed = finish(step, sig, state, in_weight, cond, part, got, final_gain[None], final_weight)
        results.append(estimate)
        state = jnp.where(slot == count - 1, fresh_noise[step], passed_along(renewed, -1))
        if step + 1 < STEPS:
            x = state.astype(BF)
            prev = jnp.where(slot == 0, x, renewed.astype(BF))
            both = jnp.concatenate([x, prev], axis=0)
            mine = spread(jnp.broadcast_to(both[None], (CHIPS,) + both.shape))
    return (jnp.stack(results)[:, None], state[None])


def solution(mesh):
    split = Mesh(mesh.devices.reshape(8, 4, 2, 2), ("frame", "y", "far", "core"))
    space = ("y", "far", "core")
    in_specs = (
        P("frame", space, None),
        P(None, space, None),
        P(),
        P(),
        P(),
        P(),
        P(),
        P(),
        P(None, None, space),
        P(),
        P(),
        P(),
        P(),
    )
    out_specs = (P(None, "frame", space, None), P("frame", space, None))
    return jax.shard_map(shards, mesh=split, in_specs=in_specs, out_specs=out_specs, check_vma=False)
```

time: 322 us -> 149 us (0.46)
  the two profiles are of different devices: /device:TPU:0 before, /device:TPU:96 now
where the time goes in v1:
time: 149 us; the launch traced here: 148 us
  Pallas kernels  51.4 us (34%)
  waiting for transfers between devices  38.2 us (26%)
  starting transfers between devices  15.3 us (10%)
  local copies, waits for them, and re-layouts  14.8 us (10%)
  other arithmetic  11.7 us (8%)
  blocking collectives  11.3 us (8%)
  between operations  5.32 us (4%)
    pallas_call x2, Pallas kernels, attend(): pl.pallas_call(functools.partial(attend_kernel, step), out_shape=(part, p...  44.9 us
    all_to_all x1, waiting for transfers between devices, spread(): return lax.all_to_all(x, ('y', 'far'), 0, 0, tiled=True)  22.6 us
    unnamed x33, local copies, waits for them, and re-layouts  13 us
    all_to_all x1, blocking collectives, spread(): return lax.all_to_all(x, ('y', 'far'), 0, 0, tiled=True)  11.3 us
    ppermute x3, waiting for transfers between devices, passed_along(): return lax.ppermute(x, 'frame', pairs)  9.61 us
    ppermute x3, starting transfers between devices, passed_along(): return lax.ppermute(x, 'frame', pairs)  7.6 us
    all_to_all x1, starting transfers between devices, spread(): return lax.all_to_all(x, ('y', 'far'), 0, 0, tiled=True)  6.82 us
    ppermute x4, waiting for transfers between devices, swapped(): return lax.ppermute(x, 'core', [(0, 1), (1, 0)])  5.95 us
  transfers between devices with their start and end apart: 8, of which 6 were waited for; matrix products, arithmetic and copies ran while one was open for 12% of the time, Pallas kernels for 0%

profile of v1, /device:TPU:96, one launch (start us, length us, event | category | flops | bytes accessed | tf_op | source)
XLA Modules:
  0.0 148.0 jit_solution(6318709993264562599)
XLA Ops:
  0.6 0.8 bitcast_convert_fusion.x_ref
  1.4 2.0 %collective-permute-start = (bf16[64,128]{1,0:T(8,128)(2,1)S(1)}, bf16[64,128]{1,0:T(8,128)(2,1)S(1)}, u32[]{:S(2)}, u32[]{:S(2)}) collective-permute-start(bf16[64,128]{1,0:T(8,128)(2,1)S(1)} %bitcast_convert_fusion.x_ref), channel_id=1, source_target_pairs={{0,16},{16,32},{32,48},{48,64},{64,80},{80,96},{96,112},{1,17},{17... | collective-permute-start | bytes 49160 | tf_op jit(solution)/shard_map/ppermute | solution.py:295
  3.4 1.3 fusion.5
  4.7 2.6 %fusion.6 = (s32[]{:T(128)}, s32[]{:T(128)}) fusion(s32[48]{0:T(128)} %param.16, s32[]{:T(128)} %get-tuple-element.32, s32[]{:T(128)} %get-tuple-element.33), kind=kLoop, calls=%fused_computation.39 | loop fusion | flops 286 | bytes 208 | tf_op jit(solution)/shard_map/reduce_sum | solution.py:314
  7.9 0.2 multiply_sine_fusion.3
  8.1 1.4 fusion.12
  10.2 0.2 multiply_sine_fusion
  11.0 0.2 multiply_sine_fusion.2
  11.9 0.2 multiply_sine_fusion.5
  12.8 0.2 multiply_sine_fusion.1
  13.6 0.2 multiply_sine_fusion.4
  13.8 0.9 fusion.4
  14.7 0.9 fusion.3
  15.5 0.0 copy-start.7
  15.5 0.0 copy-start.1
  15.6 6.4 %copy.15.qkv_ref = bf16[3,3072,192]{2,1,0:T(8,128)(2,1)} copy(bf16[3,3072,192]{1,2,0:T(8,128)(2,1)} %param.21) | data formatting | bytes 7077888 | tf_op args[8]
  21.9 0.1 stack.41.cond_ref
  22.1 2.3 %copy-done = bf16[3,3072,192]{2,1,0:T(8,128)(2,1)S(1)} copy-done((bf16[3,3072,192]{2,1,0:T(8,128)(2,1)S(1)}, bf16[3,3072,192]{2,1,0:T(8,128)(2,1)}, u32[]{:S(2)}) %copy-start) | copy-done | bytes 3538968
  24.5 4.2 %fold.1 = (bf16[8,752,128]{2,1,0:T(8,128)(2,1)}, bf16[256,256]{1,0:T(8,128)(2,1)S(1)}, bf16[256,256]{1,0:T(8,128)(2,1)S(1)}) custom-call(bf16[3,3072,192]{2,1,0:T(8,128)(2,1)S(1)} %copy-done, bf16[128,3072]{1,0:T(8,128)(2,1)S(1)} %copy-done.1, f32[8,3072]{1,0:T(8,128)S(1)} %stack.41.cond_ref, f32[1,3072]{1,0:T(1,128)S(1)} %bitcast.33, ...), custom_call_target="tpu_custom_call" | custom-call | tf_op jit(solution)/shard_map/fold/pallas_call | solution.py:98
  28.7 0.6 copy-done.5
  29.3 6.8 %all-to-all-start = ((bf16[8,752,128]{2,1,0:T(8,128)(2,1)}), bf16[8,752,128]{2,1,0:T(8,128)(2,1)}, u32[]{:S(2)}, u32[]{:S(2)}) async-start(bf16[8,752,128]{2,1,0:T(8,128)(2,1)} %get-tuple-element.13), calls=%async_computation | async-start | bytes 3080192 | tf_op jit(solution)/shard_map/all_to_all | solution.py:303
  36.1 22.6 %all-to-all-done.pay_ref = bf16[8,752,128]{2,1,0:T(8,128)(2,1)} async-done(((bf16[8,752,128]{2,1,0:T(8,128)(2,1)}), bf16[8,752,128]{2,1,0:T(8,128)(2,1)}, u32[]{:S(2)}, u32[]{:S(2)}) %all-to-all-start) | async-done | bytes 1540128 | tf_op jit(solution)/shard_map/all_to_all | solution.py:303
  58.7 1.0 slice.32.mine_ref
  59.7 0.1 collective-permute-start.1
  59.8 0.7 multiply_bitcast_fusion
  60.5 0.6 broadcast_in_dim_tile.3.qk_ref
  61.9 0.6 pad_add_fusion.place_ref
  62.5 0.7 copy-done.12
  63.2 22.6 %attend.2 = (f32[64,3072]{1,0:T(8,128)}, f32[64,3072]{1,0:T(8,128)}) custom-call(s32[2]{0:T(128)} %pad_add_fusion.place_ref, s32[1]{0:T(128)} %bitcast.5.safe_ref, bf16[8,752,128]{2,1,0:T(8,128)(2,1)} %all-to-all-done.pay_ref, bf16[8,128,128]{2,1,0:T(8,128)(2,1)} %copy-done.10, bf16[8,128,128]{2,1,0:T(8,128)(2,1)} %copy-done.12, bf16[256,256]{1,0:T(8,128)(2,1)} %copy-done.5, ...), custom_call_target="tpu_custom_call" | custom-call | tf_op jit(solution)/shard_map/attend/pallas_call | solution.py:246
  85.8 0.6 collective-permute-start.2
  86.3 0.1 pad_maximum_fusion.1.sig_ref
  86.4 2.0 %collective-permute-done.2.got_ref = f32[64,3072]{1,0:T(8,128)S(1)} collective-permute-done((f32[64,3072]{1,0:T(8,128)}, f32[64,3072]{1,0:T(8,128)S(1)}, u32[]{:S(2)}, u32[]{:S(2)}) %collective-permute-start.2) | collective-permute-done | bytes 786464 | tf_op jit(solution)/shard_map/ppermute | solution.py:299
  88.4 1.1 copy-done.3
  89.6 1.2 finish.2
  90.8 3.7 %collective-permute-start.3 = (f32[64,128]{1,0:T(8,128)S(1)}, f32[64,128]{1,0:T(8,128)S(1)}, u32[]{:S(2)}, u32[]{:S(2)}) collective-permute-start(f32[64,128]{1,0:T(8,128)S(1)} %get-tuple-element.19), channel_id=1, source_target_pairs={{16,0},{32,16},{48,32},{64,48},{80,64},{96,80},{112,96},{17,1},{33... | collective-permute-start | bytes 98312 | tf_op jit(solution)/shard_map/ppermute | solution.py:295
  94.4 4.3 %collective-permute-done.3 = f32[64,128]{1,0:T(8,128)S(1)} collective-permute-done((f32[64,128]{1,0:T(8,128)S(1)}, f32[64,128]{1,0:T(8,128)S(1)}, u32[]{:S(2)}, u32[]{:S(2)}) %collective-permute-start.3) | collective-permute-done | bytes 32800 | tf_op jit(solution)/shard_map/ppermute | solution.py:295
  98.8 11.3 %all_to_all.10.mine_ref = bf16[8,128,128]{2,1,0:T(8,128)(2,1)S(1)} all-to-all(bf16[8,128,128]{2,1,0:T(8,128)(2,1)S(1)} %broadcast_in_dim.48), channel_id=1, replica_groups=mesh['frame'=8,'y'=4,'far'=2,'core'=2] {'y','far'}, dimensions={0} | all-to-all | bytes 524288 | tf_op jit(solution)/shard_map/all_to_all | solution.py:303
  110.0 1.5 %collective-permute-done.4.other_ref = bf16[8,128,128]{2,1,0:T(8,128)(2,1)S(1)} collective-permute-done((bf16[8,128,128]{2,1,0:T(8,128)(2,1)S(1)}, bf16[8,128,128]{2,1,0:T(8,128)(2,1)S(1)}, u32[]{:S(2)}, u32[]{:S(2)}) %collective-permute-start.4) | collective-permute-done | bytes 262176 | tf_op jit(solution)/shard_map/ppermute | solution.py:299
  111.6 0.7 copy-done.13
  112.3 22.3 %attend.3 = (f32[64,3072]{1,0:T(8,128)}, f32[64,3072]{1,0:T(8,128)}) custom-call(s32[2]{0:T(128)} %pad_add_fusion.place_ref, s32[1]{0:T(128)} %bitcast.5.safe_ref, bf16[8,752,128]{2,1,0:T(8,128)(2,1)} %all-to-all-done.pay_ref, bf16[8,128,128]{2,1,0:T(8,128)(2,1)} %copy-done.11, bf16[8,128,128]{2,1,0:T(8,128)(2,1)} %copy-done.13, bf16[256,256]{1,0:T(8,128)(2,1)} %copy-done.5, ...), custom_call_target="tpu_custom_call" | custom-call | tf_op jit(solution)/shard_map/attend/pallas_call | solution.py:246
  134.6 0.2 collective-permute-start.5
  134.8 2.4 %collective-permute-done.5.got_ref = f32[64,3072]{1,0:T(8,128)S(1)} collective-permute-done((f32[64,3072]{1,0:T(8,128)}, f32[64,3072]{1,0:T(8,128)S(1)}, u32[]{:S(2)}, u32[]{:S(2)}) %collective-permute-start.5) | collective-permute-done | bytes 786464 | tf_op jit(solution)/shard_map/ppermute | solution.py:299
  137.2 1.1 copy-done.4
  138.3 1.2 finish.3
  139.5 1.9 %collective-permute-start.6 = (f32[64,128]{1,0:T(8,128)S(1)}, f32[64,128]{1,0:T(8,128)S(1)}, u32[]{:S(2)}, u32[]{:S(2)}) collective-permute-start(f32[64,128]{1,0:T(8,128)S(1)} %get-tuple-element.23), channel_id=1, source_target_pairs={{16,0},{32,16},{48,32},{64,48},{80,64},{96,80},{112,96},{17,1},{33... | collective-permute-start | bytes 98312 | tf_op jit(solution)/shard_map/ppermute | solution.py:295
  141.4 0.6 maximum_bitcast_fusion
  142.1 5.4 %collective-permute-done.6 = f32[64,128]{1,0:T(8,128)S(1)} collective-permute-done((f32[64,128]{1,0:T(8,128)S(1)}, f32[64,128]{1,0:T(8,128)S(1)}, u32[]{:S(2)}, u32[]{:S(2)}) %collective-permute-start.6) | collective-permute-done | bytes 32800 | tf_op jit(solution)/shard_map/ppermute | solution.py:295
  147.4 0.6 fusion
  (32 shorter events, 0.1 us)
Async XLA Ops:
  1.4 20.7 %collective-permute-start = (bf16[64,128]{1,0:T(8,128)(2,1)S(1)}, bf16[64,128]{1,0:T(8,128)(2,1)S(1)}, u32[]{:S(2)}, u32[]{:S(2)}) collective-permute-start(bf16[64,128]{1,0:T(8,128)(2,1)S(1)} %bitcast_convert_fusion.x_ref), channel_id=1, source_target_pairs={{0,16},{16,32},{32,48},{48,64},{64,80},{80,96},{96,112},{1,17},{17... | collective-permute-start | bytes 49160 | tf_op jit(solution)/shard_map/ppermute | solution.py:295
  15.5 6.5 %copy-start.7 = (f32[1,64,128]{2,1,0:T(8,128)S(1)}, f32[1,64,128]{2,1,0:T(8,128)}, u32[]{:S(2)}) copy-start(f32[1,64,128]{2,1,0:T(8,128)} %param.13) | copy-start | bytes 98308
  15.5 6.6 %copy-start.1 = (bf16[128,3072]{1,0:T(8,128)(2,1)S(1)}, bf16[128,3072]{1,0:T(8,128)(2,1)}, u32[]{:S(2)}) copy-start(bf16[128,3072]{1,0:T(8,128)(2,1)} %in_ref.5) | copy-start | bytes 2359300
  15.5 6.6 %copy-start.9 = (f32[3072]{0:T(1024)S(1)}, f32[3072]{0:T(1024)}, u32[]{:S(2)}) copy-start(f32[3072]{0:T(1024)} %param.20) | copy-start | bytes 36868
  22.1 2.3 %copy-start = (bf16[3,3072,192]{2,1,0:T(8,128)(2,1)S(1)}, bf16[3,3072,192]{2,1,0:T(8,128)(2,1)}, u32[]{:S(2)}) copy-start(bf16[3,3072,192]{2,1,0:T(8,128)(2,1)} %copy.15.qkv_ref) | copy-start | bytes 10616836
  24.5 35.4 %copy-start.15 = (f32[2,64]{1,0:T(2,128)S(1)}, f32[2,64]{1,0:T(2,128)}, u32[]{:S(2)}) copy-start(f32[2,64]{1,0:T(2,128)} %param.22) | copy-start | bytes 1540
  28.7 0.6 copy-start.5
  29.3 33.2 %copy-start.6 = (bf16[256,256]{1,0:T(8,128)(2,1)}, bf16[256,256]{1,0:T(8,128)(2,1)S(1)}, u32[]{:S(2)}) copy-start(bf16[256,256]{1,0:T(8,128)(2,1)S(1)} %get-tuple-element.15.gram_lo_ref) | copy-start | bytes 393220
  29.3 29.4 %all-to-all-start = ((bf16[8,752,128]{2,1,0:T(8,128)(2,1)}), bf16[8,752,128]{2,1,0:T(8,128)(2,1)}, u32[]{:S(2)}, u32[]{:S(2)}) async-start(bf16[8,752,128]{2,1,0:T(8,128)(2,1)} %get-tuple-element.13), calls=%async_computation | async-start | bytes 3080192 | tf_op jit(solution)/shard_map/all_to_all | solution.py:303
  59.7 2.8 %copy-start.10 = (bf16[8,128,128]{2,1,0:T(8,128)(2,1)}, bf16[8,128,128]{2,1,0:T(8,128)(2,1)S(1)}, u32[]{:S(2)}) copy-start(bf16[8,128,128]{2,1,0:T(8,128)(2,1)S(1)} %slice.32.mine_ref) | copy-start | bytes 786436
  59.7 2.7 %collective-permute-start.1 = (bf16[8,128,128]{2,1,0:T(8,128)(2,1)S(1)}, bf16[8,128,128]{2,1,0:T(8,128)(2,1)S(1)}, u32[]{:S(2)}, u32[]{:S(2)}) collective-permute-start(bf16[8,128,128]{2,1,0:T(8,128)(2,1)S(1)} %slice.32.mine_ref), channel_id=1, source_target_pairs={{0,1},{1,0},{2,3},{3,2},{4,5},{5,4},{6,7},{7,6},{8,9},{9,8},{10,11... | collective-permute-start | bytes 786440 | tf_op jit(solution)/shard_map/ppermute | solution.py:299
  62.5 0.7 copy-start.12
  63.2 25.3 %copy-start.2 = (bf16[3072,128]{1,0:T(8,128)(2,1)S(1)}, bf16[3072,128]{1,0:T(8,128)(2,1)}, u32[]{:S(2)}) copy-start(bf16[3072,128]{1,0:T(8,128)(2,1)} %final_ref.3) | copy-start | bytes 2359300
  63.2 25.3 %copy-start.8 = (f32[3072]{0:T(1024)S(1)}, f32[3072]{0:T(1024)}, u32[]{:S(2)}) copy-start(f32[3072]{0:T(1024)} %param.24) | copy-start | bytes 36868
  63.2 35.5 %copy-start.14 = (f32[2,64,128]{2,1,0:T(8,128)S(1)}, f32[2,64,128]{2,1,0:T(8,128)}, u32[]{:S(2)}) copy-start(f32[2,64,128]{2,1,0:T(8,128)} %param.14) | copy-start | bytes 196612
  85.8 2.7 %collective-permute-start.2 = (f32[64,3072]{1,0:T(8,128)}, f32[64,3072]{1,0:T(8,128)S(1)}, u32[]{:S(2)}, u32[]{:S(2)}) collective-permute-start(f32[64,3072]{1,0:T(8,128)} %get-tuple-element.17), channel_id=1, source_target_pairs={{0,1},{1,0},{2,3},{3,2},{4,5},{5,4},{6,7},{7,6},{8,9},{9,8},{10,11... | collective-permute-start | bytes 2359304 | tf_op jit(solution)/shard_map/ppermute | solution.py:299
  88.4 1.1 copy-start.3
  90.8 7.9 %collective-permute-start.3 = (f32[64,128]{1,0:T(8,128)S(1)}, f32[64,128]{1,0:T(8,128)S(1)}, u32[]{:S(2)}, u32[]{:S(2)}) collective-permute-start(f32[64,128]{1,0:T(8,128)S(1)} %get-tuple-element.19), channel_id=1, source_target_pairs={{16,0},{32,16},{48,32},{64,48},{80,64},{96,80},{112,96},{17,1},{33... | collective-permute-start | bytes 98312 | tf_op jit(solution)/shard_map/ppermute | solution.py:295
  110.0 1.5 %copy-start.11 = (bf16[8,128,128]{2,1,0:T(8,128)(2,1)}, bf16[8,128,128]{2,1,0:T(8,128)(2,1)S(1)}, u32[]{:S(2)}) copy-start(bf16[8,128,128]{2,1,0:T(8,128)(2,1)S(1)} %all_to_all.10.mine_ref) | copy-start | bytes 786436
  110.0 1.5 %collective-permute-start.4 = (bf16[8,128,128]{2,1,0:T(8,128)(2,1)S(1)}, bf16[8,128,128]{2,1,0:T(8,128)(2,1)S(1)}, u32[]{:S(2)}, u32[]{:S(2)}) collective-permute-start(bf16[8,128,128]{2,1,0:T(8,128)(2,1)S(1)} %all_to_all.10.mine_ref), channel_id=1, source_target_pairs={{0,1},{1,0},{2,3},{3,2},{4,5},{5,4},{6,7},{7,6},{8,9},{9,8},{10,11... | collective-permute-start | bytes 786440 | tf_op jit(solution)/shard_map/ppermute | solution.py:299
  111.6 0.7 copy-start.13
  134.6 2.6 %collective-permute-start.5 = (f32[64,3072]{1,0:T(8,128)}, f32[64,3072]{1,0:T(8,128)S(1)}, u32[]{:S(2)}, u32[]{:S(2)}) collective-permute-start(f32[64,3072]{1,0:T(8,128)} %get-tuple-element.21), channel_id=1, source_target_pairs={{0,1},{1,0},{2,3},{3,2},{4,5},{5,4},{6,7},{7,6},{8,9},{9,8},{10,11... | collective-permute-start | bytes 2359304 | tf_op jit(solution)/shard_map/ppermute | solution.py:299
  137.2 1.1 copy-start.4
  139.5 7.9 %collective-permute-start.6 = (f32[64,128]{1,0:T(8,128)S(1)}, f32[64,128]{1,0:T(8,128)S(1)}, u32[]{:S(2)}, u32[]{:S(2)}) collective-permute-start(f32[64,128]{1,0:T(8,128)S(1)} %get-tuple-element.23), channel_id=1, source_target_pairs={{16,0},{32,16},{48,32},{64,48},{80,64},{96,80},{112,96},{17,1},{33... | collective-permute-start | bytes 98312 | tf_op jit(solution)/shard_map/ppermute | solution.py:295

commit v2 on v1

v2 whole, which is shorter than its diff:
```python
import functools
import math

import jax
import jax.numpy as jnp
from jax import lax
from jax.experimental import pallas as pl
from jax.experimental.pallas import tpu as pltpu
from jax.sharding import Mesh
from jax.sharding import PartitionSpec as P

HEAD = 64
STEPS = 2
FEAT = 128
WIDE = 256
CHIPS = 8
TOK = 64
COLS = 192
PACK = 48
PAY = 3 * COLS + PACK + 2 * TOK
HEADS = CHIPS * 3
GROUPS = HEADS // 4
KEYS = 2048
ONE = 136
EPS = 1e-06
SAFE = 60.0

BF = jnp.bfloat16
F32 = jnp.float32
VMEM = pl.BlockSpec(memory_space=pltpu.VMEM)
SMEM = pl.BlockSpec(memory_space=pltpu.SMEM)
ANY = pl.BlockSpec(memory_space=pl.ANY)


def dot(a, b):
    return jnp.dot(a, b, preferred_element_type=F32)


def dot_t(a, b):
    return lax.dot_general(a, b, (((1,), (1,)), ((), ())), preferred_element_type=F32)


def halves(x):
    high = x.astype(BF)
    return high, (x - high.astype(F32)).astype(BF)


def in_vmem(x):
    return pltpu.with_memory_space_constraint(x, pltpu.VMEM)


def lanes(shape):
    return lax.broadcasted_iota(jnp.int32, shape, len(shape) - 1)


def rows(shape):
    return lax.broadcasted_iota(jnp.int32, shape, len(shape) - 2)


def fold_kernel(
    level_ref,
    plan_ref,
    ids_ref,
    freq_ref,
    qkv_ref,
    in_ref,
    cond_gain_ref,
    gain_ref,
    qk_gain_ref,
    state_ref,
    pay_ref,
    gram_hi_ref,
    gram_lo_ref,
    cond_ref,
    qk_ref,
    safe_ref,
    sig_ref,
    w_ref,
    sems,
):
    copies = [pltpu.make_async_copy(qkv_ref.at[j], w_ref.at[j], sems.at[j]) for j in range(3)]
    for copy in copies:
        copy.start()

    slot = lax.axis_index("frame")
    before = jnp.maximum(slot - 1, 0)
    stamp_now = plan_ref[level_ref[slot]].astype(F32)
    stamp_prev = plan_ref[level_ref[before]].astype(F32)
    sigma = stamp_now / 1000.0
    sig_ref[0] = sigma
    sig_ref[1] = jnp.where(slot > 0, stamp_prev / 1000.0, 0.0) - sigma

    product = qk_gain_ref[0:1, :] * qk_gain_ref[1:2, :]
    safe_ref[0] = (HEAD**0.5 * jnp.max(jnp.abs(product)) <= SAFE).astype(jnp.int32)
    product = product * (math.log2(math.e) / math.sqrt(HEAD))
    qk_ref[...] = jnp.concatenate([product] * 4, axis=1)

    row = rows((8, freq_ref.shape[1]))
    stamp = jnp.where(row % 2 == 0, stamp_now, stamp_prev)
    ident = jnp.zeros_like(stamp)
    for step in range(STEPS):
        now = ids_ref[slot + step].astype(F32)
        prev = ids_ref[before + step].astype(F32)
        ident = jnp.where((row // 2) % 2 == step, jnp.where(row % 2 == 0, now, prev), ident)
    freq = freq_ref[...]
    wave_stamp = jnp.concatenate([jnp.cos(stamp * freq), jnp.sin(stamp * freq)], axis=1)
    wave_ident = jnp.concatenate([jnp.cos(ident * freq), jnp.sin(ident * freq)], axis=1)
    cond = cond_gain_ref[0:1, :] * wave_stamp + cond_gain_ref[1:2, :] * wave_ident
    cond_ref[...] = cond

    embed = in_ref[...]
    c_hi, c_lo = halves(cond)
    four = rows(cond.shape) < 4
    c_hi = jnp.where(four, c_hi.astype(F32), 0.0).astype(BF)
    c_lo = jnp.where(four, c_lo.astype(F32), 0.0).astype(BF)
    none = jnp.zeros((120, embed.shape[1]), BF)
    l_hi = jnp.concatenate([embed, jnp.concatenate([c_hi, none], axis=0)], axis=0)
    l_lo = jnp.concatenate([jnp.zeros_like(embed), jnp.concatenate([c_lo, none], axis=0)], axis=0)
    gram = dot_t(l_hi, l_hi) + dot_t(l_hi, l_lo) + dot_t(l_lo, l_hi)
    g_hi, g_lo = halves(gram)
    gram_hi_ref[...] = g_hi
    gram_lo_ref[...] = g_lo

    gain = gain_ref[...]
    emb_hi, emb_lo = halves(embed.astype(F32) * gain)
    cg_hi, cg_lo = halves(cond * gain)
    none = jnp.zeros((112, embed.shape[1]), BF)
    right = jnp.concatenate([emb_hi, jnp.concatenate([cg_hi, cg_lo], axis=0), none], axis=0)
    packed = jnp.zeros((PACK, FEAT), F32)
    for j in range(3):
        copies[j].wait()
        full = dot_t(w_ref[j], right)
        mat = (full[:, 0:FEAT] + dot_t(w_ref[j], emb_lo)).astype(BF)
        bias = full[:, FEAT:WIDE]
        bias = bias + pltpu.roll(bias, FEAT - 8, 1)
        bias = jnp.where(lanes(bias.shape) < 8, bias, 0.0)
        high = bias.astype(BF).astype(F32)
        bias = jnp.where(lanes(bias.shape) < 4, high, bias - high)
        for i in range(4):
            part = bias[PACK * i : PACK * (i + 1)]
            shift = 8 * (4 * j + i)
            packed = packed + (pltpu.roll(part, shift, 1) if shift else part)
        for chip in range(CHIPS):
            pay_ref[chip, COLS * j : COLS * (j + 1)] = mat
    packed = packed.astype(BF)
    x = state_ref[0].astype(BF)
    for chip in range(CHIPS):
        pay_ref[chip, 3 * COLS : 3 * COLS + PACK] = packed
        pay_ref[chip, 3 * COLS + PACK : PAY - TOK] = x
        pay_ref[chip, PAY - TOK : PAY] = x


def fold(level_index, plan, frame_ids, freq, qkv, in_weight, cond_gain, gain, qk_gain, latents):
    width = in_weight.shape[1]
    return pl.pallas_call(
        fold_kernel,
        out_shape=(
            pltpu.VMEM((CHIPS, PAY, FEAT), BF),
            pltpu.VMEM((WIDE, WIDE), BF),
            pltpu.VMEM((WIDE, WIDE), BF),
            pltpu.VMEM((8, width), F32),
            pltpu.VMEM((1, WIDE), F32),
            jax.ShapeDtypeStruct((1,), jnp.int32),
            jax.ShapeDtypeStruct((2,), F32),
        ),
        in_specs=[SMEM] * 3 + [VMEM, ANY] + [VMEM] * 5,
        out_specs=(VMEM,) * 5 + (SMEM,) * 2,
        scratch_shapes=[pltpu.VMEM(qkv.shape, BF), pltpu.SemaphoreType.DMA((3,))],
        compiler_params=pltpu.CompilerParams(vmem_limit_bytes=40 * 2**20),
        name="fold",
    )(level_index, plan, frame_ids, freq, qkv, in_weight, cond_gain, gain, qk_gain, latents)


def attend_kernel(
    step,
    safe_ref,
    pay_ref,
    mine_ref,
    other_ref,
    gram_hi_ref,
    gram_lo_ref,
    qk_ref,
    out_w_ref,
    part_ref,
    part_other_ref,
    xk_ref,
    xkt_ref,
    val_ref,
    aq_ref,
    ak_ref,
    av_ref,
    rk_ref,
    p_ref,
    s_ref,
    qc_ref,
    z_ref,
    w_ref,
    sem,
):
    chip, core = lax.axis_index(("y", "far")), lax.axis_index("core")
    first = lax.axis_index("frame") == 0
    copies = []
    for m in range(CHIPS):
        begin = pl.multiple_of((2 * m + core) * COLS, COLS)
        copies.append(pltpu.make_async_copy(out_w_ref.at[pl.ds(begin, COLS)], w_ref.at[pl.ds(m * COLS, COLS)], sem))
    for copy in copies:
        copy.start()

    half = CHIPS * TOK
    for group in range(2):
        for side, ref in enumerate((mine_ref, other_ref)):
            base = (2 * group + side) * half
            block = ref[:, TOK * group : TOK * (group + 1), :].reshape(half, FEAT)
            if group == 1:
                block = jnp.where(first, ref[:, 0:TOK, :].reshape(half, FEAT), block)
            xk_ref[base : base + half, 0:FEAT] = block
        lane = lanes((KEYS // 2, FEAT))
        mark = jnp.logical_or(lane == 2 * step + group, lane == 4 + 2 * step + group)
        xk_ref[group * KEYS // 2 : (group + 1) * KEYS // 2, FEAT:WIDE] = mark.astype(F32).astype(BF)
    xkt_ref[0:FEAT, :] = jnp.transpose(xk_ref[:, 0:FEAT])
    row = rows((FEAT, KEYS))
    group = (lanes((FEAT, KEYS)) >= KEYS // 2).astype(jnp.int32)
    mark = jnp.logical_or(row == 2 * step + group, row == 4 + 2 * step + group)
    xkt_ref[FEAT:WIDE, :] = mark.astype(F32).astype(BF)

    xkt = xkt_ref[...]
    square = dot(gram_hi_ref[...], xkt) + dot(gram_lo_ref[...], xkt)
    m_row = jnp.sum(square * xkt.astype(F32), axis=0, keepdims=True) * (1.0 / 3072.0) + EPS
    r_col = jnp.transpose(jnp.broadcast_to(lax.rsqrt(m_row), (8, KEYS)))[:, 0:1]
    val = xk_ref[...].astype(F32) * r_col
    val_ref[...] = jnp.where(lanes((KEYS, WIDE)) == ONE, 1.0, val).astype(BF)

    lane = lanes((PACK, FEAT))
    for m in range(CHIPS):
        packed = pay_ref[m, 3 * COLS : 3 * COLS + PACK, :].astype(F32)
        for j, ref in enumerate((aq_ref, ak_ref, av_ref)):
            ref[m * COLS : (m + 1) * COLS, 0:FEAT] = pay_ref[m, j * COLS : (j + 1) * COLS, :]
            for i in range(4):
                shift = 8 * (4 * j + i)
                part = pltpu.roll(packed, FEAT - shift, 1) if shift else packed
                part = jnp.where(lane < 8, part, 0.0)
                ref[m * COLS + i * PACK : m * COLS + (i + 1) * PACK, FEAT:WIDE] = part.astype(BF)

    xq = jnp.concatenate([mine_ref[chip, 0:TOK, :], other_ref[chip, 0:TOK, :]], axis=0)
    lane = lanes((2 * TOK, FEAT))
    mark = jnp.logical_or(lane == 2 * step, lane == 4 + 2 * step)
    xq = jnp.concatenate([xq, mark.astype(F32).astype(BF)], axis=1)
    square = dot(xq, gram_hi_ref[...]) + dot(xq, gram_lo_ref[...])
    m_q = jnp.sum(square * xq.astype(F32), axis=1, keepdims=True) * (1.0 / 3072.0) + EPS
    ones = (rows((WIDE, WIDE)) // HEAD == lanes((WIDE, WIDE)) // HEAD).astype(F32).astype(BF)
    head_of = lanes((2 * TOK, WIDE)) // HEAD

    def norms(g, carry):
        begin = pl.multiple_of(g * WIDE, WIDE)
        u = dot(ak_ref[pl.ds(begin, WIDE), :], xkt_ref[...])
        u = jnp.sum((u * u).reshape(4, HEAD, KEYS), axis=1)
        rk = lax.rsqrt(u * (1.0 / HEAD) + EPS * m_row)
        rk_ref[g] = jnp.concatenate([rk, rk], axis=0)
        return carry

    lax.fori_loop(0, GROUPS, norms, 0, unroll=True)

    for g in range(GROUPS):
        span = slice(g * WIDE, (g + 1) * WIDE)
        q = dot_t(xq, aq_ref[span, :])
        sq_hi, sq_lo = halves(q * q)
        mean = (dot(sq_hi, ones) + dot(sq_lo, ones)) * (1.0 / HEAD)
        q = q * lax.rsqrt(mean + EPS * m_q) * qk_ref[...]
        q = jnp.concatenate([jnp.where(head_of == h, q, 0.0) for h in range(4)], axis=0)
        qc_ref[g] = dot(q.astype(BF), ak_ref[span, :]).astype(BF)

    def one_group(g, fast):
        carried = qc_ref[g]
        rk = rk_ref[g]
        for h in range(4):
            span = slice(2 * TOK * h, 2 * TOK * (h + 1))
            s = dot(carried[span], xkt_ref[...]) * rk[h : h + 1]
            if not fast:
                s_ref[...] = s
                s = s_ref[...]
                s = s - jnp.max(s, axis=1, keepdims=True)
            p_ref[span, :] = jnp.exp2(s).astype(BF)
        for h in range(4):
            span = slice(2 * TOK * h, 2 * TOK * (h + 1))
            z = dot(p_ref[span, :], val_ref[...])
            z_ref[g, span] = (z * (1.0 / z[:, ONE : ONE + 1])).astype(BF)

    @pl.when(safe_ref[0] == 1)
    def _():
        def body(g, carry):
            one_group(g, True)
            return carry

        lax.fori_loop(0, GROUPS, body, 0, unroll=3)

    @pl.when(safe_ref[0] != 1)
    def _():
        def body(g, carry):
            one_group(g, False)
            return carry

        lax.fori_loop(0, GROUPS, body, 0)

    outs = []
    for g in range(GROUPS):
        o = dot_t(z_ref[g], av_ref[g * WIDE : (g + 1) * WIDE, :])
        picked = jnp.where(head_of == 0, o[0:128], 0.0)
        for h in range(1, 4):
            picked = jnp.where(head_of == h, o[128 * h : 128 * (h + 1)], picked)
        outs.append(picked.astype(BF))
    for copy in copies:
        copy.wait()
    y = dot(jnp.concatenate(outs, axis=1), w_ref[...])
    part_ref[...] = y[0:TOK]
    part_other_ref[...] = y[TOK:].astype(BF)


def attend(step, safe, pay, mine, other, gram_hi, gram_lo, qk, out_weight):
    width = out_weight.shape[1]
    half = HEADS * HEAD
    return pl.pallas_call(
        functools.partial(attend_kernel, step),
        out_shape=(pltpu.VMEM((TOK, width), F32), pltpu.VMEM((TOK, width), BF)),
        in_specs=[SMEM] + [VMEM] * 6 + [ANY],
        out_specs=(VMEM, VMEM),
        scratch_shapes=[
            pltpu.VMEM((KEYS, WIDE), BF),
            pltpu.VMEM((WIDE, KEYS), BF),
            pltpu.VMEM((KEYS, WIDE), BF),
            pltpu.VMEM((half, WIDE), BF),
            pltpu.VMEM((half, WIDE), BF),
            pltpu.VMEM((half, WIDE), BF),
            pltpu.VMEM((GROUPS, 8, KEYS), F32),
            pltpu.VMEM((512, KEYS), BF),
            pltpu.VMEM((128, KEYS), F32),
            pltpu.VMEM((GROUPS, 512, WIDE), BF),
            pltpu.VMEM((GROUPS, 512, WIDE), BF),
            pltpu.VMEM((half, width), BF),
            pltpu.SemaphoreType.DMA,
        ],
        compiler_params=pltpu.CompilerParams(vmem_limit_bytes=56 * 2**20),
        name="attend",
    )(safe, *[in_vmem(v) for v in (pay, mine, other, gram_hi, gram_lo, qk)], out_weight)


def finish_kernel(
    step, sig_ref, state_ref, in_ref, cond_ref, part_ref, got_ref, gain_ref, final_ref, fresh_ref, est_ref, sent_ref, prev_ref
):
    state = state_ref[...]
    y = dot(state.astype(BF), in_ref[...]) + cond_ref[2 * step : 2 * step + 1, :]
    y = y + part_ref[...] + got_ref[...].astype(F32)
    scale = lax.rsqrt(jnp.mean(y * y, axis=1, keepdims=True) + EPS)
    velocity = dot((y * scale * gain_ref[...]).astype(BF), final_ref[...])
    est_ref[...] = state - sig_ref[0] * velocity
    renewed = state + sig_ref[1] * velocity
    sent_ref[...] = jnp.where(lax.axis_index("frame") == 0, fresh_ref[step], renewed)
    prev_ref[...] = renewed.astype(BF)


def finish(step, sig, state, in_weight, cond, part, got, gain, final_weight, fresh):
    out = jax.ShapeDtypeStruct(state.shape, F32)
    return pl.pallas_call(
        functools.partial(finish_kernel, step),
        out_shape=(out, out, jax.ShapeDtypeStruct(state.shape, BF)),
        in_specs=[SMEM] + [VMEM] * 8,
        out_specs=(VMEM,) * 3,
        compiler_params=pltpu.CompilerParams(vmem_limit_bytes=32 * 2**20),
        name="finish",
    )(sig, state, in_weight, in_vmem(cond), in_vmem(part), in_vmem(got), gain, final_weight, fresh)


def passed_along(x, by):
    peers = lax.axis_size("frame")
    return lax.ppermute(x, "frame", [(i, (i + by) % peers) for i in range(peers)])


def swapped(x):
    return lax.ppermute(x, "core", [(0, 1), (1, 0)])


def spread(x):
    return lax.all_to_all(x, ("y", "far"), 0, 0, tiled=True)


def shards(
    latents,
    fresh_noise,
    level_index,
    plan,
    frame_ids,
    in_weight,
    cond_gain,
    norm_gain,
    qkv_weight,
    qk_gain,
    out_weight,
    final_gain,
    final_weight,
):
    half = in_weight.shape[1] // 2
    freq = jnp.exp(-math.log(10000.0) * jnp.arange(half, dtype=F32) / half)
    state = latents[0]
    prev = passed_along(state, 1).astype(BF)
    sent, gram_hi, gram_lo, cond, qk, safe, sig = fold(
        level_index,
        plan,
        frame_ids,
        freq[None],
        jnp.swapaxes(qkv_weight, 1, 2),
        in_weight,
        cond_gain,
        norm_gain[None],
        qk_gain,
        latents,
    )
    pay = spread(sent.at[:, PAY - TOK :, :].set(prev[None]))
    mine = pay[:, PAY - 2 * TOK :, :]
    results = []
    for step in range(STEPS):
        other = swapped(mine)
        part, part_other = attend(step, safe, pay, mine, other, gram_hi, gram_lo, qk, out_weight)
        got = swapped(part_other)
        estimate, out, prev = finish(
            step, sig, state, in_weight, cond, part, got, final_gain[None], final_weight, fresh_noise
        )
        results.append(estimate)
        state = passed_along(out, -1)
        if step + 1 < STEPS:
            both = jnp.concatenate([state.astype(BF), prev], axis=0)
            mine = spread(jnp.broadcast_to(both[None], (CHIPS,) + both.shape))
    return (jnp.stack(results)[:, None], state[None])


def solution(mesh):
    split = Mesh(mesh.devices.reshape(8, 4, 2, 2), ("frame", "y", "far", "core"))
    space = ("y", "far", "core")
    in_specs = (
        P("frame", space, None),
        P(None, space, None),
        P(),
        P(),
        P(),
        P(),
        P(),
        P(),
        P(None, None, space),
        P(),
        P(),
        P(),
        P(),
    )
    out_specs = (P(None, "frame", space, None), P("frame", space, None))
    return jax.shard_map(shards, mesh=split, in_specs=in_specs, out_specs=out_specs, check_vma=False)
```

time: 149 us -> 115 us (0.77)
  the two profiles are of different devices: /device:TPU:96 before, /device:TPU:0 now
where the time goes in v2:
time: 115 us; the launch traced here: 114 us
  Pallas kernels  44.2 us (38%)
  blocking collectives  40.8 us (35%)
  starting transfers between devices  9.03 us (8%)
  waiting for transfers between devices  8.79 us (8%)
  local copies, waits for them, and re-layouts  8.7 us (8%)
  other arithmetic  1.43 us (1%)
    all_to_all x2, blocking collectives, spread(): return lax.all_to_all(x, ('y', 'far'), 0, 0, tiled=True)  40.8 us
    pallas_call x2, Pallas kernels, attend(): pl.pallas_call(functools.partial(attend_kernel, step), out_shape=(pltpu.V...  33.5 us
    unnamed x29, local copies, waits for them, and re-layouts  8.61 us
    ppermute x3, starting transfers between devices, passed_along(): lax.ppermute(x, 'frame', [(i, (i + by) % peers) for i in range(peers)])  8.5 us
    pallas_call x1, Pallas kernels, fold(): pl.pallas_call(fold_kernel, out_shape=(pltpu.VMEM((CHIPS, PAY, FEAT), BF)...  7.71 us
    ppermute x4, waiting for transfers between devices, swapped(): return lax.ppermute(x, 'core', [(0, 1), (1, 0)])  6.22 us
    pallas_call x2, Pallas kernels, finish(): pl.pallas_call(functools.partial(finish_kernel, step), out_shape=(out, ou...  2.99 us
    ppermute x3, waiting for transfers between devices, passed_along(): lax.ppermute(x, 'frame', [(i, (i + by) % peers) for i in range(peers)])  2.56 us
  transfers between devices with their start and end apart: 7, of which 6 were waited for; matrix products, arithmetic and copies ran while one was open for 1% of the time, Pallas kernels for 7%

profile of v2, /device:TPU:0, one launch (start us, length us, event | category | flops | bytes accessed | tf_op | source)
XLA Modules:
  0.0 113.7 jit_solution(1797736974860929921)
XLA Ops:
  0.6 0.8 bitcast_convert_fusion
  1.4 2.0 %collective-permute-start = (bf16[64,128]{1,0:T(8,128)(2,1)S(1)}, bf16[64,128]{1,0:T(8,128)(2,1)S(1)}, u32[]{:S(2)}, u32[]{:S(2)}) collective-permute-start(bf16[64,128]{1,0:T(8,128)(2,1)S(1)} %bitcast_convert_fusion), channel_id=1, source_target_pairs={{0,16},{16,32},{32,48},{48,64},{64,80},{80,96},{96,112},{112,0},{1... | collective-permute-start | bytes 49160 | tf_op jit(solution)/shard_map/ppermute | solution.py:374
  3.4 0.0 copy-start
  3.4 1.1 copy-done
  4.6 0.0 copy-start.2
  4.6 2.0 %copy-done.2 = bf16[3,3072,192]{1,2,0:T(8,128)(2,1)S(1)} copy-done((bf16[3,3072,192]{1,2,0:T(8,128)(2,1)S(1)}, bf16[3,3072,192]{1,2,0:T(8,128)(2,1)}, u32[]{:S(2)}) %copy-start.2) | copy-done | bytes 3538968
  6.6 0.0 copy-start.4
  6.6 0.8 copy-done.4
  7.3 0.0 copy-start.8
  7.3 0.7 copy-done.8
  8.1 0.0 copy-start.9
  8.1 0.7 copy-done.9
  8.8 0.0 copy-start.10
  8.8 0.7 copy-done.10
  9.4 0.0 copy-start.11
  9.4 0.7 copy-done.11
  10.1 0.0 copy-start.12
  10.1 0.7 copy-done.12
  10.8 0.0 copy-start.13
  10.8 0.7 copy-done.13
  11.4 7.7 %fold.1 = (bf16[8,752,128]{2,1,0:T(8,128)(2,1)S(1)}, bf16[256,256]{1,0:T(8,128)(2,1)S(1)}, bf16[256,256]{1,0:T(8,128)(2,1)S(1)}, f32[8,3072]{1,0:T(8,128)S(1)}, ...) custom-call(s32[8]{0:T(128)S(1)} %copy-done.11, s32[48]{0:T(128)S(1)} %copy-done.12, s32[10]{0:T(128)S(1)} %copy-done.13, ...), custom_call_target="tpu_custom_call" | custom-call | tf_op jit(solution)/shard_map/fold/pallas_call | solution.py:155
  19.1 0.0 collective-permute-done
  19.2 28.9 %all_to_all.10.pay_ref = bf16[8,752,128]{2,1,0:T(8,128)(2,1)S(1)} all-to-all(bf16[8,752,128]{2,1,0:T(8,128)(2,1)S(1)} %broadcast_dynamic-update-slice_fusion), channel_id=1, replica_groups=mesh['frame'=8,'y'=4,'far'=2,'core'=2] {'y','far'}, dimensions={0} | all-to-all | bytes 3080192 | tf_op jit(solution)/shard_map/all_to_all | solution.py:382
  48.1 0.1 collective-permute-start.1
  48.2 1.5 %collective-permute-done.1.other_ref = bf16[8,128,128]{2,1,0:T(8,128)(2,1)S(1)} collective-permute-done((bf16[8,128,128]{2,1,0:T(8,128)(2,1)S(1)}, bf16[8,128,128]{2,1,0:T(8,128)(2,1)S(1)}, u32[]{:S(2)}, u32[]{:S(2)}) %collective-permute-start.1) | collective-permute-done | bytes 262176 | tf_op jit(solution)/shard_map/ppermute | solution.py:378
  49.7 0.0 copy-start.7
  49.8 16.9 %attend.2 = (f32[64,3072]{1,0:T(8,128)S(1)}, bf16[64,3072]{1,0:T(8,128)(2,1)S(1)}) custom-call(s32[1]{0:T(128)} %get-tuple-element.32.safe_ref, bf16[8,752,128]{2,1,0:T(8,128)(2,1)S(1)} %all_to_all.10.pay_ref, bf16[8,128,128]{2,1,0:T(8,128)(2,1)S(1)} %slice.26.mine_ref, bf16[8,128,128]{2,1,0:T(8,128)(2,1)S(1)} %collective-permute-done.1.other_ref, ...), custom_call_target="tpu_custom_call" | custom-call | tf_op jit(solution)/shard_map/attend/pallas_call | solution.py:321
  66.7 0.2 collective-permute-start.2
  66.9 1.6 %collective-permute-done.2.got_ref = bf16[64,3072]{1,0:T(8,128)(2,1)S(1)} collective-permute-done((bf16[64,3072]{1,0:T(8,128)(2,1)S(1)}, bf16[64,3072]{1,0:T(8,128)(2,1)S(1)}, u32[]{:S(2)}, u32[]{:S(2)}) %collective-permute-start.2) | collective-permute-done | bytes 393248 | tf_op jit(solution)/shard_map/ppermute | solution.py:378
  68.5 0.0 copy-done.1
  68.5 0.0 copy-done.3
  68.5 0.0 copy-done.5
  68.5 0.0 copy-done.6
  68.5 0.0 copy-done.7
  68.5 1.2 %finish.2 = (f32[64,128]{1,0:T(8,128)S(1)}, f32[64,128]{1,0:T(8,128)S(1)}, bf16[64,128]{1,0:T(8,128)(2,1)S(1)}) custom-call(f32[2]{0:T(128)S(1)} %get-tuple-element.30.sig_ref, f32[64,128]{1,0:T(8,128)S(1)} %bitcast.13, bf16[128,3072]{1,0:T(8,128)(2,1)S(1)} %copy-done.1, f32[8,3072]{1,0:T(8,128)S(1)} %get-tuple-element.31.cond_ref, ...), custom_call_target="tpu_custom_call" | custom-call | tf_op jit(solution)/shard_map/finish/pallas_call | solution.py:362
  69.7 2.7 %collective-permute-start.3 = (f32[64,128]{1,0:T(8,128)S(1)}, f32[64,128]{1,0:T(8,128)S(1)}, u32[]{:S(2)}, u32[]{:S(2)}) collective-permute-start(f32[64,128]{1,0:T(8,128)S(1)} %get-tuple-element.40), channel_id=1, source_target_pairs={{0,112},{16,0},{32,16},{48,32},{64,48},{80,64},{96,80},{112,96},{1... | collective-permute-start | bytes 98312 | tf_op jit(solution)/shard_map/ppermute | solution.py:374
  72.4 1.6 %collective-permute-done.3.state_ref = f32[64,128]{1,0:T(8,128)S(1)} collective-permute-done((f32[64,128]{1,0:T(8,128)S(1)}, f32[64,128]{1,0:T(8,128)S(1)}, u32[]{:S(2)}, u32[]{:S(2)}) %collective-permute-start.3) | collective-permute-done | bytes 32800 | tf_op jit(solution)/shard_map/ppermute | solution.py:374
  74.0 11.9 %all_to_all.11.mine_ref = bf16[8,128,128]{2,1,0:T(8,128)(2,1)S(1)} all-to-all(bf16[8,128,128]{2,1,0:T(8,128)(2,1)S(1)} %broadcast_in_dim.12), channel_id=1, replica_groups=mesh['frame'=8,'y'=4,'far'=2,'core'=2] {'y','far'}, dimensions={0} | all-to-all | bytes 524288 | tf_op jit(solution)/shard_map/all_to_all | solution.py:382
  85.9 0.0 collective-permute-start.4
  85.9 1.5 %collective-permute-done.4.other_ref = bf16[8,128,128]{2,1,0:T(8,128)(2,1)S(1)} collective-permute-done((bf16[8,128,128]{2,1,0:T(8,128)(2,1)S(1)}, bf16[8,128,128]{2,1,0:T(8,128)(2,1)S(1)}, u32[]{:S(2)}, u32[]{:S(2)}) %collective-permute-start.4) | collective-permute-done | bytes 262176 | tf_op jit(solution)/shard_map/ppermute | solution.py:378
  87.4 16.6 %attend.3 = (f32[64,3072]{1,0:T(8,128)S(1)}, bf16[64,3072]{1,0:T(8,128)(2,1)S(1)}) custom-call(s32[1]{0:T(128)} %get-tuple-element.32.safe_ref, bf16[8,752,128]{2,1,0:T(8,128)(2,1)S(1)} %all_to_all.10.pay_ref, bf16[8,128,128]{2,1,0:T(8,128)(2,1)S(1)} %all_to_all.11.mine_ref, bf16[8,128,128]{2,1,0:T(8,128)(2,1)S(1)} %collective-permute-done.4.other_ref, ...), custom_call_target="tpu_custom_call" | custom-call | tf_op jit(solution)/shard_map/attend/pallas_call | solution.py:321
  104.0 0.2 collective-permute-start.5
  104.3 1.6 %collective-permute-done.5.got_ref = bf16[64,3072]{1,0:T(8,128)(2,1)S(1)} collective-permute-done((bf16[64,3072]{1,0:T(8,128)(2,1)S(1)}, bf16[64,3072]{1,0:T(8,128)(2,1)S(1)}, u32[]{:S(2)}, u32[]{:S(2)}) %collective-permute-start.5) | collective-permute-done | bytes 393248 | tf_op jit(solution)/shard_map/ppermute | solution.py:378
  105.8 1.8 %finish.3 = (f32[64,128]{1,0:T(8,128)S(1)}, f32[64,128]{1,0:T(8,128)S(1)}, bf16[64,128]{1,0:T(8,128)(2,1)}) custom-call(f32[2]{0:T(128)S(1)} %get-tuple-element.30.sig_ref, f32[64,128]{1,0:T(8,128)S(1)} %collective-permute-done.3.state_ref, bf16[128,3072]{1,0:T(8,128)(2,1)S(1)} %copy-done.1, f32[8,3072]{1,0:T(8,128)S(1)} %get-tuple-element.31.cond_ref, ...), custom_call_target="tpu_custom_call" | custom-call | tf_op jit(solution)/shard_map/finish/pallas_call | solution.py:362
  107.6 3.8 %collective-permute-start.6 = (f32[64,128]{1,0:T(8,128)S(1)}, f32[64,128]{1,0:T(8,128)S(1)}, u32[]{:S(2)}, u32[]{:S(2)}) collective-permute-start(f32[64,128]{1,0:T(8,128)S(1)} %get-tuple-element.45), channel_id=1, source_target_pairs={{0,112},{16,0},{32,16},{48,32},{64,48},{80,64},{96,80},{112,96},{1... | collective-permute-start | bytes 98312 | tf_op jit(solution)/shard_map/ppermute | solution.py:374
  111.5 0.6 maximum_bitcast_fusion
  112.1 1.0 collective-permute-done.6
  113.1 0.6 copy.18
  (10 shorter events, 0.1 us)
Async XLA Ops:
  1.4 17.7 %collective-permute-start = (bf16[64,128]{1,0:T(8,128)(2,1)S(1)}, bf16[64,128]{1,0:T(8,128)(2,1)S(1)}, u32[]{:S(2)}, u32[]{:S(2)}) collective-permute-start(bf16[64,128]{1,0:T(8,128)(2,1)S(1)} %bitcast_convert_fusion), channel_id=1, source_target_pairs={{0,16},{16,32},{32,48},{48,64},{64,80},{80,96},{96,112},{112,0},{1... | collective-permute-start | bytes 49160 | tf_op jit(solution)/shard_map/ppermute | solution.py:374
  3.4 1.1 copy-start
  4.6 2.0 %copy-start.2 = (bf16[3,3072,192]{1,2,0:T(8,128)(2,1)S(1)}, bf16[3,3072,192]{1,2,0:T(8,128)(2,1)}, u32[]{:S(2)}) copy-start(bf16[3,3072,192]{1,2,0:T(8,128)(2,1)} %param.23) | copy-start | bytes 10616836
  6.6 0.8 copy-start.4
  7.3 0.7 copy-start.8
  8.1 0.7 copy-start.9
  8.8 0.7 copy-start.10
  9.4 0.7 copy-start.11
  10.1 0.7 copy-start.12
  10.8 0.7 copy-start.13
  48.1 1.6 %collective-permute-start.1 = (bf16[8,128,128]{2,1,0:T(8,128)(2,1)S(1)}, bf16[8,128,128]{2,1,0:T(8,128)(2,1)S(1)}, u32[]{:S(2)}, u32[]{:S(2)}) collective-permute-start(bf16[8,128,128]{2,1,0:T(8,128)(2,1)S(1)} %slice.26.mine_ref), channel_id=1, source_target_pairs={{0,1},{1,0},{2,3},{3,2},{4,5},{5,4},{6,7},{7,6},{8,9},{9,8},{10,11... | collective-permute-start | bytes 786440 | tf_op jit(solution)/shard_map/ppermute | solution.py:378
  49.7 18.7 %copy-start.1 = (bf16[128,3072]{1,0:T(8,128)(2,1)S(1)}, bf16[128,3072]{1,0:T(8,128)(2,1)}, u32[]{:S(2)}) copy-start(bf16[128,3072]{1,0:T(8,128)(2,1)} %in_ref.5) | copy-start | bytes 2359300
  49.7 18.7 %copy-start.3 = (bf16[3072,128]{1,0:T(8,128)(2,1)S(1)}, bf16[3072,128]{1,0:T(8,128)(2,1)}, u32[]{:S(2)}) copy-start(bf16[3072,128]{1,0:T(8,128)(2,1)} %final_ref.3) | copy-start | bytes 2359300
  49.7 18.7 %copy-start.5 = (f32[1,64,128]{2,1,0:T(8,128)S(1)}, f32[1,64,128]{2,1,0:T(8,128)}, u32[]{:S(2)}) copy-start(f32[1,64,128]{2,1,0:T(8,128)} %state_ref.1) | copy-start | bytes 98308
  49.7 18.7 %copy-start.6 = (f32[2,64,128]{2,1,0:T(8,128)S(1)}, f32[2,64,128]{2,1,0:T(8,128)}, u32[]{:S(2)}) copy-start(f32[2,64,128]{2,1,0:T(8,128)} %fresh_ref.3) | copy-start | bytes 196612
  49.7 18.8 %copy-start.7 = (f32[3072]{0:T(1024)S(1)}, f32[3072]{0:T(1024)}, u32[]{:S(2)}) copy-start(f32[3072]{0:T(1024)} %param.26) | copy-start | bytes 36868
  66.7 1.8 %collective-permute-start.2 = (bf16[64,3072]{1,0:T(8,128)(2,1)S(1)}, bf16[64,3072]{1,0:T(8,128)(2,1)S(1)}, u32[]{:S(2)}, u32[]{:S(2)}) collective-permute-start(bf16[64,3072]{1,0:T(8,128)(2,1)S(1)} %get-tuple-element.38), channel_id=1, source_target_pairs={{0,1},{1,0},{2,3},{3,2},{4,5},{5,4},{6,7},{7,6},{8,9},{9,8},{10,11... | collective-permute-start | bytes 1179656 | tf_op jit(solution)/shard_map/ppermute | solution.py:378
  69.7 4.3 %collective-permute-start.3 = (f32[64,128]{1,0:T(8,128)S(1)}, f32[64,128]{1,0:T(8,128)S(1)}, u32[]{:S(2)}, u32[]{:S(2)}) collective-permute-start(f32[64,128]{1,0:T(8,128)S(1)} %get-tuple-element.40), channel_id=1, source_target_pairs={{0,112},{16,0},{32,16},{48,32},{64,48},{80,64},{96,80},{112,96},{1... | collective-permute-start | bytes 98312 | tf_op jit(solution)/shard_map/ppermute | solution.py:374
  85.9 1.5 %collective-permute-start.4 = (bf16[8,128,128]{2,1,0:T(8,128)(2,1)S(1)}, bf16[8,128,128]{2,1,0:T(8,128)(2,1)S(1)}, u32[]{:S(2)}, u32[]{:S(2)}) collective-permute-start(bf16[8,128,128]{2,1,0:T(8,128)(2,1)S(1)} %all_to_all.11.mine_ref), channel_id=1, source_target_pairs={{0,1},{1,0},{2,3},{3,2},{4,5},{5,4},{6,7},{7,6},{8,9},{9,8},{10,11... | collective-permute-start | bytes 786440 | tf_op jit(solution)/shard_map/ppermute | solution.py:378
  104.0 1.8 %collective-permute-start.5 = (bf16[64,3072]{1,0:T(8,128)(2,1)S(1)}, bf16[64,3072]{1,0:T(8,128)(2,1)S(1)}, u32[]{:S(2)}, u32[]{:S(2)}) collective-permute-start(bf16[64,3072]{1,0:T(8,128)(2,1)S(1)} %get-tuple-element.43), channel_id=1, source_target_pairs={{0,1},{1,0},{2,3},{3,2},{4,5},{5,4},{6,7},{7,6},{8,9},{9,8},{10,11... | collective-permute-start | bytes 1179656 | tf_op jit(solution)/shard_map/ppermute | solution.py:378
  107.6 5.4 %collective-permute-start.6 = (f32[64,128]{1,0:T(8,128)S(1)}, f32[64,128]{1,0:T(8,128)S(1)}, u32[]{:S(2)}, u32[]{:S(2)}) collective-permute-start(f32[64,128]{1,0:T(8,128)S(1)} %get-tuple-element.45), channel_id=1, source_target_pairs={{0,112},{16,0},{32,16},{48,32},{64,48},{80,64},{96,80},{112,96},{1... | collective-permute-start | bytes 98312 | tf_op jit(solution)/shard_map/ppermute | solution.py:374

commit v3 on v2

--- a/solution.py
+++ b/solution.py
@@ -3,6 +3,7 @@
 
 import jax
 import jax.numpy as jnp
+import numpy as np
 from jax import lax
 from jax.experimental import pallas as pl
 from jax.experimental.pallas import tpu as pltpu
@@ -49,6 +50,10 @@
     return pltpu.with_memory_space_constraint(x, pltpu.VMEM)
 
 
+def in_hbm(x):
+    return pltpu.with_memory_space_constraint(x, pltpu.HBM)
+
+
 def lanes(shape):
     return lax.broadcasted_iota(jnp.int32, shape, len(shape) - 1)
 
@@ -58,16 +63,16 @@
 
 
 def fold_kernel(
-    level_ref,
-    plan_ref,
-    ids_ref,
-    freq_ref,
-    qkv_ref,
-    in_ref,
-    cond_gain_ref,
-    gain_ref,
-    qk_gain_ref,
-    state_ref,
+    level_hbm,
+    plan_hbm,
+    ids_hbm,
+    freq_hbm,
+    qkv_hbm,
+    in_hbm,
+    cond_gain_hbm,
+    gain_hbm,
+    qk_gain_hbm,
+    state_hbm,
     pay_ref,
     gram_hi_ref,
     gram_lo_ref,
@@ -75,12 +80,35 @@
     qk_ref,
     safe_ref,
     sig_ref,
+    level_ref,
+    plan_ref,
+    ids_ref,
+    freq_ref,
     w_ref,
+    in_ref,
+    cond_gain_ref,
+    gain_ref,
+    qk_gain_ref,
+    state_ref,
     sems,
 ):
-    copies = [pltpu.make_async_copy(qkv_ref.at[j], w_ref.at[j], sems.at[j]) for j in range(3)]
+    pairs = (
+        (level_hbm, level_ref),
+        (plan_hbm, plan_ref),
+        (ids_hbm, ids_ref),
+        (freq_hbm, freq_ref),
+        (in_hbm, in_ref),
+        (qkv_hbm, w_ref),
+        (cond_gain_hbm, cond_gain_ref),
+        (gain_hbm, gain_ref),
+        (qk_gain_hbm, qk_gain_ref),
+        (state_hbm, state_ref),
+    )
+    copies = [pltpu.make_async_copy(src, dst, sems.at[i]) for i, (src, dst) in enumerate(pairs)]
     for copy in copies:
         copy.start()
+    for i in (0, 1, 2, 3):
+        copies[i].wait()
 
     slot = lax.axis_index("frame")
     before = jnp.maximum(slot - 1, 0)
@@ -90,61 +118,60 @@
     sig_ref[0] = sigma
     sig_ref[1] = jnp.where(slot > 0, stamp_prev / 1000.0, 0.0) - sigma
 
+    freq = freq_ref[...]
+    row = rows((8, freq.shape[1]))
+    angle = jnp.where(row == 0, stamp_now, stamp_prev)
+    for step in range(STEPS):
+        angle = jnp.where(row == 2 + 2 * step, ids_ref[slot + step].astype(F32), angle)
+        angle = jnp.where(row == 3 + 2 * step, ids_ref[before + step].astype(F32), angle)
+    angle = angle * freq
+    wave = jnp.concatenate([jnp.cos(angle), jnp.sin(angle)], axis=1)
+
+    for i in (4, 6, 7, 8, 9):
+        copies[i].wait()
     product = qk_gain_ref[0:1, :] * qk_gain_ref[1:2, :]
     safe_ref[0] = (HEAD**0.5 * jnp.max(jnp.abs(product)) <= SAFE).astype(jnp.int32)
     product = product * (math.log2(math.e) / math.sqrt(HEAD))
     qk_ref[...] = jnp.concatenate([product] * 4, axis=1)
 
-    row = rows((8, freq_ref.shape[1]))
-    stamp = jnp.where(row % 2 == 0, stamp_now, stamp_prev)
-    ident = jnp.zeros_like(stamp)
-    for step in range(STEPS):
-        now = ids_ref[slot + step].astype(F32)
-        prev = ids_ref[before + step].astype(F32)
-        ident = jnp.where((row // 2) % 2 == step, jnp.where(row % 2 == 0, now, prev), ident)
-    freq = freq_ref[...]
-    wave_stamp = jnp.concatenate([jnp.cos(stamp * freq), jnp.sin(stamp * freq)], axis=1)
-    wave_ident = jnp.concatenate([jnp.cos(ident * freq), jnp.sin(ident * freq)], axis=1)
-    cond = cond_gain_ref[0:1, :] * wave_stamp + cond_gain_ref[1:2, :] * wave_ident
+    stamps = cond_gain_ref[0:1, :] * wave
+    idents = cond_gain_ref[1:2, :] * wave
+    cond = jnp.concatenate([stamps[0:2] + idents[2:4], stamps[0:2] + idents[4:6]], axis=0)
+    cond = jnp.concatenate([cond, jnp.zeros_like(cond)], axis=0)
     cond_ref[...] = cond
 
     embed = in_ref[...]
+    none = jnp.zeros((112, embed.shape[1]), BF)
     c_hi, c_lo = halves(cond)
-    four = rows(cond.shape) < 4
-    c_hi = jnp.where(four, c_hi.astype(F32), 0.0).astype(BF)
-    c_lo = jnp.where(four, c_lo.astype(F32), 0.0).astype(BF)
-    none = jnp.zeros((120, embed.shape[1]), BF)
-    l_hi = jnp.concatenate([embed, jnp.concatenate([c_hi, none], axis=0)], axis=0)
-    l_lo = jnp.concatenate([jnp.zeros_like(embed), jnp.concatenate([c_lo, none], axis=0)], axis=0)
-    gram = dot_t(l_hi, l_hi) + dot_t(l_hi, l_lo) + dot_t(l_lo, l_hi)
+    left = jnp.concatenate([embed, jnp.concatenate([c_hi, c_lo], axis=0), none], axis=0)
+    gram = dot_t(left, left)
+    lane, row = lanes(gram.shape), rows(gram.shape)
+    gram = jnp.where(lane < FEAT + 8, gram + jnp.where(lane >= FEAT, pltpu.roll(gram, WIDE - 8, 1), 0.0), 0.0)
+    gram = jnp.where(row < FEAT + 8, gram + jnp.where(row >= FEAT, pltpu.roll(gram, WIDE - 8, 0), 0.0), 0.0)
     g_hi, g_lo = halves(gram)
     gram_hi_ref[...] = g_hi
     gram_lo_ref[...] = g_lo
 
     gain = gain_ref[...]
-    emb_hi, emb_lo = halves(embed.astype(F32) * gain)
+    emb = (embed.astype(F32) * gain).astype(BF)
     cg_hi, cg_lo = halves(cond * gain)
-    none = jnp.zeros((112, embed.shape[1]), BF)
-    right = jnp.concatenate([emb_hi, jnp.concatenate([cg_hi, cg_lo], axis=0), none], axis=0)
-    packed = jnp.zeros((PACK, FEAT), F32)
-    for j in range(3):
-        copies[j].wait()
-        full = dot_t(w_ref[j], right)
-        mat = (full[:, 0:FEAT] + dot_t(w_ref[j], emb_lo)).astype(BF)
-        bias = full[:, FEAT:WIDE]
-        bias = bias + pltpu.roll(bias, FEAT - 8, 1)
-        bias = jnp.where(lanes(bias.shape) < 8, bias, 0.0)
-        high = bias.astype(BF).astype(F32)
-        bias = jnp.where(lanes(bias.shape) < 4, high, bias - high)
-        for i in range(4):
-            part = bias[PACK * i : PACK * (i + 1)]
-            shift = 8 * (4 * j + i)
-            packed = packed + (pltpu.roll(part, shift, 1) if shift else part)
-        for chip in range(CHIPS):
-            pay_ref[chip, COLS * j : COLS * (j + 1)] = mat
+    right = jnp.concatenate([emb, jnp.concatenate([cg_hi, cg_lo], axis=0), none], axis=0)
+    copies[5].wait()
+    full = dot_t(w_ref[...].reshape(3 * COLS, embed.shape[1]), right)
+    mat = full[:, 0:FEAT].astype(BF)
+    bias = full[:, FEAT:WIDE]
+    bias = bias + pltpu.roll(bias, FEAT - 8, 1)
+    lane = lanes(bias.shape)
+    bias = jnp.where(lane < 4, bias, 0.0)
+    high = bias.astype(BF).astype(F32)
+    bias = high + pltpu.roll(bias - high, 4, 1)
+    packed = bias[0:PACK]
+    for i in range(1, 12):
+        packed = packed + pltpu.roll(bias[PACK * i : PACK * (i + 1)], 8 * i, 1)
     packed = packed.astype(BF)
     x = state_ref[0].astype(BF)
     for chip in range(CHIPS):
+        pay_ref[chip, 0 : 3 * COLS] = mat
         pay_ref[chip, 3 * COLS : 3 * COLS + PACK] = packed
         pay_ref[chip, 3 * COLS + PACK : PAY - TOK] = x
         pay_ref[chip, PAY - TOK : PAY] = x
@@ -152,6 +179,7 @@
 
 def fold(level_index, plan, frame_ids, freq, qkv, in_weight, cond_gain, gain, qk_gain, latents):
     width = in_weight.shape[1]
+    args = (level_index, plan, frame_ids, freq, qkv, in_weight, cond_gain, gain, qk_gain, latents)
     return pl.pallas_call(
         fold_kernel,
         out_shape=(
@@ -163,12 +191,31 @@
             jax.ShapeDtypeStruct((1,), jnp.int32),
             jax.ShapeDtypeStruct((2,), F32),
         ),
-        in_specs=[SMEM] * 3 + [VMEM, ANY] + [VMEM] * 5,
+        in_specs=[ANY] * len(args),
         out_specs=(VMEM,) * 5 + (SMEM,) * 2,
-        scratch_shapes=[pltpu.VMEM(qkv.shape, BF), pltpu.SemaphoreType.DMA((3,))],
+        scratch_shapes=[pltpu.SMEM(v.shape, v.dtype) for v in args[:3]]
+        + [pltpu.VMEM(v.shape, v.dtype) for v in args[3:]]
+        + [pltpu.SemaphoreType.DMA((len(args),))],
         compiler_params=pltpu.CompilerParams(vmem_limit_bytes=40 * 2**20),
         name="fold",
-    )(level_index, plan, frame_ids, freq, qkv, in_weight, cond_gain, gain, qk_gain, latents)
+    )(*[in_hbm(v) for v in args])
+
+
+def enter_kernel(prev_ref, pay_ref, out_ref):
+    prev = prev_ref[...].astype(BF)
+    for chip in range(CHIPS):
+        out_ref[chip, PAY - TOK : PAY] = prev
+
+
+def enter(prev, pay):
+    return pl.pallas_call(
+        enter_kernel,
+        out_shape=pltpu.VMEM(pay.shape, pay.dtype),
+        in_specs=[VMEM, VMEM],
+        out_specs=VMEM,
+        input_output_aliases={1: 0},
+        name="enter",
+    )(in_vmem(prev), in_vmem(pay))
 
 
 def attend_kernel(
@@ -242,12 +289,11 @@
                 ref[m * COLS + i * PACK : m * COLS + (i + 1) * PACK, FEAT:WIDE] = part.astype(BF)
 
     xq = jnp.concatenate([mine_ref[chip, 0:TOK, :], other_ref[chip, 0:TOK, :]], axis=0)
-    lane = lanes((2 * TOK, FEAT))
-    mark = jnp.logical_or(lane == 2 * step, lane == 4 + 2 * step)
-    xq = jnp.concatenate([xq, mark.astype(F32).astype(BF)], axis=1)
-    square = dot(xq, gram_hi_ref[...]) + dot(xq, gram_lo_ref[...])
-    m_q = jnp.sum(square * xq.astype(F32), axis=1, keepdims=True) * (1.0 / 3072.0) + EPS
-    ones = (rows((WIDE, WIDE)) // HEAD == lanes((WIDE, WIDE)) // HEAD).astype(F32).astype(BF)
+    row = rows((FEAT, 2 * TOK))
+    mark = jnp.logical_or(row == 2 * step, row == 4 + 2 * step)
+    xqt = jnp.concatenate([jnp.transpose(xq), mark.astype(F32).astype(BF)], axis=0)
+    square = dot(gram_hi_ref[...], xqt) + dot(gram_lo_ref[...], xqt)
+    m_q = jnp.sum(square * xqt.astype(F32), axis=0, keepdims=True) * (1.0 / 3072.0) + EPS
     head_of = lanes((2 * TOK, WIDE)) // HEAD
 
     def norms(g, carry):
@@ -260,14 +306,14 @@
 
     lax.fori_loop(0, GROUPS, norms, 0, unroll=True)
 
+    q = dot(aq_ref[...], xqt).reshape(HEADS, HEAD, 2 * TOK)
+    q = q * lax.rsqrt(jnp.sum(q * q, axis=1, keepdims=True) * (1.0 / HEAD) + EPS * m_q[None])
+    q = q.reshape(HEADS * HEAD, 2 * TOK)
     for g in range(GROUPS):
         span = slice(g * WIDE, (g + 1) * WIDE)
-        q = dot_t(xq, aq_ref[span, :])
-        sq_hi, sq_lo = halves(q * q)
-        mean = (dot(sq_hi, ones) + dot(sq_lo, ones)) * (1.0 / HEAD)
-        q = q * lax.rsqrt(mean + EPS * m_q) * qk_ref[...]
-        q = jnp.concatenate([jnp.where(head_of == h, q, 0.0) for h in range(4)], axis=0)
-        qc_ref[g] = dot(q.astype(BF), ak_ref[span, :]).astype(BF)
+        some = jnp.transpose(q[span]) * qk_ref[...]
+        some = jnp.concatenate([jnp.where(head_of == h, some, 0.0) for h in range(4)], axis=0)
+        qc_ref[g] = dot(some.astype(BF), ak_ref[span, :]).astype(BF)
 
     def one_group(g, fast):
         carried = qc_ref[g]
@@ -398,9 +444,9 @@
     final_weight,
 ):
     half = in_weight.shape[1] // 2
-    freq = jnp.exp(-math.log(10000.0) * jnp.arange(half, dtype=F32) / half)
+    freq = jnp.asarray(np.exp(-math.log(10000.0) * np.arange(half, dtype=np.float32) / half), F32)
     state = latents[0]
-    prev = passed_along(state, 1).astype(BF)
+    prev = passed_along(state, 1)
     sent, gram_hi, gram_lo, cond, qk, safe, sig = fold(
         level_index,
         plan,
@@ -413,7 +459,7 @@
         qk_gain,
         latents,
     )
-    pay = spread(sent.at[:, PAY - TOK :, :].set(prev[None]))
+    pay = spread(enter(prev, sent))
     mine = pay[:, PAY - 2 * TOK :, :]
     results = []
     for step in range(STEPS):

time: 115 us -> 101 us (0.88)
  local copies, waits for them, and re-layouts: 8.7 us -> 0.69 us
  Pallas kernels: 44.2 us -> 39.8 us
    unnamed x29 -> x11, local copies, waits for them, and re-layouts: 8.61 us -> 0.64 us
    pallas_call x1, Pallas kernels: 7.71 us -> 4.93 us  [fold(): pl.pallas_call(fold_kernel, out_shape=(pltpu.VMEM((CHIPS, PAY, FEAT), BF)...]
    pallas_call x2, Pallas kernels: 33.5 us -> 31.9 us  [attend(): pl.pallas_call(functools.partial(attend_kernel, step), out_shape=(pltpu.V...]
  transfers between devices with their start and end apart: 7 -> 7, of which waited for: 6 -> 7; matrix products, arithmetic and copies ran while one was open for 1% -> 1% of each run, Pallas kernels for 7% -> 5%
where the time goes in v3:
time: 101 us
  blocking collectives  40.6 us (40%)
  Pallas kernels  39.8 us (39%)
  starting transfers between devices  9.11 us (9%)
  waiting for transfers between devices  9 us (9%)
    all_to_all x2, blocking collectives, spread(): return lax.all_to_all(x, ('y', 'far'), 0, 0, tiled=True)  40.6 us
    pallas_call x2, Pallas kernels, attend(): pl.pallas_call(functools.partial(attend_kernel, step), out_shape=(pltpu.V...  31.9 us
    ppermute x3, starting transfers between devices, passed_along(): lax.ppermute(x, 'frame', [(i, (i + by) % peers) for i in range(peers)])  8.59 us
    ppermute x4, waiting for transfers between devices, swapped(): return lax.ppermute(x, 'core', [(0, 1), (1, 0)])  6.23 us
    pallas_call x1, Pallas kernels, fold(): pl.pallas_call(fold_kernel, out_shape=(pltpu.VMEM((CHIPS, PAY, FEAT), BF)...  4.93 us
    pallas_call x2, Pallas kernels, finish(): pl.pallas_call(functools.partial(finish_kernel, step), out_shape=(out, ou...  2.98 us
    ppermute x3, waiting for transfers between devices, passed_along(): lax.ppermute(x, 'frame', [(i, (i + by) % peers) for i in range(peers)])  2.77 us
  transfers between devices with their start and end apart: 7, of which 7 were waited for; matrix products, arithmetic and copies ran while one was open for 1% of the time, Pallas kernels for 5%

profile of v3, /device:TPU:0, one launch (start us, length us, event | category | flops | bytes accessed | tf_op | source)
XLA Modules:
  0.0 100.6 jit_solution(12262783081783085507)
XLA Ops:
  0.6 2.1 %collective-permute-start = (f32[64,128]{1,0:T(8,128)}, f32[64,128]{1,0:T(8,128)S(1)}, u32[]{:S(2)}, u32[]{:S(2)}) collective-permute-start(f32[64,128]{1,0:T(8,128)} %bitcast.11), channel_id=1, source_target_pairs={{0,16},{16,32},{32,48},{48,64},{64,80},{80,96},{96,112},{112,0},{1... | collective-permute-start | bytes 98312 | tf_op jit(solution)/shard_map/ppermute | solution.py:420
  2.7 4.9 %fold.1 = (bf16[8,752,128]{2,1,0:T(8,128)(2,1)S(1)}, bf16[256,256]{1,0:T(8,128)(2,1)S(1)}, bf16[256,256]{1,0:T(8,128)(2,1)S(1)}, f32[8,3072]{1,0:T(8,128)S(1)}, ...) custom-call(s32[8]{0:T(128)} %level_hbm.1, s32[48]{0:T(128)} %plan_hbm.1, s32[10]{0:T(128)} %ids_hbm.1, ...), custom_call_target="tpu_custom_call" | custom-call | tf_op jit(solution)/shard_map/fold/pallas_call | solution.py:183
  7.6 0.2 collective-permute-done.prev_ref
  7.9 28.7 %all_to_all.10.pay_ref = bf16[8,752,128]{2,1,0:T(8,128)(2,1)S(1)} all-to-all(bf16[8,752,128]{2,1,0:T(8,128)(2,1)S(1)} %enter.1), channel_id=1, replica_groups=mesh['frame'=8,'y'=4,'far'=2,'core'=2] {'y','far'}, dimensions={0} | all-to-all | bytes 3080192 | tf_op jit(solution)/shard_map/all_to_all | solution.py:428
  36.6 0.1 collective-permute-start.1
  36.7 1.5 %collective-permute-done.1.other_ref = bf16[8,128,128]{2,1,0:T(8,128)(2,1)S(1)} collective-permute-done((bf16[8,128,128]{2,1,0:T(8,128)(2,1)S(1)}, bf16[8,128,128]{2,1,0:T(8,128)(2,1)S(1)}, u32[]{:S(2)}, u32[]{:S(2)}) %collective-permute-start.1) | collective-permute-done | bytes 262176 | tf_op jit(solution)/shard_map/ppermute | solution.py:424
  38.2 0.0 copy-start
  38.2 0.0 copy-start.1
  38.2 0.0 copy-start.2
  38.2 0.0 copy-start.3
  38.2 0.0 copy-start.4
  38.3 16.0 %attend.2 = (f32[64,3072]{1,0:T(8,128)S(1)}, bf16[64,3072]{1,0:T(8,128)(2,1)S(1)}) custom-call(s32[1]{0:T(128)} %get-tuple-element.20.safe_ref, bf16[8,752,128]{2,1,0:T(8,128)(2,1)S(1)} %all_to_all.10.pay_ref, bf16[8,128,128]{2,1,0:T(8,128)(2,1)S(1)} %slice.4.mine_ref, bf16[8,128,128]{2,1,0:T(8,128)(2,1)S(1)} %collective-permute-done.1.other_ref, ...), custom_call_target="tpu_custom_call" | custom-call | tf_op jit(solution)/shard_map/attend/pallas_call | solution.py:367
  54.3 0.2 collective-permute-start.2
  54.5 1.6 %collective-permute-done.2.got_ref = bf16[64,3072]{1,0:T(8,128)(2,1)S(1)} collective-permute-done((bf16[64,3072]{1,0:T(8,128)(2,1)S(1)}, bf16[64,3072]{1,0:T(8,128)(2,1)S(1)}, u32[]{:S(2)}, u32[]{:S(2)}) %collective-permute-start.2) | collective-permute-done | bytes 393248 | tf_op jit(solution)/shard_map/ppermute | solution.py:424
  56.1 0.0 copy-done
  56.1 0.0 copy-done.1
  56.1 0.0 copy-done.2
  56.1 0.0 copy-done.3
  56.1 0.0 copy-done.4
  56.1 1.2 %finish.2 = (f32[64,128]{1,0:T(8,128)S(1)}, f32[64,128]{1,0:T(8,128)S(1)}, bf16[64,128]{1,0:T(8,128)(2,1)S(1)}) custom-call(f32[2]{0:T(128)S(1)} %get-tuple-element.18.sig_ref, f32[64,128]{1,0:T(8,128)S(1)} %bitcast.12, bf16[128,3072]{1,0:T(8,128)(2,1)S(1)} %copy-done, f32[8,3072]{1,0:T(8,128)S(1)} %get-tuple-element.19.cond_ref, ...), custom_call_target="tpu_custom_call" | custom-call | tf_op jit(solution)/shard_map/finish/pallas_call | solution.py:408
  57.3 2.7 %collective-permute-start.3 = (f32[64,128]{1,0:T(8,128)S(1)}, f32[64,128]{1,0:T(8,128)S(1)}, u32[]{:S(2)}, u32[]{:S(2)}) collective-permute-start(f32[64,128]{1,0:T(8,128)S(1)} %get-tuple-element.28), channel_id=1, source_target_pairs={{0,112},{16,0},{32,16},{48,32},{64,48},{80,64},{96,80},{112,96},{1... | collective-permute-start | bytes 98312 | tf_op jit(solution)/shard_map/ppermute | solution.py:420
  60.0 1.6 %collective-permute-done.3.state_ref = f32[64,128]{1,0:T(8,128)S(1)} collective-permute-done((f32[64,128]{1,0:T(8,128)S(1)}, f32[64,128]{1,0:T(8,128)S(1)}, u32[]{:S(2)}, u32[]{:S(2)}) %collective-permute-start.3) | collective-permute-done | bytes 32800 | tf_op jit(solution)/shard_map/ppermute | solution.py:420
  61.6 11.9 %all_to_all.11.mine_ref = bf16[8,128,128]{2,1,0:T(8,128)(2,1)S(1)} all-to-all(bf16[8,128,128]{2,1,0:T(8,128)(2,1)S(1)} %broadcast_in_dim.25), channel_id=1, replica_groups=mesh['frame'=8,'y'=4,'far'=2,'core'=2] {'y','far'}, dimensions={0} | all-to-all | bytes 524288 | tf_op jit(solution)/shard_map/all_to_all | solution.py:428
  73.5 0.0 collective-permute-start.4
  73.5 1.5 %collective-permute-done.4.other_ref = bf16[8,128,128]{2,1,0:T(8,128)(2,1)S(1)} collective-permute-done((bf16[8,128,128]{2,1,0:T(8,128)(2,1)S(1)}, bf16[8,128,128]{2,1,0:T(8,128)(2,1)S(1)}, u32[]{:S(2)}, u32[]{:S(2)}) %collective-permute-start.4) | collective-permute-done | bytes 262176 | tf_op jit(solution)/shard_map/ppermute | solution.py:424
  75.0 15.9 %attend.3 = (f32[64,3072]{1,0:T(8,128)S(1)}, bf16[64,3072]{1,0:T(8,128)(2,1)S(1)}) custom-call(s32[1]{0:T(128)} %get-tuple-element.20.safe_ref, bf16[8,752,128]{2,1,0:T(8,128)(2,1)S(1)} %all_to_all.10.pay_ref, bf16[8,128,128]{2,1,0:T(8,128)(2,1)S(1)} %all_to_all.11.mine_ref, bf16[8,128,128]{2,1,0:T(8,128)(2,1)S(1)} %collective-permute-done.4.other_ref, ...), custom_call_target="tpu_custom_call" | custom-call | tf_op jit(solution)/shard_map/attend/pallas_call | solution.py:367
  91.0 0.2 collective-permute-start.5
  91.2 1.6 %collective-permute-done.5.got_ref = bf16[64,3072]{1,0:T(8,128)(2,1)S(1)} collective-permute-done((bf16[64,3072]{1,0:T(8,128)(2,1)S(1)}, bf16[64,3072]{1,0:T(8,128)(2,1)S(1)}, u32[]{:S(2)}, u32[]{:S(2)}) %collective-permute-start.5) | collective-permute-done | bytes 393248 | tf_op jit(solution)/shard_map/ppermute | solution.py:424
  92.8 1.8 %finish.3 = (f32[64,128]{1,0:T(8,128)S(1)}, f32[64,128]{1,0:T(8,128)S(1)}, bf16[64,128]{1,0:T(8,128)(2,1)}) custom-call(f32[2]{0:T(128)S(1)} %get-tuple-element.18.sig_ref, f32[64,128]{1,0:T(8,128)S(1)} %collective-permute-done.3.state_ref, bf16[128,3072]{1,0:T(8,128)(2,1)S(1)} %copy-done, f32[8,3072]{1,0:T(8,128)S(1)} %get-tuple-element.19.cond_ref, ...), custom_call_target="tpu_custom_call" | custom-call | tf_op jit(solution)/shard_map/finish/pallas_call | solution.py:408
  94.6 3.8 %collective-permute-start.6 = (f32[64,128]{1,0:T(8,128)S(1)}, f32[64,128]{1,0:T(8,128)S(1)}, u32[]{:S(2)}, u32[]{:S(2)}) collective-permute-start(f32[64,128]{1,0:T(8,128)S(1)} %get-tuple-element.33), channel_id=1, source_target_pairs={{0,112},{16,0},{32,16},{48,32},{64,48},{80,64},{96,80},{112,96},{1... | collective-permute-start | bytes 98312 | tf_op jit(solution)/shard_map/ppermute | solution.py:420
  98.4 0.6 maximum_bitcast_fusion
  99.0 1.0 collective-permute-done.6
  100.0 0.6 copy.20
  (5 shorter events, 0.1 us)
Async XLA Ops:
  0.6 7.2 %collective-permute-start = (f32[64,128]{1,0:T(8,128)}, f32[64,128]{1,0:T(8,128)S(1)}, u32[]{:S(2)}, u32[]{:S(2)}) collective-permute-start(f32[64,128]{1,0:T(8,128)} %bitcast.11), channel_id=1, source_target_pairs={{0,16},{16,32},{32,48},{48,64},{64,80},{80,96},{96,112},{112,0},{1... | collective-permute-start | bytes 98312 | tf_op jit(solution)/shard_map/ppermute | solution.py:420
  36.6 1.6 %collective-permute-start.1 = (bf16[8,128,128]{2,1,0:T(8,128)(2,1)S(1)}, bf16[8,128,128]{2,1,0:T(8,128)(2,1)S(1)}, u32[]{:S(2)}, u32[]{:S(2)}) collective-permute-start(bf16[8,128,128]{2,1,0:T(8,128)(2,1)S(1)} %slice.4.mine_ref), channel_id=1, source_target_pairs={{0,1},{1,0},{2,3},{3,2},{4,5},{5,4},{6,7},{7,6},{8,9},{9,8},{10,11... | collective-permute-start | bytes 786440 | tf_op jit(solution)/shard_map/ppermute | solution.py:424
  38.2 17.8 %copy-start = (bf16[128,3072]{1,0:T(8,128)(2,1)S(1)}, bf16[128,3072]{1,0:T(8,128)(2,1)}, u32[]{:S(2)}) copy-start(bf16[128,3072]{1,0:T(8,128)(2,1)} %in_ref.3) | copy-start | bytes 2359300
  38.2 17.8 %copy-start.1 = (bf16[3072,128]{1,0:T(8,128)(2,1)S(1)}, bf16[3072,128]{1,0:T(8,128)(2,1)}, u32[]{:S(2)}) copy-start(bf16[3072,128]{1,0:T(8,128)(2,1)} %final_ref.3) | copy-start | bytes 2359300
  38.2 17.8 %copy-start.2 = (f32[2,64,128]{2,1,0:T(8,128)S(1)}, f32[2,64,128]{2,1,0:T(8,128)}, u32[]{:S(2)}) copy-start(f32[2,64,128]{2,1,0:T(8,128)} %fresh_ref.3) | copy-start | bytes 196612
  38.2 17.8 %copy-start.3 = (f32[1,64,128]{2,1,0:T(8,128)S(1)}, f32[1,64,128]{2,1,0:T(8,128)}, u32[]{:S(2)}) copy-start(f32[1,64,128]{2,1,0:T(8,128)} %state_hbm.1) | copy-start | bytes 98308
  38.2 17.8 %copy-start.4 = (f32[3072]{0:T(1024)S(1)}, f32[3072]{0:T(1024)}, u32[]{:S(2)}) copy-start(f32[3072]{0:T(1024)} %param.25) | copy-start | bytes 36868
  54.3 1.8 %collective-permute-start.2 = (bf16[64,3072]{1,0:T(8,128)(2,1)S(1)}, bf16[64,3072]{1,0:T(8,128)(2,1)S(1)}, u32[]{:S(2)}, u32[]{:S(2)}) collective-permute-start(bf16[64,3072]{1,0:T(8,128)(2,1)S(1)} %get-tuple-element.26), channel_id=1, source_target_pairs={{0,1},{1,0},{2,3},{3,2},{4,5},{5,4},{6,7},{7,6},{8,9},{9,8},{10,11... | collective-permute-start | bytes 1179656 | tf_op jit(solution)/shard_map/ppermute | solution.py:424
  57.3 4.3 %collective-permute-start.3 = (f32[64,128]{1,0:T(8,128)S(1)}, f32[64,128]{1,0:T(8,128)S(1)}, u32[]{:S(2)}, u32[]{:S(2)}) collective-permute-start(f32[64,128]{1,0:T(8,128)S(1)} %get-tuple-element.28), channel_id=1, source_target_pairs={{0,112},{16,0},{32,16},{48,32},{64,48},{80,64},{96,80},{112,96},{1... | collective-permute-start | bytes 98312 | tf_op jit(solution)/shard_map/ppermute | solution.py:420
  73.5 1.5 %collective-permute-start.4 = (bf16[8,128,128]{2,1,0:T(8,128)(2,1)S(1)}, bf16[8,128,128]{2,1,0:T(8,128)(2,1)S(1)}, u32[]{:S(2)}, u32[]{:S(2)}) collective-permute-start(bf16[8,128,128]{2,1,0:T(8,128)(2,1)S(1)} %all_to_all.11.mine_ref), channel_id=1, source_target_pairs={{0,1},{1,0},{2,3},{3,2},{4,5},{5,4},{6,7},{7,6},{8,9},{9,8},{10,11... | collective-permute-start | bytes 786440 | tf_op jit(solution)/shard_map/ppermute | solution.py:424
  91.0 1.8 %collective-permute-start.5 = (bf16[64,3072]{1,0:T(8,128)(2,1)S(1)}, bf16[64,3072]{1,0:T(8,128)(2,1)S(1)}, u32[]{:S(2)}, u32[]{:S(2)}) collective-permute-start(bf16[64,3072]{1,0:T(8,128)(2,1)S(1)} %get-tuple-element.31), channel_id=1, source_target_pairs={{0,1},{1,0},{2,3},{3,2},{4,5},{5,4},{6,7},{7,6},{8,9},{9,8},{10,11... | collective-permute-start | bytes 1179656 | tf_op jit(solution)/shard_map/ppermute | solution.py:424
  94.6 5.4 %collective-permute-start.6 = (f32[64,128]{1,0:T(8,128)S(1)}, f32[64,128]{1,0:T(8,128)S(1)}, u32[]{:S(2)}, u32[]{:S(2)}) collective-permute-start(f32[64,128]{1,0:T(8,128)S(1)} %get-tuple-element.33), channel_id=1, source_target_pairs={{0,112},{16,0},{32,16},{48,32},{64,48},{80,64},{96,80},{112,96},{1... | collective-permute-start | bytes 98312 | tf_op jit(solution)/shard_map/ppermute | solution.py:420

commit v4 on v3

--- a/solution.py
+++ b/solution.py
@@ -21,7 +21,7 @@
 PAY = 3 * COLS + PACK + 2 * TOK
 HEADS = CHIPS * 3
 GROUPS = HEADS // 4
-KEYS = 2048
+SIDE = 1024
 ONE = 136
 EPS = 1e-06
 SAFE = 60.0
@@ -48,6 +48,10 @@
 
 def in_vmem(x):
     return pltpu.with_memory_space_constraint(x, pltpu.VMEM)
+
+
+def cost(products, bytes_moved=0):
+    return pl.CostEstimate(flops=2 * products, transcendentals=0, bytes_accessed=bytes_moved)
 
 
 def in_hbm(x):
@@ -218,6 +222,72 @@
     )(in_vmem(prev), in_vmem(pay))
 
 
+def unpack(pay_ref, ref, j):
+    lane = lanes((PACK, FEAT))
+    for m in range(CHIPS):
+        packed = pay_ref[m, 3 * COLS : 3 * COLS + PACK, :].astype(F32)
+        ref[m * COLS : (m + 1) * COLS, 0:FEAT] = pay_ref[m, j * COLS : (j + 1) * COLS, :]
+        for i in range(4):
+            shift = 8 * (4 * j + i)
+            part = pltpu.roll(packed, FEAT - shift, 1) if shift else packed
+            part = jnp.where(lane < 8, part, 0.0)
+            ref[m * COLS + i * PACK : m * COLS + (i + 1) * PACK, FEAT:WIDE] = part.astype(BF)
+
+
+def prepare(step, first, block_ref, gram_hi_ref, gram_lo_ref, ak_ref, xkt_ref, val_ref, rk_ref):
+    half = CHIPS * TOK
+    own = block_ref[:, 0:TOK, :].reshape(half, FEAT)
+    prev = block_ref[:, TOK : 2 * TOK, :].reshape(half, FEAT)
+    prev = jnp.where(first, own, prev)
+    x = jnp.concatenate([own, prev], axis=0)
+    group = (rows((SIDE, FEAT)) >= half).astype(jnp.int32)
+    lane = lanes((SIDE, FEAT))
+    mark = jnp.logical_or(lane == 2 * step + group, lane == 4 + 2 * step + group)
+    xk = jnp.concatenate([x, mark.astype(F32).astype(BF)], axis=1)
+    group = (lanes((FEAT, SIDE)) >= half).astype(jnp.int32)
+    row = rows((FEAT, SIDE))
+    mark = jnp.logical_or(row == 2 * step + group, row == 4 + 2 * step + group)
+    xkt_ref[0:FEAT, :] = jnp.transpose(x)
+    xkt_ref[FEAT:WIDE, :] = mark.astype(F32).astype(BF)
+    xkt = xkt_ref[...]
+    square = dot(gram_hi_ref[...], xkt) + dot(gram_lo_ref[...], xkt)
+    m_row = jnp.sum(square * xkt.astype(F32), axis=0, keepdims=True) * (1.0 / 3072.0) + EPS
+    r_col = jnp.transpose(jnp.broadcast_to(lax.rsqrt(m_row), (8, SIDE)))[:, 0:1]
+    val = jnp.where(lanes((SIDE, WIDE)) == ONE, 1.0, xk.astype(F32) * r_col)
+    val_ref[...] = val.astype(BF)
+    for g in range(GROUPS):
+        u = dot(ak_ref[g * WIDE : (g + 1) * WIDE, :], xkt_ref[...])
+        u = jnp.sum((u * u).reshape(4, HEAD, SIDE), axis=1)
+        rk = lax.rsqrt(u * (1.0 / HEAD) + EPS * m_row)
+        rk_ref[g] = jnp.concatenate([rk, rk], axis=0)
+
+
+def prepare_kernel(step, pay_ref, block_ref, gram_hi_ref, gram_lo_ref, ak_ref, xkt_ref, val_ref, rk_ref):
+    unpack(pay_ref, ak_ref, 1)
+    first = lax.axis_index("frame") == 0
+    prepare(step, first, block_ref, gram_hi_ref, gram_lo_ref, ak_ref, xkt_ref, val_ref, rk_ref)
+
+
+def side_shapes():
+    return [
+        pltpu.VMEM((WIDE, SIDE), BF),
+        pltpu.VMEM((SIDE, WIDE), BF),
+        pltpu.VMEM((GROUPS, 8, SIDE), F32),
+    ]
+
+
+def prepared(step, pay, block, gram_hi, gram_lo):
+    return pl.pallas_call(
+        functools.partial(prepare_kernel, step),
+        out_shape=[pltpu.VMEM((HEADS * HEAD, WIDE), BF)] + side_shapes(),
+        in_specs=[VMEM] * 4,
+        out_specs=[VMEM] * 4,
+        compiler_params=pltpu.CompilerParams(vmem_limit_bytes=24 * 2**20),
+        cost_estimate=cost(HEADS * HEAD * WIDE * SIDE, 2 * CHIPS * PAY * FEAT),
+        name="prepare",
+    )(*[in_vmem(v) for v in (pay, block, gram_hi, gram_lo)])
+
+
 def attend_kernel(
     step,
     safe_ref,
@@ -227,16 +297,18 @@
     gram_hi_ref,
     gram_lo_ref,
     qk_ref,
+    ak_ref,
+    xkt_a_ref,
+    val_a_ref,
+    rk_a_ref,
     out_w_ref,
     part_ref,
     part_other_ref,
-    xk_ref,
-    xkt_ref,
-    val_ref,
+    xkt_b_ref,
+    val_b_ref,
+    rk_b_ref,
     aq_ref,
-    ak_ref,
     av_ref,
-    rk_ref,
     p_ref,
     s_ref,
     qc_ref,
@@ -252,42 +324,12 @@
         copies.append(pltpu.make_async_copy(out_w_ref.at[pl.ds(begin, COLS)], w_ref.at[pl.ds(m * COLS, COLS)], sem))
     for copy in copies:
         copy.start()
-
-    half = CHIPS * TOK
-    for group in range(2):
-        for side, ref in enumerate((mine_ref, other_ref)):
-            base = (2 * group + side) * half
-            block = ref[:, TOK * group : TOK * (group + 1), :].reshape(half, FEAT)
-            if group == 1:
-                block = jnp.where(first, ref[:, 0:TOK, :].reshape(half, FEAT), block)
-            xk_ref[base : base + half, 0:FEAT] = block
-        lane = lanes((KEYS // 2, FEAT))
-        mark = jnp.logical_or(lane == 2 * step + group, lane == 4 + 2 * step + group)
-        xk_ref[group * KEYS // 2 : (group + 1) * KEYS // 2, FEAT:WIDE] = mark.astype(F32).astype(BF)
-    xkt_ref[0:FEAT, :] = jnp.transpose(xk_ref[:, 0:FEAT])
-    row = rows((FEAT, KEYS))
-    group = (lanes((FEAT, KEYS)) >= KEYS // 2).astype(jnp.int32)
-    mark = jnp.logical_or(row == 2 * step + group, row == 4 + 2 * step + group)
-    xkt_ref[FEAT:WIDE, :] = mark.astype(F32).astype(BF)
-
-    xkt = xkt_ref[...]
-    square = dot(gram_hi_ref[...], xkt) + dot(gram_lo_ref[...], xkt)
-    m_row = jnp.sum(square * xkt.astype(F32), axis=0, keepdims=True) * (1.0 / 3072.0) + EPS
-    r_col = jnp.transpose(jnp.broadcast_to(lax.rsqrt(m_row), (8, KEYS)))[:, 0:1]
-    val = xk_ref[...].astype(F32) * r_col
-    val_ref[...] = jnp.where(lanes((KEYS, WIDE)) == ONE, 1.0, val).astype(BF)
-
-    lane = lanes((PACK, FEAT))
-    for m in range(CHIPS):
-        packed = pay_ref[m, 3 * COLS : 3 * COLS + PACK, :].astype(F32)
-        for j, ref in enumerate((aq_ref, ak_ref, av_ref)):
-            ref[m * COLS : (m + 1) * COLS, 0:FEAT] = pay_ref[m, j * COLS : (j + 1) * COLS, :]
-            for i in range(4):
-                shift = 8 * (4 * j + i)
-                part = pltpu.roll(packed, FEAT - shift, 1) if shift else packed
-                part = jnp.where(lane < 8, part, 0.0)
-                ref[m * COLS + i * PACK : m * COLS + (i + 1) * PACK, FEAT:WIDE] = part.astype(BF)
-
+    sides = ((xkt_a_ref, val_a_ref, rk_a_ref), (xkt_b_ref, val_b_ref, rk_b_ref))
+    spans = (slice(0, SIDE), slice(SIDE, 2 * SIDE))
+    prepare(step, first, other_ref, gram_hi_ref, gram_lo_ref, ak_ref, *sides[1])
+
+    unpack(pay_ref, aq_ref, 0)
+    unpack(pay_ref, av_ref, 2)
     xq = jnp.concatenate([mine_ref[chip, 0:TOK, :], other_ref[chip, 0:TOK, :]], axis=0)
     row = rows((FEAT, 2 * TOK))
     mark = jnp.logical_or(row == 2 * step, row == 4 + 2 * step)
@@ -295,16 +337,6 @@
     square = dot(gram_hi_ref[...], xqt) + dot(gram_lo_ref[...], xqt)
     m_q = jnp.sum(square * xqt.astype(F32), axis=0, keepdims=True) * (1.0 / 3072.0) + EPS
     head_of = lanes((2 * TOK, WIDE)) // HEAD
-
-    def norms(g, carry):
-        begin = pl.multiple_of(g * WIDE, WIDE)
-        u = dot(ak_ref[pl.ds(begin, WIDE), :], xkt_ref[...])
-        u = jnp.sum((u * u).reshape(4, HEAD, KEYS), axis=1)
-        rk = lax.rsqrt(u * (1.0 / HEAD) + EPS * m_row)
-        rk_ref[g] = jnp.concatenate([rk, rk], axis=0)
-        return carry
-
-    lax.fori_loop(0, GROUPS, norms, 0, unroll=True)
 
     q = dot(aq_ref[...], xqt).reshape(HEADS, HEAD, 2 * TOK)
     q = q * lax.rsqrt(jnp.sum(q * q, axis=1, keepdims=True) * (1.0 / HEAD) + EPS * m_q[None])
@@ -315,34 +347,42 @@
         some = jnp.concatenate([jnp.where(head_of == h, some, 0.0) for h in range(4)], axis=0)
         qc_ref[g] = dot(some.astype(BF), ak_ref[span, :]).astype(BF)
 
-    def one_group(g, fast):
-        carried = qc_ref[g]
-        rk = rk_ref[g]
+    def weigh(g):
         for h in range(4):
             span = slice(2 * TOK * h, 2 * TOK * (h + 1))
-            s = dot(carried[span], xkt_ref[...]) * rk[h : h + 1]
-            if not fast:
-                s_ref[...] = s
-                s = s_ref[...]
-                s = s - jnp.max(s, axis=1, keepdims=True)
-            p_ref[span, :] = jnp.exp2(s).astype(BF)
+            for (xkt_ref, _, rk_ref), keys in zip(sides, spans):
+                s = dot(qc_ref[g, span], xkt_ref[...]) * rk_ref[g, h : h + 1, :]
+                p_ref[span, keys] = jnp.exp2(s).astype(BF)
+
+    def weigh_wide(g):
         for h in range(4):
             span = slice(2 * TOK * h, 2 * TOK * (h + 1))
-            z = dot(p_ref[span, :], val_ref[...])
+            for (xkt_ref, _, rk_ref), keys in zip(sides, spans):
+                s_ref[:, keys] = dot(qc_ref[g, span], xkt_ref[...]) * rk_ref[g, h : h + 1, :]
+            s = s_ref[...]
+            p_ref[span, :] = jnp.exp2(s - jnp.max(s, axis=1, keepdims=True)).astype(BF)
+
+    def collect(g):
+        for h in range(4):
+            span = slice(2 * TOK * h, 2 * TOK * (h + 1))
+            z = dot(p_ref[span, spans[0]], val_a_ref[...]) + dot(p_ref[span, spans[1]], val_b_ref[...])
             z_ref[g, span] = (z * (1.0 / z[:, ONE : ONE + 1])).astype(BF)
 
     @pl.when(safe_ref[0] == 1)
     def _():
-        def body(g, carry):
-            one_group(g, True)
+        def body(i, carry):
+            for k in range(3):
+                weigh(3 * i + k)
+                collect(3 * i + k)
             return carry
 
-        lax.fori_loop(0, GROUPS, body, 0, unroll=3)
+        lax.fori_loop(0, GROUPS // 3, body, 0)
 
     @pl.when(safe_ref[0] != 1)
     def _():
         def body(g, carry):
-            one_group(g, False)
+            weigh_wide(g)
+            collect(g)
             return carry
 
         lax.fori_loop(0, GROUPS, body, 0)
@@ -361,32 +401,30 @@
     part_other_ref[...] = y[TOK:].astype(BF)
 
 
-def attend(step, safe, pay, mine, other, gram_hi, gram_lo, qk, out_weight):
+def attend(step, safe, pay, mine, other, gram_hi, gram_lo, qk, ready, out_weight):
     width = out_weight.shape[1]
     half = HEADS * HEAD
+    held = [in_vmem(v) for v in (pay, mine, other, gram_hi, gram_lo, qk, *ready)]
     return pl.pallas_call(
         functools.partial(attend_kernel, step),
         out_shape=(pltpu.VMEM((TOK, width), F32), pltpu.VMEM((TOK, width), BF)),
-        in_specs=[SMEM] + [VMEM] * 6 + [ANY],
+        in_specs=[SMEM] + [VMEM] * len(held) + [ANY],
         out_specs=(VMEM, VMEM),
-        scratch_shapes=[
-            pltpu.VMEM((KEYS, WIDE), BF),
-            pltpu.VMEM((WIDE, KEYS), BF),
-            pltpu.VMEM((KEYS, WIDE), BF),
+        scratch_shapes=side_shapes()
+        + [
             pltpu.VMEM((half, WIDE), BF),
             pltpu.VMEM((half, WIDE), BF),
-            pltpu.VMEM((half, WIDE), BF),
-            pltpu.VMEM((GROUPS, 8, KEYS), F32),
-            pltpu.VMEM((512, KEYS), BF),
-            pltpu.VMEM((128, KEYS), F32),
-            pltpu.VMEM((GROUPS, 512, WIDE), BF),
-            pltpu.VMEM((GROUPS, 512, WIDE), BF),
+            pltpu.VMEM((8 * TOK, 2 * SIDE), BF),
+            pltpu.VMEM((2 * TOK, 2 * SIDE), F32),
+            pltpu.VMEM((GROUPS, 8 * TOK, WIDE), BF),
+            pltpu.VMEM((GROUPS, 8 * TOK, WIDE), BF),
             pltpu.VMEM((half, width), BF),
             pltpu.SemaphoreType.DMA,
         ],
-        compiler_params=pltpu.CompilerParams(vmem_limit_bytes=56 * 2**20),
+        compiler_params=pltpu.CompilerParams(vmem_limit_bytes=48 * 2**20),
+        cost_estimate=cost(HEADS * 2 * TOK * WIDE * 4 * SIDE),
         name="attend",
-    )(safe, *[in_vmem(v) for v in (pay, mine, other, gram_hi, gram_lo, qk)], out_weight)
+    )(safe, *held, out_weight)
 
 
 def finish_kernel(
@@ -412,7 +450,7 @@
         out_specs=(VMEM,) * 3,
         compiler_params=pltpu.CompilerParams(vmem_limit_bytes=32 * 2**20),
         name="finish",
-    )(sig, state, in_weight, in_vmem(cond), in_vmem(part), in_vmem(got), gain, final_weight, fresh)
+    )(sig, *[in_vmem(v) for v in (state, in_weight, cond, part, got, gain, final_weight, fresh)])
 
 
 def passed_along(x, by):
@@ -464,7 +502,8 @@
     results = []
     for step in range(STEPS):
         other = swapped(mine)
-        part, part_other = attend(step, safe, pay, mine, other, gram_hi, gram_lo, qk, out_weight)
+        ready = prepared(step, pay, mine, gram_hi, gram_lo)
+        part, part_other = attend(step, safe, pay, mine, other, gram_hi, gram_lo, qk, ready, out_weight)
         got = swapped(part_other)
         estimate, out, prev = finish(
             step, sig, state, in_weight, cond, part, got, final_gain[None], final_weight, fresh_noise

time: 101 us -> 100 us (0.990)
  waiting for transfers between devices: 9 us -> 5.48 us
  Pallas kernels: 39.8 us -> 41.5 us
    ppermute x4, waiting for transfers between devices: 6.23 us -> 2.7 us  [swapped(): return lax.ppermute(x, 'core', [(0, 1), (1, 0)])]
    pallas_call x0 -> x2, Pallas kernels: none -> 3.08 us  [prepared(): pl.pallas_call(functools.partial(prepare_kernel, step), out_shape=[pltpu....]
    pallas_call x2, Pallas kernels: 31.9 us -> 30.5 us  [attend(): pl.pallas_call(functools.partial(attend_kernel, step), out_shape=(pltpu.V...]
  transfers between devices with their start and end apart: 7 -> 7, of which waited for: 7 -> 5; matrix products, arithmetic and copies ran while one was open for 1% -> 1% of each run, Pallas kernels for 5% -> 8%
where the time goes in v4:
time: 100 us; the launch traced here: 99.6 us
  Pallas kernels  41.5 us (42%)
  blocking collectives  40.6 us (41%)
  starting transfers between devices  9.88 us (10%)
  waiting for transfers between devices  5.48 us (5%)
    all_to_all x2, blocking collectives, spread(): return lax.all_to_all(x, ('y', 'far'), 0, 0, tiled=True)  40.6 us
    pallas_call x2, Pallas kernels, attend(): pl.pallas_call(functools.partial(attend_kernel, step), out_shape=(pltpu.V...  30.5 us
    ppermute x3, starting transfers between devices, passed_along(): lax.ppermute(x, 'frame', [(i, (i + by) % peers) for i in range(peers)])  8.63 us
    pallas_call x1, Pallas kernels, fold(): pl.pallas_call(fold_kernel, out_shape=(pltpu.VMEM((CHIPS, PAY, FEAT), BF)...  4.93 us
    pallas_call x2, Pallas kernels, prepared(): pl.pallas_call(functools.partial(prepare_kernel, step), out_shape=[pltpu....  3.08 us
    pallas_call x2, Pallas kernels, finish(): pl.pallas_call(functools.partial(finish_kernel, step), out_shape=(out, ou...  3 us
    ppermute x3, waiting for transfers between devices, passed_along(): lax.ppermute(x, 'frame', [(i, (i + by) % peers) for i in range(peers)])  2.77 us
    ppermute x4, waiting for transfers between devices, swapped(): return lax.ppermute(x, 'core', [(0, 1), (1, 0)])  2.7 us
  transfers between devices with their start and end apart: 7, of which 5 were waited for; matrix products, arithmetic and copies ran while one was open for 1% of the time, Pallas kernels for 8%

profile of v4, /device:TPU:0, one launch (start us, length us, event | category | flops | bytes accessed | tf_op | source)
XLA Modules:
  0.0 99.6 jit_solution(6030010979500428918)
XLA Ops:
  0.6 2.1 %collective-permute-start = (f32[64,128]{1,0:T(8,128)}, f32[64,128]{1,0:T(8,128)S(1)}, u32[]{:S(2)}, u32[]{:S(2)}) collective-permute-start(f32[64,128]{1,0:T(8,128)} %bitcast.11), channel_id=1, source_target_pairs={{0,16},{16,32},{32,48},{48,64},{64,80},{80,96},{96,112},{112,0},{1... | collective-permute-start | bytes 98312 | tf_op jit(solution)/shard_map/ppermute | solution.py:458
  2.7 4.9 %fold.1 = (bf16[8,752,128]{2,1,0:T(8,128)(2,1)S(1)}, bf16[256,256]{1,0:T(8,128)(2,1)S(1)}, bf16[256,256]{1,0:T(8,128)(2,1)S(1)}, f32[8,3072]{1,0:T(8,128)S(1)}, ...) custom-call(s32[8]{0:T(128)} %level_hbm.1, s32[48]{0:T(128)} %plan_hbm.1, s32[10]{0:T(128)} %ids_hbm.1, ...), custom_call_target="tpu_custom_call" | custom-call | tf_op jit(solution)/shard_map/fold/pallas_call | solution.py:187
  7.6 0.2 collective-permute-done.prev_ref
  7.9 28.7 %all_to_all.10.pay_ref = bf16[8,752,128]{2,1,0:T(8,128)(2,1)S(1)} all-to-all(bf16[8,752,128]{2,1,0:T(8,128)(2,1)S(1)} %enter.1), channel_id=1, replica_groups=mesh['frame'=8,'y'=4,'far'=2,'core'=2] {'y','far'}, dimensions={0} | all-to-all | bytes 3080192 | tf_op jit(solution)/shard_map/all_to_all | solution.py:466
  36.6 0.1 collective-permute-start.1
  36.7 1.5 %prepare.2 = (bf16[1536,256]{1,0:T(8,128)(2,1)S(1)}, bf16[256,1024]{1,0:T(8,128)(2,1)S(1)}, bf16[1024,256]{1,0:T(8,128)(2,1)S(1)}, f32[6,8,1024]{2,1,0:T(8,128)S(1)}) custom-call(bf16[8,752,128]{2,1,0:T(8,128)(2,1)S(1)} %all_to_all.10.pay_ref, bf16[8,128,128]{2,1,0:T(8,128)(2,1)S(1)} %slice.4.block_ref.mine_ref, ...), custom_call_target="tpu_custom_call" | custom-call | flops 805306368 | bytes 1540096 | tf_op jit(solution)/shard_map/prepare/pallas_call | solution.py:280
  38.3 0.0 collective-permute-done.1.other_ref
  38.3 0.0 copy-start
  38.3 0.0 copy-start.1
  38.3 0.0 copy-start.2
  38.3 0.0 copy-start.3
  38.3 0.0 copy-start.4
  38.3 15.3 %attend.2 = (f32[64,3072]{1,0:T(8,128)S(1)}, bf16[64,3072]{1,0:T(8,128)(2,1)S(1)}) custom-call(s32[1]{0:T(128)} %get-tuple-element.28.safe_ref, bf16[8,752,128]{2,1,0:T(8,128)(2,1)S(1)} %all_to_all.10.pay_ref, bf16[8,128,128]{2,1,0:T(8,128)(2,1)S(1)} %slice.4.block_ref.mine_ref, bf16[8,128,128]{2,1,0:T(8,128)(2,1)S(1)} %collective-permute-done.1.other_ref, ...), custom_call_target="tpu_custom_call" | custom-call | flops 6442450944 | tf_op jit(solution)/shard_map/attend/pallas_call | solution.py:408
  53.6 0.6 collective-permute-start.2
  54.2 1.3 %collective-permute-done.2.got_ref = bf16[64,3072]{1,0:T(8,128)(2,1)S(1)} collective-permute-done((bf16[64,3072]{1,0:T(8,128)(2,1)S(1)}, bf16[64,3072]{1,0:T(8,128)(2,1)S(1)}, u32[]{:S(2)}, u32[]{:S(2)}) %collective-permute-start.2) | collective-permute-done | bytes 393248 | tf_op jit(solution)/shard_map/ppermute | solution.py:462
  55.5 0.0 copy-done
  55.6 0.0 copy-done.1
  55.6 0.0 copy-done.2
  55.6 0.0 copy-done.3
  55.6 0.0 copy-done.4
  55.6 1.2 %finish.2 = (f32[64,128]{1,0:T(8,128)S(1)}, f32[64,128]{1,0:T(8,128)S(1)}, bf16[64,128]{1,0:T(8,128)(2,1)S(1)}) custom-call(f32[2]{0:T(128)S(1)} %get-tuple-element.26.sig_ref, f32[64,128]{1,0:T(8,128)S(1)} %bitcast.12, bf16[128,3072]{1,0:T(8,128)(2,1)S(1)} %copy-done, f32[8,3072]{1,0:T(8,128)S(1)} %get-tuple-element.27.cond_ref, ...), custom_call_target="tpu_custom_call" | custom-call | tf_op jit(solution)/shard_map/finish/pallas_call | solution.py:446
  56.8 2.7 %collective-permute-start.3 = (f32[64,128]{1,0:T(8,128)S(1)}, f32[64,128]{1,0:T(8,128)S(1)}, u32[]{:S(2)}, u32[]{:S(2)}) collective-permute-start(f32[64,128]{1,0:T(8,128)S(1)} %get-tuple-element.40), channel_id=1, source_target_pairs={{0,112},{16,0},{32,16},{48,32},{64,48},{80,64},{96,80},{112,96},{1... | collective-permute-start | bytes 98312 | tf_op jit(solution)/shard_map/ppermute | solution.py:458
  59.5 1.6 %collective-permute-done.3.state_ref = f32[64,128]{1,0:T(8,128)S(1)} collective-permute-done((f32[64,128]{1,0:T(8,128)S(1)}, f32[64,128]{1,0:T(8,128)S(1)}, u32[]{:S(2)}, u32[]{:S(2)}) %collective-permute-start.3) | collective-permute-done | bytes 32800 | tf_op jit(solution)/shard_map/ppermute | solution.py:458
  61.1 11.9 %all_to_all.11.block_ref.mine_ref = bf16[8,128,128]{2,1,0:T(8,128)(2,1)S(1)} all-to-all(bf16[8,128,128]{2,1,0:T(8,128)(2,1)S(1)} %broadcast_in_dim.25), channel_id=1, replica_groups=mesh['frame'=8,'y'=4,'far'=2,'core'=2] {'y','far'}, dimensions={0} | all-to-all | bytes 524288 | tf_op jit(solution)/shard_map/all_to_all | solution.py:466
  73.0 0.0 collective-permute-start.4
  73.0 1.5 %prepare.3 = (bf16[1536,256]{1,0:T(8,128)(2,1)S(1)}, bf16[256,1024]{1,0:T(8,128)(2,1)S(1)}, bf16[1024,256]{1,0:T(8,128)(2,1)S(1)}, f32[6,8,1024]{2,1,0:T(8,128)S(1)}) custom-call(bf16[8,752,128]{2,1,0:T(8,128)(2,1)S(1)} %all_to_all.10.pay_ref, bf16[8,128,128]{2,1,0:T(8,128)(2,1)S(1)} %all_to_all.11.block_ref.mine_ref, ...), custom_call_target="tpu_custom_call" | custom-call | flops 805306368 | bytes 1540096 | tf_op jit(solution)/shard_map/prepare/pallas_call | solution.py:280
  74.6 0.0 collective-permute-done.4.other_ref
  74.6 15.2 %attend.3 = (f32[64,3072]{1,0:T(8,128)S(1)}, bf16[64,3072]{1,0:T(8,128)(2,1)S(1)}) custom-call(s32[1]{0:T(128)} %get-tuple-element.28.safe_ref, bf16[8,752,128]{2,1,0:T(8,128)(2,1)S(1)} %all_to_all.10.pay_ref, bf16[8,128,128]{2,1,0:T(8,128)(2,1)S(1)} %all_to_all.11.block_ref.mine_ref, bf16[8,128,128]{2,1,0:T(8,128)(2,1)S(1)} %collective-permute-done.4.other_ref, ...), custom_call_target="tpu_custom_call" | custom-call | flops 6442450944 | tf_op jit(solution)/shard_map/attend/pallas_call | solution.py:408
  89.8 0.6 collective-permute-start.5
  90.4 1.3 %collective-permute-done.5.got_ref = bf16[64,3072]{1,0:T(8,128)(2,1)S(1)} collective-permute-done((bf16[64,3072]{1,0:T(8,128)(2,1)S(1)}, bf16[64,3072]{1,0:T(8,128)(2,1)S(1)}, u32[]{:S(2)}, u32[]{:S(2)}) %collective-permute-start.5) | collective-permute-done | bytes 393248 | tf_op jit(solution)/shard_map/ppermute | solution.py:462
  91.7 1.8 %finish.3 = (f32[64,128]{1,0:T(8,128)S(1)}, f32[64,128]{1,0:T(8,128)S(1)}, bf16[64,128]{1,0:T(8,128)(2,1)}) custom-call(f32[2]{0:T(128)S(1)} %get-tuple-element.26.sig_ref, f32[64,128]{1,0:T(8,128)S(1)} %collective-permute-done.3.state_ref, bf16[128,3072]{1,0:T(8,128)(2,1)S(1)} %copy-done, f32[8,3072]{1,0:T(8,128)S(1)} %get-tuple-element.27.cond_ref, ...), custom_call_target="tpu_custom_call" | custom-call | tf_op jit(solution)/shard_map/finish/pallas_call | solution.py:446
  93.5 3.8 %collective-permute-start.6 = (f32[64,128]{1,0:T(8,128)S(1)}, f32[64,128]{1,0:T(8,128)S(1)}, u32[]{:S(2)}, u32[]{:S(2)}) collective-permute-start(f32[64,128]{1,0:T(8,128)S(1)} %get-tuple-element.49), channel_id=1, source_target_pairs={{0,112},{16,0},{32,16},{48,32},{64,48},{80,64},{96,80},{112,96},{1... | collective-permute-start | bytes 98312 | tf_op jit(solution)/shard_map/ppermute | solution.py:458
  97.4 0.6 maximum_bitcast_fusion
  98.0 1.0 collective-permute-done.6
  99.0 0.6 copy.20
  (5 shorter events, 0.1 us)
Async XLA Ops:
  0.6 7.2 %collective-permute-start = (f32[64,128]{1,0:T(8,128)}, f32[64,128]{1,0:T(8,128)S(1)}, u32[]{:S(2)}, u32[]{:S(2)}) collective-permute-start(f32[64,128]{1,0:T(8,128)} %bitcast.11), channel_id=1, source_target_pairs={{0,16},{16,32},{32,48},{48,64},{64,80},{80,96},{96,112},{112,0},{1... | collective-permute-start | bytes 98312 | tf_op jit(solution)/shard_map/ppermute | solution.py:458
  36.6 1.6 %collective-permute-start.1 = (bf16[8,128,128]{2,1,0:T(8,128)(2,1)S(1)}, bf16[8,128,128]{2,1,0:T(8,128)(2,1)S(1)}, u32[]{:S(2)}, u32[]{:S(2)}) collective-permute-start(bf16[8,128,128]{2,1,0:T(8,128)(2,1)S(1)} %slice.4.block_ref.mine_ref), channel_id=1, source_target_pairs={{0,1},{1,0},{2,3},{3,2},{4,5},{5,4},{6,7},{7,6},{8,9},{9,8},{10,11... | collective-permute-start | bytes 786440 | tf_op jit(solution)/shard_map/ppermute | solution.py:462
  38.3 17.3 %copy-start = (bf16[128,3072]{1,0:T(8,128)(2,1)S(1)}, bf16[128,3072]{1,0:T(8,128)(2,1)}, u32[]{:S(2)}) copy-start(bf16[128,3072]{1,0:T(8,128)(2,1)} %in_ref.3) | copy-start | bytes 2359300
  38.3 17.3 %copy-start.1 = (bf16[3072,128]{1,0:T(8,128)(2,1)S(1)}, bf16[3072,128]{1,0:T(8,128)(2,1)}, u32[]{:S(2)}) copy-start(bf16[3072,128]{1,0:T(8,128)(2,1)} %final_ref.3) | copy-start | bytes 2359300
  38.3 17.3 %copy-start.2 = (f32[2,64,128]{2,1,0:T(8,128)S(1)}, f32[2,64,128]{2,1,0:T(8,128)}, u32[]{:S(2)}) copy-start(f32[2,64,128]{2,1,0:T(8,128)} %fresh_ref.3) | copy-start | bytes 196612
  38.3 17.3 %copy-start.3 = (f32[1,64,128]{2,1,0:T(8,128)S(1)}, f32[1,64,128]{2,1,0:T(8,128)}, u32[]{:S(2)}) copy-start(f32[1,64,128]{2,1,0:T(8,128)} %state_hbm.1) | copy-start | bytes 98308
  38.3 17.2 %copy-start.4 = (f32[3072]{0:T(1024)S(1)}, f32[3072]{0:T(1024)}, u32[]{:S(2)}) copy-start(f32[3072]{0:T(1024)} %param.25) | copy-start | bytes 36868
  53.6 1.9 %collective-permute-start.2 = (bf16[64,3072]{1,0:T(8,128)(2,1)S(1)}, bf16[64,3072]{1,0:T(8,128)(2,1)S(1)}, u32[]{:S(2)}, u32[]{:S(2)}) collective-permute-start(bf16[64,3072]{1,0:T(8,128)(2,1)S(1)} %get-tuple-element.38), channel_id=1, source_target_pairs={{0,1},{1,0},{2,3},{3,2},{4,5},{5,4},{6,7},{7,6},{8,9},{9,8},{10,11... | collective-permute-start | bytes 1179656 | tf_op jit(solution)/shard_map/ppermute | solution.py:462
  56.8 4.3 %collective-permute-start.3 = (f32[64,128]{1,0:T(8,128)S(1)}, f32[64,128]{1,0:T(8,128)S(1)}, u32[]{:S(2)}, u32[]{:S(2)}) collective-permute-start(f32[64,128]{1,0:T(8,128)S(1)} %get-tuple-element.40), channel_id=1, source_target_pairs={{0,112},{16,0},{32,16},{48,32},{64,48},{80,64},{96,80},{112,96},{1... | collective-permute-start | bytes 98312 | tf_op jit(solution)/shard_map/ppermute | solution.py:458
  73.0 1.6 %collective-permute-start.4 = (bf16[8,128,128]{2,1,0:T(8,128)(2,1)S(1)}, bf16[8,128,128]{2,1,0:T(8,128)(2,1)S(1)}, u32[]{:S(2)}, u32[]{:S(2)}) collective-permute-start(bf16[8,128,128]{2,1,0:T(8,128)(2,1)S(1)} %all_to_all.11.block_ref.mine_ref), channel_id=1, source_target_pairs={{0,1},{1,0},{2,3},{3,2},{4,5},{5,4},{6,7},{7,6},{8,9},{9,8},{10,11... | collective-permute-start | bytes 786440 | tf_op jit(solution)/shard_map/ppermute | solution.py:462
  89.8 1.9 %collective-permute-start.5 = (bf16[64,3072]{1,0:T(8,128)(2,1)S(1)}, bf16[64,3072]{1,0:T(8,128)(2,1)S(1)}, u32[]{:S(2)}, u32[]{:S(2)}) collective-permute-start(bf16[64,3072]{1,0:T(8,128)(2,1)S(1)} %get-tuple-element.47), channel_id=1, source_target_pairs={{0,1},{1,0},{2,3},{3,2},{4,5},{5,4},{6,7},{7,6},{8,9},{9,8},{10,11... | collective-permute-start | bytes 1179656 | tf_op jit(solution)/shard_map/ppermute | solution.py:462
  93.5 5.4 %collective-permute-start.6 = (f32[64,128]{1,0:T(8,128)S(1)}, f32[64,128]{1,0:T(8,128)S(1)}, u32[]{:S(2)}, u32[]{:S(2)}) collective-permute-start(f32[64,128]{1,0:T(8,128)S(1)} %get-tuple-element.49), channel_id=1, source_target_pairs={{0,112},{16,0},{32,16},{48,32},{64,48},{80,64},{96,80},{112,96},{1... | collective-permute-start | bytes 98312 | tf_op jit(solution)/shard_map/ppermute | solution.py:458

commit v5 on v4

--- a/solution.py
+++ b/solution.py
@@ -18,10 +18,10 @@
 TOK = 64
 COLS = 192
 PACK = 48
-PAY = 3 * COLS + PACK + 2 * TOK
+PAY = 3 * COLS + PACK + TOK
 HEADS = CHIPS * 3
 GROUPS = HEADS // 4
-SIDE = 1024
+SIDE = CHIPS * TOK
 ONE = 136
 EPS = 1e-06
 SAFE = 60.0
@@ -64,6 +64,11 @@
 
 def rows(shape):
     return lax.broadcasted_iota(jnp.int32, shape, len(shape) - 2)
+
+
+def slot_of(step):
+    count = lax.axis_size("frame")
+    return lax.rem(lax.axis_index("frame") + count - step, count)
 
 
 def fold_kernel(
@@ -114,20 +119,21 @@
     for i in (0, 1, 2, 3):
         copies[i].wait()
 
-    slot = lax.axis_index("frame")
-    before = jnp.maximum(slot - 1, 0)
-    stamp_now = plan_ref[level_ref[slot]].astype(F32)
-    stamp_prev = plan_ref[level_ref[before]].astype(F32)
-    sigma = stamp_now / 1000.0
-    sig_ref[0] = sigma
-    sig_ref[1] = jnp.where(slot > 0, stamp_prev / 1000.0, 0.0) - sigma
-
     freq = freq_ref[...]
     row = rows((8, freq.shape[1]))
-    angle = jnp.where(row == 0, stamp_now, stamp_prev)
+    angle = jnp.zeros((8, freq.shape[1]), F32)
     for step in range(STEPS):
-        angle = jnp.where(row == 2 + 2 * step, ids_ref[slot + step].astype(F32), angle)
-        angle = jnp.where(row == 3 + 2 * step, ids_ref[before + step].astype(F32), angle)
+        slot = slot_of(step)
+        before = jnp.maximum(slot - 1, 0)
+        stamp_now = plan_ref[level_ref[slot]].astype(F32)
+        stamp_prev = plan_ref[level_ref[before]].astype(F32)
+        sigma = stamp_now / 1000.0
+        sig_ref[2 * step] = sigma
+        sig_ref[2 * step + 1] = jnp.where(slot > 0, stamp_prev / 1000.0, 0.0) - sigma
+        angle = jnp.where(row == 2 * step, stamp_now, angle)
+        angle = jnp.where(row == 2 * step + 1, stamp_prev, angle)
+        angle = jnp.where(row == 2 * step + 4, ids_ref[slot + step].astype(F32), angle)
+        angle = jnp.where(row == 2 * step + 5, ids_ref[before + step].astype(F32), angle)
     angle = angle * freq
     wave = jnp.concatenate([jnp.cos(angle), jnp.sin(angle)], axis=1)
 
@@ -138,9 +144,7 @@
     product = product * (math.log2(math.e) / math.sqrt(HEAD))
     qk_ref[...] = jnp.concatenate([product] * 4, axis=1)
 
-    stamps = cond_gain_ref[0:1, :] * wave
-    idents = cond_gain_ref[1:2, :] * wave
-    cond = jnp.concatenate([stamps[0:2] + idents[2:4], stamps[0:2] + idents[4:6]], axis=0)
+    cond = cond_gain_ref[0:1, :] * wave[0:4] + cond_gain_ref[1:2, :] * wave[4:8]
     cond = jnp.concatenate([cond, jnp.zeros_like(cond)], axis=0)
     cond_ref[...] = cond
 
@@ -177,7 +181,6 @@
     for chip in range(CHIPS):
         pay_ref[chip, 0 : 3 * COLS] = mat
         pay_ref[chip, 3 * COLS : 3 * COLS + PACK] = packed
-        pay_ref[chip, 3 * COLS + PACK : PAY - TOK] = x
         pay_ref[chip, PAY - TOK : PAY] = x
 
 
@@ -193,7 +196,7 @@
             pltpu.VMEM((8, width), F32),
             pltpu.VMEM((1, WIDE), F32),
             jax.ShapeDtypeStruct((1,), jnp.int32),
-            jax.ShapeDtypeStruct((2,), F32),
+            jax.ShapeDtypeStruct((2 * STEPS,), F32),
         ),
         in_specs=[ANY] * len(args),
         out_specs=(VMEM,) * 5 + (SMEM,) * 2,
@@ -203,23 +206,6 @@
         compiler_params=pltpu.CompilerParams(vmem_limit_bytes=40 * 2**20),
         name="fold",
     )(*[in_hbm(v) for v in args])
-
-
-def enter_kernel(prev_ref, pay_ref, out_ref):
-    prev = prev_ref[...].astype(BF)
-    for chip in range(CHIPS):
-        out_ref[chip, PAY - TOK : PAY] = prev
-
-
-def enter(prev, pay):
-    return pl.pallas_call(
-        enter_kernel,
-        out_shape=pltpu.VMEM(pay.shape, pay.dtype),
-        in_specs=[VMEM, VMEM],
-        out_specs=VMEM,
-        input_output_aliases={1: 0},
-        name="enter",
-    )(in_vmem(prev), in_vmem(pay))
 
 
 def unpack(pay_ref, ref, j):
@@ -234,17 +220,11 @@
             ref[m * COLS + i * PACK : m * COLS + (i + 1) * PACK, FEAT:WIDE] = part.astype(BF)
 
 
-def prepare(step, first, block_ref, gram_hi_ref, gram_lo_ref, ak_ref, xkt_ref, val_ref, rk_ref):
-    half = CHIPS * TOK
-    own = block_ref[:, 0:TOK, :].reshape(half, FEAT)
-    prev = block_ref[:, TOK : 2 * TOK, :].reshape(half, FEAT)
-    prev = jnp.where(first, own, prev)
-    x = jnp.concatenate([own, prev], axis=0)
-    group = (rows((SIDE, FEAT)) >= half).astype(jnp.int32)
+def prepare(step, group, block_ref, gram_hi_ref, gram_lo_ref, ak_ref, xkt_ref, val_ref, rk_ref):
+    x = block_ref[...].reshape(SIDE, FEAT)
     lane = lanes((SIDE, FEAT))
     mark = jnp.logical_or(lane == 2 * step + group, lane == 4 + 2 * step + group)
     xk = jnp.concatenate([x, mark.astype(F32).astype(BF)], axis=1)
-    group = (lanes((FEAT, SIDE)) >= half).astype(jnp.int32)
     row = rows((FEAT, SIDE))
     mark = jnp.logical_or(row == 2 * step + group, row == 4 + 2 * step + group)
     xkt_ref[0:FEAT, :] = jnp.transpose(x)
@@ -254,6 +234,8 @@
     m_row = jnp.sum(square * xkt.astype(F32), axis=0, keepdims=True) * (1.0 / 3072.0) + EPS
     r_col = jnp.transpose(jnp.broadcast_to(lax.rsqrt(m_row), (8, SIDE)))[:, 0:1]
     val = jnp.where(lanes((SIDE, WIDE)) == ONE, 1.0, xk.astype(F32) * r_col)
+    if group == 1:
+        val = jnp.where(slot_of(step) == 0, 0.0, val)
     val_ref[...] = val.astype(BF)
     for g in range(GROUPS):
         u = dot(ak_ref[g * WIDE : (g + 1) * WIDE, :], xkt_ref[...])
@@ -262,10 +244,13 @@
         rk_ref[g] = jnp.concatenate([rk, rk], axis=0)
 
 
-def prepare_kernel(step, pay_ref, block_ref, gram_hi_ref, gram_lo_ref, ak_ref, xkt_ref, val_ref, rk_ref):
+def prepare_own_kernel(step, pay_ref, block_ref, gram_hi_ref, gram_lo_ref, ak_ref, xkt_ref, val_ref, rk_ref):
     unpack(pay_ref, ak_ref, 1)
-    first = lax.axis_index("frame") == 0
-    prepare(step, first, block_ref, gram_hi_ref, gram_lo_ref, ak_ref, xkt_ref, val_ref, rk_ref)
+    prepare(step, 0, block_ref, gram_hi_ref, gram_lo_ref, ak_ref, xkt_ref, val_ref, rk_ref)
+
+
+def prepare_prev_kernel(step, ak_ref, block_ref, gram_hi_ref, gram_lo_ref, xkt_ref, val_ref, rk_ref):
+    prepare(step, 1, block_ref, gram_hi_ref, gram_lo_ref, ak_ref, xkt_ref, val_ref, rk_ref)
 
 
 def side_shapes():
@@ -276,19 +261,38 @@
     ]
 
 
-def prepared(step, pay, block, gram_hi, gram_lo):
+def prepared(step, group, source, block, gram):
+    shapes = side_shapes()
+    if group == 0:
+        shapes = [pltpu.VMEM((HEADS * HEAD, WIDE), BF)] + shapes
     return pl.pallas_call(
-        functools.partial(prepare_kernel, step),
-        out_shape=[pltpu.VMEM((HEADS * HEAD, WIDE), BF)] + side_shapes(),
+        functools.partial(prepare_own_kernel if group == 0 else prepare_prev_kernel, step),
+        out_shape=shapes,
         in_specs=[VMEM] * 4,
-        out_specs=[VMEM] * 4,
+        out_specs=[VMEM] * len(shapes),
         compiler_params=pltpu.CompilerParams(vmem_limit_bytes=24 * 2**20),
         cost_estimate=cost(HEADS * HEAD * WIDE * SIDE, 2 * CHIPS * PAY * FEAT),
         name="prepare",
-    )(*[in_vmem(v) for v in (pay, block, gram_hi, gram_lo)])
-
-
-def attend_kernel(
+    )(*[in_vmem(v) for v in (source, block, *gram)])
+
+
+def weigh(g, qc_ref, sides, p_ref):
+    for h in range(4):
+        span = slice(2 * TOK * h, 2 * TOK * (h + 1))
+        for i, (xkt_ref, _, rk_ref) in enumerate(sides):
+            s = dot(qc_ref[g, span], xkt_ref[...]) * rk_ref[g, h : h + 1, :]
+            p_ref[span, SIDE * i : SIDE * (i + 1)] = jnp.exp2(s).astype(BF)
+
+
+def collect(g, h, sides, p_ref):
+    span = slice(2 * TOK * h, 2 * TOK * (h + 1))
+    z = dot(p_ref[span, 0:SIDE], sides[0][1][...])
+    for i in range(1, len(sides)):
+        z = z + dot(p_ref[span, SIDE * i : SIDE * (i + 1)], sides[i][1][...])
+    return z
+
+
+def own_kernel(
     step,
     safe_ref,
     pay_ref,
@@ -301,36 +305,20 @@
     xkt_a_ref,
     val_a_ref,
     rk_a_ref,
-    out_w_ref,
-    part_ref,
-    part_other_ref,
+    sum_ref,
+    qc_ref,
     xkt_b_ref,
     val_b_ref,
     rk_b_ref,
     aq_ref,
-    av_ref,
     p_ref,
-    s_ref,
-    qc_ref,
-    z_ref,
-    w_ref,
-    sem,
 ):
-    chip, core = lax.axis_index(("y", "far")), lax.axis_index("core")
-    first = lax.axis_index("frame") == 0
-    copies = []
-    for m in range(CHIPS):
-        begin = pl.multiple_of((2 * m + core) * COLS, COLS)
-        copies.append(pltpu.make_async_copy(out_w_ref.at[pl.ds(begin, COLS)], w_ref.at[pl.ds(m * COLS, COLS)], sem))
-    for copy in copies:
-        copy.start()
+    chip = lax.axis_index(("y", "far"))
     sides = ((xkt_a_ref, val_a_ref, rk_a_ref), (xkt_b_ref, val_b_ref, rk_b_ref))
-    spans = (slice(0, SIDE), slice(SIDE, 2 * SIDE))
-    prepare(step, first, other_ref, gram_hi_ref, gram_lo_ref, ak_ref, *sides[1])
+    prepare(step, 0, other_ref, gram_hi_ref, gram_lo_ref, ak_ref, *sides[1])
 
     unpack(pay_ref, aq_ref, 0)
-    unpack(pay_ref, av_ref, 2)
-    xq = jnp.concatenate([mine_ref[chip, 0:TOK, :], other_ref[chip, 0:TOK, :]], axis=0)
+    xq = jnp.concatenate([mine_ref[chip], other_ref[chip]], axis=0)
     row = rows((FEAT, 2 * TOK))
     mark = jnp.logical_or(row == 2 * step, row == 4 + 2 * step)
     xqt = jnp.concatenate([jnp.transpose(xq), mark.astype(F32).astype(BF)], axis=0)
@@ -347,46 +335,112 @@
         some = jnp.concatenate([jnp.where(head_of == h, some, 0.0) for h in range(4)], axis=0)
         qc_ref[g] = dot(some.astype(BF), ak_ref[span, :]).astype(BF)
 
-    def weigh(g):
-        for h in range(4):
-            span = slice(2 * TOK * h, 2 * TOK * (h + 1))
-            for (xkt_ref, _, rk_ref), keys in zip(sides, spans):
-                s = dot(qc_ref[g, span], xkt_ref[...]) * rk_ref[g, h : h + 1, :]
-                p_ref[span, keys] = jnp.exp2(s).astype(BF)
-
-    def weigh_wide(g):
-        for h in range(4):
-            span = slice(2 * TOK * h, 2 * TOK * (h + 1))
-            for (xkt_ref, _, rk_ref), keys in zip(sides, spans):
-                s_ref[:, keys] = dot(qc_ref[g, span], xkt_ref[...]) * rk_ref[g, h : h + 1, :]
-            s = s_ref[...]
-            p_ref[span, :] = jnp.exp2(s - jnp.max(s, axis=1, keepdims=True)).astype(BF)
-
-    def collect(g):
-        for h in range(4):
-            span = slice(2 * TOK * h, 2 * TOK * (h + 1))
-            z = dot(p_ref[span, spans[0]], val_a_ref[...]) + dot(p_ref[span, spans[1]], val_b_ref[...])
-            z_ref[g, span] = (z * (1.0 / z[:, ONE : ONE + 1])).astype(BF)
-
     @pl.when(safe_ref[0] == 1)
     def _():
         def body(i, carry):
             for k in range(3):
-                weigh(3 * i + k)
-                collect(3 * i + k)
+                g = 3 * i + k
+                weigh(g, qc_ref, sides, p_ref)
+                for h in range(4):
+                    sum_ref[g, 2 * TOK * h : 2 * TOK * (h + 1)] = collect(g, h, sides, p_ref)
+            return carry
+
+        lax.fori_loop(0, GROUPS // 3, body, 0)
+
+
+def attend_own(step, safe, pay, mine, other, gram, qk, ready):
+    group = (GROUPS, 8 * TOK, WIDE)
+    held = [in_vmem(v) for v in (pay, mine, other, *gram, qk, *ready)]
+    return pl.pallas_call(
+        functools.partial(own_kernel, step),
+        out_shape=[pltpu.VMEM(group, F32), pltpu.VMEM(group, BF)] + side_shapes(),
+        in_specs=[SMEM] + [VMEM] * len(held),
+        out_specs=[VMEM] * 5,
+        scratch_shapes=[pltpu.VMEM((HEADS * HEAD, WIDE), BF), pltpu.VMEM((8 * TOK, 2 * SIDE), BF)],
+        compiler_params=pltpu.CompilerParams(vmem_limit_bytes=32 * 2**20),
+        cost_estimate=cost(HEADS * 2 * TOK * WIDE * 4 * SIDE),
+        name="attend_own",
+    )(safe, *held)
+
+
+def prev_kernel(
+    step,
+    safe_ref,
+    pay_ref,
+    other_ref,
+    gram_hi_ref,
+    gram_lo_ref,
+    ak_ref,
+    sum_ref,
+    qc_ref,
+    xkt_a_ref,
+    val_a_ref,
+    rk_a_ref,
+    xkt_b_ref,
+    val_b_ref,
+    rk_b_ref,
+    xkt_c_ref,
+    val_c_ref,
+    rk_c_ref,
+    out_w_ref,
+    part_ref,
+    part_other_ref,
+    xkt_d_ref,
+    val_d_ref,
+    rk_d_ref,
+    av_ref,
+    p_ref,
+    s_ref,
+    z_ref,
+    w_ref,
+    sem,
+):
+    core = lax.axis_index("core")
+    copies = []
+    for m in range(CHIPS):
+        begin = pl.multiple_of((2 * m + core) * COLS, COLS)
+        copies.append(pltpu.make_async_copy(out_w_ref.at[pl.ds(begin, COLS)], w_ref.at[pl.ds(m * COLS, COLS)], sem))
+    for copy in copies:
+        copy.start()
+    own = ((xkt_a_ref, val_a_ref, rk_a_ref), (xkt_b_ref, val_b_ref, rk_b_ref))
+    prev = ((xkt_c_ref, val_c_ref, rk_c_ref), (xkt_d_ref, val_d_ref, rk_d_ref))
+    prepare(step, 1, other_ref, gram_hi_ref, gram_lo_ref, ak_ref, *prev[1])
+    unpack(pay_ref, av_ref, 2)
+
+    def settle(g, h, z):
+        z_ref[g, 2 * TOK * h : 2 * TOK * (h + 1)] = (z * (1.0 / z[:, ONE : ONE + 1])).astype(BF)
+
+    @pl.when(safe_ref[0] == 1)
+    def _():
+        def body(i, carry):
+            for k in range(3):
+                g = 3 * i + k
+                weigh(g, qc_ref, prev, p_ref)
+                for h in range(4):
+                    settle(g, h, collect(g, h, prev, p_ref) + sum_ref[g, 2 * TOK * h : 2 * TOK * (h + 1)])
             return carry
 
         lax.fori_loop(0, GROUPS // 3, body, 0)
 
     @pl.when(safe_ref[0] != 1)
     def _():
+        every = own + prev
+        alone = slot_of(step) == 0
+
         def body(g, carry):
-            weigh_wide(g)
-            collect(g)
+            for h in range(4):
+                span = slice(2 * TOK * h, 2 * TOK * (h + 1))
+                for i, (xkt_ref, _, rk_ref) in enumerate(every):
+                    s = dot(qc_ref[g, span], xkt_ref[...]) * rk_ref[g, h : h + 1, :]
+                    s_ref[:, SIDE * i : SIDE * (i + 1)] = jnp.where(alone, -1e30, s) if i > 1 else s
+                s = s_ref[...]
+                p_ref[span, :] = jnp.exp2(s - jnp.max(s, axis=1, keepdims=True)).astype(BF)
+                settle(g, h, collect(g, h, every, p_ref))
             return carry
 
         lax.fori_loop(0, GROUPS, body, 0)
 
+    head_of = lanes((2 * TOK, WIDE)) // HEAD
     outs = []
     for g in range(GROUPS):
         o = dot_t(z_ref[g], av_ref[g * WIDE : (g + 1) * WIDE, :])
@@ -401,53 +455,56 @@
     part_other_ref[...] = y[TOK:].astype(BF)
 
 
-def attend(step, safe, pay, mine, other, gram_hi, gram_lo, qk, ready, out_weight):
+def attend_prev(step, safe, pay, other, gram, ak, begun, own, ready, out_weight):
     width = out_weight.shape[1]
     half = HEADS * HEAD
-    held = [in_vmem(v) for v in (pay, mine, other, gram_hi, gram_lo, qk, *ready)]
+    held = [in_vmem(v) for v in (pay, other, *gram, ak, *begun, *own, *ready)]
     return pl.pallas_call(
-        functools.partial(attend_kernel, step),
+        functools.partial(prev_kernel, step),
         out_shape=(pltpu.VMEM((TOK, width), F32), pltpu.VMEM((TOK, width), BF)),
         in_specs=[SMEM] + [VMEM] * len(held) + [ANY],
         out_specs=(VMEM, VMEM),
         scratch_shapes=side_shapes()
         + [
             pltpu.VMEM((half, WIDE), BF),
-            pltpu.VMEM((half, WIDE), BF),
-            pltpu.VMEM((8 * TOK, 2 * SIDE), BF),
-            pltpu.VMEM((2 * TOK, 2 * SIDE), F32),
-            pltpu.VMEM((GROUPS, 8 * TOK, WIDE), BF),
+            pltpu.VMEM((8 * TOK, 4 * SIDE), BF),
+            pltpu.VMEM((2 * TOK, 4 * SIDE), F32),
             pltpu.VMEM((GROUPS, 8 * TOK, WIDE), BF),
             pltpu.VMEM((half, width), BF),
             pltpu.SemaphoreType.DMA,
         ],
-        compiler_params=pltpu.CompilerParams(vmem_limit_bytes=48 * 2**20),
+        compiler_params=pltpu.CompilerParams(vmem_limit_bytes=40 * 2**20),
         cost_estimate=cost(HEADS * 2 * TOK * WIDE * 4 * SIDE),
-        name="attend",
+        name="attend_prev",
     )(safe, *held, out_weight)
 
 
 def finish_kernel(
-    step, sig_ref, state_ref, in_ref, cond_ref, part_ref, got_ref, gain_ref, final_ref, fresh_ref, est_ref, sent_ref, prev_ref
+    step, sig_ref, state_ref, in_ref, cond_ref, part_ref, got_ref, gain_ref, final_ref, fresh_ref, est_ref, new_ref, *sent
 ):
     state = state_ref[...]
     y = dot(state.astype(BF), in_ref[...]) + cond_ref[2 * step : 2 * step + 1, :]
     y = y + part_ref[...] + got_ref[...].astype(F32)
     scale = lax.rsqrt(jnp.mean(y * y, axis=1, keepdims=True) + EPS)
     velocity = dot((y * scale * gain_ref[...]).astype(BF), final_ref[...])
-    est_ref[...] = state - sig_ref[0] * velocity
-    renewed = state + sig_ref[1] * velocity
-    sent_ref[...] = jnp.where(lax.axis_index("frame") == 0, fresh_ref[step], renewed)
-    prev_ref[...] = renewed.astype(BF)
+    est_ref[...] = state - sig_ref[2 * step] * velocity
+    new = jnp.where(slot_of(step) == 0, fresh_ref[step], state + sig_ref[2 * step + 1] * velocity)
+    new_ref[...] = new
+    for sent_ref in sent:
+        for chip in range(CHIPS):
+            sent_ref[chip] = new.astype(BF)
 
 
 def finish(step, sig, state, in_weight, cond, part, got, gain, final_weight, fresh):
     out = jax.ShapeDtypeStruct(state.shape, F32)
+    shapes = [out, out]
+    if step + 1 < STEPS:
+        shapes.append(pltpu.VMEM((CHIPS,) + state.shape, BF))
     return pl.pallas_call(
         functools.partial(finish_kernel, step),
-        out_shape=(out, out, jax.ShapeDtypeStruct(state.shape, BF)),
+        out_shape=shapes,
         in_specs=[SMEM] + [VMEM] * 8,
-        out_specs=(VMEM,) * 3,
+        out_specs=[VMEM] * len(shapes),
         compiler_params=pltpu.CompilerParams(vmem_limit_bytes=32 * 2**20),
         name="finish",
     )(sig, *[in_vmem(v) for v in (state, in_weight, cond, part, got, gain, final_weight, fresh)])
@@ -484,7 +541,6 @@
     half = in_weight.shape[1] // 2
     freq = jnp.asarray(np.exp(-math.log(10000.0) * np.arange(half, dtype=np.float32) / half), F32)
     state = latents[0]
-    prev = passed_along(state, 1)
     sent, gram_hi, gram_lo, cond, qk, safe, sig = fold(
         level_index,
         plan,
@@ -497,22 +553,29 @@
         qk_gain,
         latents,
     )
-    pay = spread(enter(prev, sent))
-    mine = pay[:, PAY - 2 * TOK :, :]
+    gram = (gram_hi, gram_lo)
+    pay = spread(sent)
+    mine = pay[:, PAY - TOK :, :]
     results = []
     for step in range(STEPS):
         other = swapped(mine)
-        ready = prepared(step, pay, mine, gram_hi, gram_lo)
-        part, part_other = attend(step, safe, pay, mine, other, gram_hi, gram_lo, qk, ready, out_weight)
+        before = passed_along(mine, 1)
+        ready = prepared(step, 0, pay, mine, gram)
+        begun = attend_own(step, safe, pay, mine, other, gram, qk, ready)
+        before, *begun = lax.optimization_barrier((before, *begun))
+        ak, own = ready[0], (*ready[1:], *begun[2:])
+        before_other = swapped(before)
+        ready = prepared(step, 1, ak, before, gram)
+        part, part_other = attend_prev(step, safe, pay, before_other, gram, ak, begun[:2], own, ready, out_weight)
         got = swapped(part_other)
-        estimate, out, prev = finish(
+        estimate, state, *sent = finish(
             step, sig, state, in_weight, cond, part, got, final_gain[None], final_weight, fresh_noise
         )
         results.append(estimate)
-        state = passed_along(out, -1)
-        if step + 1 < STEPS:
-            both = jnp.concatenate([state.astype(BF), prev], axis=0)
-            mine = spread(jnp.broadcast_to(both[None], (CHIPS,) + both.shape))
+        if sent:
+            mine = spread(sent[0])
+    results[1] = passed_along(results[1], -1)
+    state = passed_along(state, -2)
     return (jnp.stack(results)[:, None], state[None])
 
 

time: 100 us -> 110 us (1.10)
  waiting for transfers between devices: 5.48 us -> 16.5 us
  Pallas kernels: 41.5 us -> 48.5 us
  starting transfers between devices: 9.88 us -> 3.55 us
  blocking collectives: 40.6 us -> 39.3 us
    ppermute x3 -> x4, waiting for transfers between devices: 2.77 us -> 11.7 us  [passed_along(): lax.ppermute(x, 'frame', [(i, (i + by) % peers) for i in range(peers)])]
    pallas_call x7 -> x10, Pallas kernels: 36.6 us -> 43.5 us  [the longest x2 33.1 us: attend_prev(): pl.pallas_call(functools.partial(prev_kernel, step), out_shape=(pltpu.VME...]
    ppermute x3 -> x4, starting transfers between devices: 8.63 us -> 3.02 us  [passed_along(): lax.ppermute(x, 'frame', [(i, (i + by) % peers) for i in range(peers)])]
    ppermute x4 -> x6, waiting for transfers between devices: 2.7 us -> 4.76 us  [swapped(): return lax.ppermute(x, 'core', [(0, 1), (1, 0)])]
    all_to_all x2, blocking collectives: 40.6 us -> 39.3 us  [spread(): return lax.all_to_all(x, ('y', 'far'), 0, 0, tiled=True)]
  transfers between devices with their start and end apart: 7 -> 10, of which waited for: 5 -> 8; matrix products, arithmetic and copies ran while one was open for 1% -> 0% of each run, Pallas kernels for 8% -> 7%
where the time goes in v5:
time: 110 us
  Pallas kernels  48.5 us (44%)
  blocking collectives  39.3 us (36%)
  waiting for transfers between devices  16.5 us (15%)
  starting transfers between devices  3.55 us (3%)
    all_to_all x2, blocking collectives, spread(): return lax.all_to_all(x, ('y', 'far'), 0, 0, tiled=True)  39.3 us
    pallas_call x2, Pallas kernels, attend_prev(): pl.pallas_call(functools.partial(prev_kernel, step), out_shape=(pltpu.VME...  33.1 us
    ppermute x4, waiting for transfers between devices, passed_along(): lax.ppermute(x, 'frame', [(i, (i + by) % peers) for i in range(peers)])  11.7 us
    pallas_call x1, Pallas kernels, fold(): pl.pallas_call(fold_kernel, out_shape=(pltpu.VMEM((CHIPS, PAY, FEAT), BF)...  4.94 us
    pallas_call x2, Pallas kernels, attend_own(): pl.pallas_call(functools.partial(own_kernel, step), out_shape=[pltpu.VMEM...  4.83 us
    ppermute x6, waiting for transfers between devices, swapped(): return lax.ppermute(x, 'core', [(0, 1), (1, 0)])  4.76 us
    pallas_call x4, Pallas kernels, prepared(): pl.pallas_call(functools.partial(prepare_own_kernel if group == 0 else pr...  3.23 us
    ppermute x4, starting transfers between devices, passed_along(): lax.ppermute(x, 'frame', [(i, (i + by) % peers) for i in range(peers)])  3.02 us
  transfers between devices with their start and end apart: 10, of which 8 were waited for; matrix products, arithmetic and copies ran while one was open for 0% of the time, Pallas kernels for 7%

profile of v5, /device:TPU:0, one launch (start us, length us, event | category | flops | bytes accessed | tf_op | source)
XLA Modules:
  0.0 109.9 jit_solution(8338930315981107098)
XLA Ops:
  0.6 4.9 %fold.1 = (bf16[8,688,128]{2,1,0:T(8,128)(2,1)S(1)}, bf16[256,256]{1,0:T(8,128)(2,1)S(1)}, bf16[256,256]{1,0:T(8,128)(2,1)S(1)}, f32[8,3072]{1,0:T(8,128)S(1)}, ...) custom-call(s32[8]{0:T(128)} %level_hbm.1, s32[48]{0:T(128)} %plan_hbm.1, s32[10]{0:T(128)} %ids_hbm.1, ...), custom_call_target="tpu_custom_call" | custom-call | tf_op jit(solution)/shard_map/fold/pallas_call | solution.py:190
  5.6 28.0 %all_to_all.10.pay_ref = bf16[8,688,128]{2,1,0:T(8,128)(2,1)S(1)} all-to-all(bf16[8,688,128]{2,1,0:T(8,128)(2,1)S(1)} %get-tuple-element.57), channel_id=1, replica_groups=mesh['frame'=8,'y'=4,'far'=2,'core'=2] {'y','far'}, dimensions={0} | all-to-all | bytes 2818048 | tf_op jit(solution)/shard_map/all_to_all | solution.py:523
  33.6 0.1 collective-permute-start.1
  33.7 2.0 %collective-permute-start = (bf16[8,64,128]{2,1,0:T(8,128)(2,1)S(1)}, bf16[8,64,128]{2,1,0:T(8,128)(2,1)S(1)}, u32[]{:S(2)}, u32[]{:S(2)}) collective-permute-start(bf16[8,64,128]{2,1,0:T(8,128)(2,1)S(1)} %slice.4.block_ref.mine_ref), channel_id=1, source_target_pairs={{0,16},{16,32},{32,48},{48,64},{64,80},{80,96},{96,112},{112,0},{1... | collective-permute-start | bytes 393224 | tf_op jit(solution)/shard_map/ppermute | solution.py:515
  35.7 0.8 prepare.4
  36.5 0.0 collective-permute-done.1.other_ref
  36.5 2.4 %attend_own.2 = (f32[6,512,256]{2,1,0:T(8,128)S(1)}, bf16[6,512,256]{2,1,0:T(8,128)(2,1)S(1)}, bf16[256,512]{1,0:T(8,128)(2,1)S(1)}, bf16[512,256]{1,0:T(8,128)(2,1)S(1)}, f32[6,8,512]{2,1,0:T(8,128)S(1)}) custom-call(s32[1]{0:T(128)} %get-tuple-element.56.safe_ref, bf16[8,688,128]{2,1,0:T(8,128)(2,1)S(1)} %all_to_all.10.pay_ref, ...), custom_call_target="tpu_custom_call" | custom-call | flops 3221225472 | tf_op jit(solution)/shard_map/attend_own/pallas_call | solution.py:354
  38.9 3.0 %collective-permute-done.block_ref = bf16[8,64,128]{2,1,0:T(8,128)(2,1)S(1)} collective-permute-done((bf16[8,64,128]{2,1,0:T(8,128)(2,1)S(1)}, bf16[8,64,128]{2,1,0:T(8,128)(2,1)S(1)}, u32[]{:S(2)}, u32[]{:S(2)}) %collective-permute-start) | collective-permute-done | bytes 131104 | tf_op jit(solution)/shard_map/ppermute | solution.py:515
  41.9 0.0 collective-permute-start.2
  42.0 0.8 prepare.5
  42.8 0.5 collective-permute-done.2.other_ref
  43.3 0.0 copy-start
  43.3 0.0 copy-start.1
  43.3 0.0 copy-start.2
  43.3 0.0 copy-start.3
  43.3 0.0 copy-start.4
  43.3 16.6 %attend_prev.2 = (f32[64,3072]{1,0:T(8,128)S(1)}, bf16[64,3072]{1,0:T(8,128)(2,1)S(1)}) custom-call(s32[1]{0:T(128)} %get-tuple-element.56.safe_ref, bf16[8,688,128]{2,1,0:T(8,128)(2,1)S(1)} %all_to_all.10.pay_ref, bf16[8,64,128]{2,1,0:T(8,128)(2,1)S(1)} %collective-permute-done.2.other_ref, bf16[256,256]{1,0:T(8,128)(2,1)S(1)} %get-tuple-element.58.gram_hi_ref, ...), custom_call_target="tpu_custom_call" | custom-call | flops 3221225472 | tf_op jit(solution)/shard_map/attend_prev/pallas_call | solution.py:462
  59.9 0.2 collective-permute-start.3
  60.1 1.6 %collective-permute-done.3.got_ref = bf16[64,3072]{1,0:T(8,128)(2,1)S(1)} collective-permute-done((bf16[64,3072]{1,0:T(8,128)(2,1)S(1)}, bf16[64,3072]{1,0:T(8,128)(2,1)S(1)}, u32[]{:S(2)}, u32[]{:S(2)}) %collective-permute-start.3) | collective-permute-done | bytes 393248 | tf_op jit(solution)/shard_map/ppermute | solution.py:519
  61.7 0.0 copy-done
  61.7 0.0 copy-done.1
  61.7 0.0 copy-done.2
  61.7 0.0 copy-done.3
  61.7 0.0 copy-done.4
  61.8 1.2 %finish.2 = (f32[64,128]{1,0:T(8,128)S(1)}, f32[64,128]{1,0:T(8,128)S(1)}, bf16[8,64,128]{2,1,0:T(8,128)(2,1)S(1)}) custom-call(f32[4]{0:T(128)S(1)} %get-tuple-element.54.sig_ref, f32[64,128]{1,0:T(8,128)S(1)} %bitcast.11, bf16[128,3072]{1,0:T(8,128)(2,1)S(1)} %copy-done, f32[8,3072]{1,0:T(8,128)S(1)} %get-tuple-element.55.cond_ref, ...), custom_call_target="tpu_custom_call" | custom-call | tf_op jit(solution)/shard_map/finish/pallas_call | solution.py:503
  63.0 11.3 %all_to_all.11.block_ref.mine_ref = bf16[8,64,128]{2,1,0:T(8,128)(2,1)S(1)} all-to-all(bf16[8,64,128]{2,1,0:T(8,128)(2,1)S(1)} %get-tuple-element.83), channel_id=1, replica_groups=mesh['frame'=8,'y'=4,'far'=2,'core'=2] {'y','far'}, dimensions={0} | all-to-all | bytes 262144 | tf_op jit(solution)/shard_map/all_to_all | solution.py:523
  74.3 0.0 collective-permute-start.5
  74.3 0.0 collective-permute-start.4
  74.3 0.8 prepare.6
  75.1 0.5 collective-permute-done.5.other_ref
  75.6 2.4 %attend_own.3 = (f32[6,512,256]{2,1,0:T(8,128)S(1)}, bf16[6,512,256]{2,1,0:T(8,128)(2,1)S(1)}, bf16[256,512]{1,0:T(8,128)(2,1)S(1)}, bf16[512,256]{1,0:T(8,128)(2,1)S(1)}, f32[6,8,512]{2,1,0:T(8,128)S(1)}) custom-call(s32[1]{0:T(128)} %get-tuple-element.56.safe_ref, bf16[8,688,128]{2,1,0:T(8,128)(2,1)S(1)} %all_to_all.10.pay_ref, ...), custom_call_target="tpu_custom_call" | custom-call | flops 3221225472 | tf_op jit(solution)/shard_map/attend_own/pallas_call | solution.py:354
  78.0 4.3 %collective-permute-done.4.block_ref = bf16[8,64,128]{2,1,0:T(8,128)(2,1)S(1)} collective-permute-done((bf16[8,64,128]{2,1,0:T(8,128)(2,1)S(1)}, bf16[8,64,128]{2,1,0:T(8,128)(2,1)S(1)}, u32[]{:S(2)}, u32[]{:S(2)}) %collective-permute-start.4) | collective-permute-done | bytes 131104 | tf_op jit(solution)/shard_map/ppermute | solution.py:515
  82.3 0.0 collective-permute-start.6
  82.3 0.8 prepare.7
  83.1 0.5 collective-permute-done.6.other_ref
  83.6 16.5 %attend_prev.3 = (f32[64,3072]{1,0:T(8,128)S(1)}, bf16[64,3072]{1,0:T(8,128)(2,1)S(1)}) custom-call(s32[1]{0:T(128)} %get-tuple-element.56.safe_ref, bf16[8,688,128]{2,1,0:T(8,128)(2,1)S(1)} %all_to_all.10.pay_ref, bf16[8,64,128]{2,1,0:T(8,128)(2,1)S(1)} %collective-permute-done.6.other_ref, bf16[256,256]{1,0:T(8,128)(2,1)S(1)} %get-tuple-element.58.gram_hi_ref, ...), custom_call_target="tpu_custom_call" | custom-call | flops 3221225472 | tf_op jit(solution)/shard_map/attend_prev/pallas_call | solution.py:462
  100.1 0.2 collective-permute-start.7
  100.4 1.6 %collective-permute-done.7.got_ref = bf16[64,3072]{1,0:T(8,128)(2,1)S(1)} collective-permute-done((bf16[64,3072]{1,0:T(8,128)(2,1)S(1)}, bf16[64,3072]{1,0:T(8,128)(2,1)S(1)}, u32[]{:S(2)}, u32[]{:S(2)}) %collective-permute-start.7) | collective-permute-done | bytes 393248 | tf_op jit(solution)/shard_map/ppermute | solution.py:519
  101.9 1.2 %finish.3 = (f32[64,128]{1,0:T(8,128)S(1)}, f32[64,128]{1,0:T(8,128)S(1)}) custom-call(f32[4]{0:T(128)S(1)} %get-tuple-element.54.sig_ref, f32[64,128]{1,0:T(8,128)S(1)} %get-tuple-element.82.state_ref, bf16[128,3072]{1,0:T(8,128)(2,1)S(1)} %copy-done, f32[8,3072]{1,0:T(8,128)S(1)} %get-tuple-element.55.cond_ref, ...), custom_call_target="tpu_custom_call" | custom-call | tf_op jit(solution)/shard_map/finish/pallas_call | solution.py:503
  103.1 0.1 collective-permute-start.9
  103.2 1.0 collective-permute-start.8
  104.2 4.4 %collective-permute-done.9 = f32[64,128]{1,0:T(8,128)S(1)} collective-permute-done((f32[64,128]{1,0:T(8,128)S(1)}, f32[64,128]{1,0:T(8,128)S(1)}, u32[]{:S(2)}, u32[]{:S(2)}) %collective-permute-start.9) | collective-permute-done | bytes 32800 | tf_op jit(solution)/shard_map/ppermute | solution.py:515
  108.6 0.0 collective-permute-done.8
  108.6 0.6 maximum_bitcast_fusion
  109.3 0.6 copy.18
  (1 shorter events, 0.0 us)
Async XLA Ops:
  33.6 2.9 %collective-permute-start.1 = (bf16[8,64,128]{2,1,0:T(8,128)(2,1)S(1)}, bf16[8,64,128]{2,1,0:T(8,128)(2,1)S(1)}, u32[]{:S(2)}, u32[]{:S(2)}) collective-permute-start(bf16[8,64,128]{2,1,0:T(8,128)(2,1)S(1)} %slice.4.block_ref.mine_ref), channel_id=1, source_target_pairs={{0,1},{1,0},{2,3},{3,2},{4,5},{5,4},{6,7},{7,6},{8,9},{9,8},{10,11... | collective-permute-start | bytes 393224 | tf_op jit(solution)/shard_map/ppermute | solution.py:519
  33.7 8.3 %collective-permute-start = (bf16[8,64,128]{2,1,0:T(8,128)(2,1)S(1)}, bf16[8,64,128]{2,1,0:T(8,128)(2,1)S(1)}, u32[]{:S(2)}, u32[]{:S(2)}) collective-permute-start(bf16[8,64,128]{2,1,0:T(8,128)(2,1)S(1)} %slice.4.block_ref.mine_ref), channel_id=1, source_target_pairs={{0,16},{16,32},{32,48},{48,64},{64,80},{80,96},{96,112},{112,0},{1... | collective-permute-start | bytes 393224 | tf_op jit(solution)/shard_map/ppermute | solution.py:515
  41.9 1.3 %collective-permute-start.2 = (bf16[8,64,128]{2,1,0:T(8,128)(2,1)S(1)}, bf16[8,64,128]{2,1,0:T(8,128)(2,1)S(1)}, u32[]{:S(2)}, u32[]{:S(2)}) collective-permute-start(bf16[8,64,128]{2,1,0:T(8,128)(2,1)S(1)} %collective-permute-done.block_ref), channel_id=1, source_target_pairs={{0,1},{1,0},{2,3},{3,2},{4,5},{5,4},{6,7},{7,6},{8,9},{9,8},{10,11... | collective-permute-start | bytes 393224 | tf_op jit(solution)/shard_map/ppermute | solution.py:519
  43.3 18.4 %copy-start = (bf16[128,3072]{1,0:T(8,128)(2,1)S(1)}, bf16[128,3072]{1,0:T(8,128)(2,1)}, u32[]{:S(2)}) copy-start(bf16[128,3072]{1,0:T(8,128)(2,1)} %in_ref.3) | copy-start | bytes 2359300
  43.3 18.4 %copy-start.1 = (bf16[3072,128]{1,0:T(8,128)(2,1)S(1)}, bf16[3072,128]{1,0:T(8,128)(2,1)}, u32[]{:S(2)}) copy-start(bf16[3072,128]{1,0:T(8,128)(2,1)} %final_ref.3) | copy-start | bytes 2359300
  43.3 18.4 %copy-start.2 = (f32[2,64,128]{2,1,0:T(8,128)S(1)}, f32[2,64,128]{2,1,0:T(8,128)}, u32[]{:S(2)}) copy-start(f32[2,64,128]{2,1,0:T(8,128)} %fresh_ref.3) | copy-start | bytes 196612
  43.3 18.4 %copy-start.3 = (f32[1,64,128]{2,1,0:T(8,128)S(1)}, f32[1,64,128]{2,1,0:T(8,128)}, u32[]{:S(2)}) copy-start(f32[1,64,128]{2,1,0:T(8,128)} %state_hbm.1) | copy-start | bytes 98308
  43.3 18.4 %copy-start.4 = (f32[3072]{0:T(1024)S(1)}, f32[3072]{0:T(1024)}, u32[]{:S(2)}) copy-start(f32[3072]{0:T(1024)} %param.25) | copy-start | bytes 36868
  59.9 1.8 %collective-permute-start.3 = (bf16[64,3072]{1,0:T(8,128)(2,1)S(1)}, bf16[64,3072]{1,0:T(8,128)(2,1)S(1)}, u32[]{:S(2)}, u32[]{:S(2)}) collective-permute-start(bf16[64,3072]{1,0:T(8,128)(2,1)S(1)} %get-tuple-element.80), channel_id=1, source_target_pairs={{0,1},{1,0},{2,3},{3,2},{4,5},{5,4},{6,7},{7,6},{8,9},{9,8},{10,11... | collective-permute-start | bytes 1179656 | tf_op jit(solution)/shard_map/ppermute | solution.py:519
  74.3 1.3 %collective-permute-start.5 = (bf16[8,64,128]{2,1,0:T(8,128)(2,1)S(1)}, bf16[8,64,128]{2,1,0:T(8,128)(2,1)S(1)}, u32[]{:S(2)}, u32[]{:S(2)}) collective-permute-start(bf16[8,64,128]{2,1,0:T(8,128)(2,1)S(1)} %all_to_all.11.block_ref.mine_ref), channel_id=1, source_target_pairs={{0,1},{1,0},{2,3},{3,2},{4,5},{5,4},{6,7},{7,6},{8,9},{9,8},{10,11... | collective-permute-start | bytes 393224 | tf_op jit(solution)/shard_map/ppermute | solution.py:519
  74.3 8.0 %collective-permute-start.4 = (bf16[8,64,128]{2,1,0:T(8,128)(2,1)S(1)}, bf16[8,64,128]{2,1,0:T(8,128)(2,1)S(1)}, u32[]{:S(2)}, u32[]{:S(2)}) collective-permute-start(bf16[8,64,128]{2,1,0:T(8,128)(2,1)S(1)} %all_to_all.11.block_ref.mine_ref), channel_id=1, source_target_pairs={{0,16},{16,32},{32,48},{48,64},{64,80},{80,96},{96,112},{112,0},{1... | collective-permute-start | bytes 393224 | tf_op jit(solution)/shard_map/ppermute | solution.py:515
  82.3 1.3 %collective-permute-start.6 = (bf16[8,64,128]{2,1,0:T(8,128)(2,1)S(1)}, bf16[8,64,128]{2,1,0:T(8,128)(2,1)S(1)}, u32[]{:S(2)}, u32[]{:S(2)}) collective-permute-start(bf16[8,64,128]{2,1,0:T(8,128)(2,1)S(1)} %collective-permute-done.4.block_ref), channel_id=1, source_target_pairs={{0,1},{1,0},{2,3},{3,2},{4,5},{5,4},{6,7},{7,6},{8,9},{9,8},{10,11... | collective-permute-start | bytes 393224 | tf_op jit(solution)/shard_map/ppermute | solution.py:519
  100.1 1.8 %collective-permute-start.7 = (bf16[64,3072]{1,0:T(8,128)(2,1)S(1)}, bf16[64,3072]{1,0:T(8,128)(2,1)S(1)}, u32[]{:S(2)}, u32[]{:S(2)}) collective-permute-start(bf16[64,3072]{1,0:T(8,128)(2,1)S(1)} %get-tuple-element.103), channel_id=1, source_target_pairs={{0,1},{1,0},{2,3},{3,2},{4,5},{5,4},{6,7},{7,6},{8,9},{9,8},{10,11... | collective-permute-start | bytes 1179656 | tf_op jit(solution)/shard_map/ppermute | solution.py:519
  103.1 5.5 %collective-permute-start.9 = (f32[64,128]{1,0:T(8,128)S(1)}, f32[64,128]{1,0:T(8,128)S(1)}, u32[]{:S(2)}, u32[]{:S(2)}) collective-permute-start(f32[64,128]{1,0:T(8,128)S(1)} %get-tuple-element.105), channel_id=1, source_target_pairs={{0,96},{16,112},{32,0},{48,16},{64,32},{80,48},{96,64},{112,80},{1... | collective-permute-start | bytes 98312 | tf_op jit(solution)/shard_map/ppermute | solution.py:515
  103.2 5.4 %collective-permute-start.8 = (f32[64,128]{1,0:T(8,128)S(1)}, f32[64,128]{1,0:T(8,128)S(1)}, u32[]{:S(2)}, u32[]{:S(2)}) collective-permute-start(f32[64,128]{1,0:T(8,128)S(1)} %get-tuple-element.104), channel_id=1, source_target_pairs={{0,112},{16,0},{32,16},{48,32},{64,48},{80,64},{96,80},{112,96},{1... | collective-permute-start | bytes 98312 | tf_op jit(solution)/shard_map/ppermute | solution.py:515

commit v6 on v5

--- a/solution.py
+++ b/solution.py
@@ -150,16 +150,6 @@
 
     embed = in_ref[...]
     none = jnp.zeros((112, embed.shape[1]), BF)
-    c_hi, c_lo = halves(cond)
-    left = jnp.concatenate([embed, jnp.concatenate([c_hi, c_lo], axis=0), none], axis=0)
-    gram = dot_t(left, left)
-    lane, row = lanes(gram.shape), rows(gram.shape)
-    gram = jnp.where(lane < FEAT + 8, gram + jnp.where(lane >= FEAT, pltpu.roll(gram, WIDE - 8, 1), 0.0), 0.0)
-    gram = jnp.where(row < FEAT + 8, gram + jnp.where(row >= FEAT, pltpu.roll(gram, WIDE - 8, 0), 0.0), 0.0)
-    g_hi, g_lo = halves(gram)
-    gram_hi_ref[...] = g_hi
-    gram_lo_ref[...] = g_lo
-
     gain = gain_ref[...]
     emb = (embed.astype(F32) * gain).astype(BF)
     cg_hi, cg_lo = halves(cond * gain)
@@ -183,6 +173,17 @@
         pay_ref[chip, 3 * COLS : 3 * COLS + PACK] = packed
         pay_ref[chip, PAY - TOK : PAY] = x
 
+    c_hi, c_lo = halves(cond)
+    left = jnp.concatenate([embed, jnp.concatenate([c_hi, c_lo], axis=0)], axis=0)
+    gram = dot_t(left, jnp.concatenate([left, none], axis=0))
+    gram = jnp.concatenate([gram, jnp.zeros((112, WIDE), F32)], axis=0)
+    lane, row = lanes(gram.shape), rows(gram.shape)
+    gram = jnp.where(lane < FEAT + 8, gram + jnp.where(lane >= FEAT, pltpu.roll(gram, WIDE - 8, 1), 0.0), 0.0)
+    gram = jnp.where(row < FEAT + 8, gram + jnp.where(row >= FEAT, pltpu.roll(gram, WIDE - 8, 0), 0.0), 0.0)
+    g_hi, g_lo = halves(gram)
+    gram_hi_ref[...] = g_hi
+    gram_lo_ref[...] = g_lo
+
 
 def fold(level_index, plan, frame_ids, freq, qkv, in_weight, cond_gain, gain, qk_gain, latents):
     width = in_weight.shape[1]
@@ -203,7 +204,7 @@
         scratch_shapes=[pltpu.SMEM(v.shape, v.dtype) for v in args[:3]]
         + [pltpu.VMEM(v.shape, v.dtype) for v in args[3:]]
         + [pltpu.SemaphoreType.DMA((len(args),))],
-        compiler_params=pltpu.CompilerParams(vmem_limit_bytes=40 * 2**20),
+        compiler_params=pltpu.CompilerParams(vmem_limit_bytes=20 * 2**20),
         name="fold",
     )(*[in_hbm(v) for v in args])
 
@@ -220,102 +221,97 @@
             ref[m * COLS + i * PACK : m * COLS + (i + 1) * PACK, FEAT:WIDE] = part.astype(BF)
 
 
-def prepare(step, group, block_ref, gram_hi_ref, gram_lo_ref, ak_ref, xkt_ref, val_ref, rk_ref):
-    x = block_ref[...].reshape(SIDE, FEAT)
-    lane = lanes((SIDE, FEAT))
+def prepare(step, group, blocks, gram_hi_ref, gram_lo_ref, ak_ref, xkt_ref, val_ref, rk_ref):
+    x = jnp.concatenate([ref[...].reshape(SIDE, FEAT) for ref in blocks], axis=0)
+    count = x.shape[0]
+    lane = lanes((count, FEAT))
     mark = jnp.logical_or(lane == 2 * step + group, lane == 4 + 2 * step + group)
     xk = jnp.concatenate([x, mark.astype(F32).astype(BF)], axis=1)
-    row = rows((FEAT, SIDE))
+    row = rows((FEAT, count))
     mark = jnp.logical_or(row == 2 * step + group, row == 4 + 2 * step + group)
     xkt_ref[0:FEAT, :] = jnp.transpose(x)
     xkt_ref[FEAT:WIDE, :] = mark.astype(F32).astype(BF)
     xkt = xkt_ref[...]
     square = dot(gram_hi_ref[...], xkt) + dot(gram_lo_ref[...], xkt)
     m_row = jnp.sum(square * xkt.astype(F32), axis=0, keepdims=True) * (1.0 / 3072.0) + EPS
-    r_col = jnp.transpose(jnp.broadcast_to(lax.rsqrt(m_row), (8, SIDE)))[:, 0:1]
-    val = jnp.where(lanes((SIDE, WIDE)) == ONE, 1.0, xk.astype(F32) * r_col)
+    r_col = jnp.transpose(jnp.broadcast_to(lax.rsqrt(m_row), (8, count)))[:, 0:1]
+    val = jnp.where(lanes((count, WIDE)) == ONE, 1.0, xk.astype(F32) * r_col)
     if group == 1:
         val = jnp.where(slot_of(step) == 0, 0.0, val)
     val_ref[...] = val.astype(BF)
     for g in range(GROUPS):
         u = dot(ak_ref[g * WIDE : (g + 1) * WIDE, :], xkt_ref[...])
-        u = jnp.sum((u * u).reshape(4, HEAD, SIDE), axis=1)
+        u = jnp.sum((u * u).reshape(4, HEAD, count), axis=1)
         rk = lax.rsqrt(u * (1.0 / HEAD) + EPS * m_row)
         rk_ref[g] = jnp.concatenate([rk, rk], axis=0)
 
 
-def prepare_own_kernel(step, pay_ref, block_ref, gram_hi_ref, gram_lo_ref, ak_ref, xkt_ref, val_ref, rk_ref):
-    unpack(pay_ref, ak_ref, 1)
-    prepare(step, 0, block_ref, gram_hi_ref, gram_lo_ref, ak_ref, xkt_ref, val_ref, rk_ref)
-
-
-def prepare_prev_kernel(step, ak_ref, block_ref, gram_hi_ref, gram_lo_ref, xkt_ref, val_ref, rk_ref):
-    prepare(step, 1, block_ref, gram_hi_ref, gram_lo_ref, ak_ref, xkt_ref, val_ref, rk_ref)
-
-
-def side_shapes():
+def prepare_kernel(step, ak_ref, block_ref, gram_hi_ref, gram_lo_ref, xkt_ref, val_ref, rk_ref):
+    prepare(step, 1, (block_ref,), gram_hi_ref, gram_lo_ref, ak_ref, xkt_ref, val_ref, rk_ref)
+
+
+def side_shapes(count):
     return [
-        pltpu.VMEM((WIDE, SIDE), BF),
-        pltpu.VMEM((SIDE, WIDE), BF),
-        pltpu.VMEM((GROUPS, 8, SIDE), F32),
+        pltpu.VMEM((WIDE, count), BF),
+        pltpu.VMEM((count, WIDE), BF),
+        pltpu.VMEM((GROUPS, 8, count), F32),
     ]
 
 
-def prepared(step, group, source, block, gram):
-    shapes = side_shapes()
-    if group == 0:
-        shapes = [pltpu.VMEM((HEADS * HEAD, WIDE), BF)] + shapes
+def prepared(step, ak, block, gram):
     return pl.pallas_call(
-        functools.partial(prepare_own_kernel if group == 0 else prepare_prev_kernel, step),
-        out_shape=shapes,
+        functools.partial(prepare_kernel, step),
+        out_shape=side_shapes(SIDE),
         in_specs=[VMEM] * 4,
-        out_specs=[VMEM] * len(shapes),
-        compiler_params=pltpu.CompilerParams(vmem_limit_bytes=24 * 2**20),
-        cost_estimate=cost(HEADS * HEAD * WIDE * SIDE, 2 * CHIPS * PAY * FEAT),
+        out_specs=[VMEM] * 3,
+        compiler_params=pltpu.CompilerParams(vmem_limit_bytes=10 * 2**20),
+        cost_estimate=cost(HEADS * HEAD * WIDE * SIDE),
         name="prepare",
-    )(*[in_vmem(v) for v in (source, block, *gram)])
+    )(*[in_vmem(v) for v in (ak, block, *gram)])
+
+
+def columns(sides):
+    begin = 0
+    for side in sides:
+        count = side[0].shape[1]
+        yield side, slice(begin, begin + count)
+        begin += count
 
 
 def weigh(g, qc_ref, sides, p_ref):
     for h in range(4):
         span = slice(2 * TOK * h, 2 * TOK * (h + 1))
-        for i, (xkt_ref, _, rk_ref) in enumerate(sides):
+        for (xkt_ref, _, rk_ref), keys in columns(sides):
             s = dot(qc_ref[g, span], xkt_ref[...]) * rk_ref[g, h : h + 1, :]
-            p_ref[span, SIDE * i : SIDE * (i + 1)] = jnp.exp2(s).astype(BF)
+            p_ref[span, keys] = jnp.exp2(s).astype(BF)
 
 
 def collect(g, h, sides, p_ref):
     span = slice(2 * TOK * h, 2 * TOK * (h + 1))
-    z = dot(p_ref[span, 0:SIDE], sides[0][1][...])
-    for i in range(1, len(sides)):
-        z = z + dot(p_ref[span, SIDE * i : SIDE * (i + 1)], sides[i][1][...])
-    return z
-
-
-def own_kernel(
-    step,
-    safe_ref,
-    pay_ref,
-    mine_ref,
-    other_ref,
-    gram_hi_ref,
-    gram_lo_ref,
-    qk_ref,
-    ak_ref,
-    xkt_a_ref,
-    val_a_ref,
-    rk_a_ref,
-    sum_ref,
-    qc_ref,
-    xkt_b_ref,
-    val_b_ref,
-    rk_b_ref,
-    aq_ref,
-    p_ref,
-):
+    parts = [dot(p_ref[span, keys], val_ref[...]) for (_, val_ref, _), keys in columns(sides)]
+    return sum(parts[1:], parts[0])
+
+
+def own_kernel(step, *refs):
+    refs = list(refs)
+    safe_ref, pay_ref, mine_ref, other_ref, gram_hi_ref, gram_lo_ref, qk_ref = refs[:7]
+    del refs[:7]
+    copies = []
+    if step == 0:
+        out_w_ref, w_ref, sem = refs.pop(0), refs.pop(6), refs.pop()
+        core = lax.axis_index("core")
+        for m in range(CHIPS):
+            begin = pl.multiple_of((2 * m + core) * COLS, COLS)
+            copies.append(
+                pltpu.make_async_copy(out_w_ref.at[pl.ds(begin, COLS)], w_ref.at[pl.ds(m * COLS, COLS)], sem)
+            )
+        for copy in copies:
+            copy.start()
+    sum_ref, qc_ref, ak_ref, xkt_ref, val_ref, rk_ref, aq_ref, p_ref = refs
     chip = lax.axis_index(("y", "far"))
-    sides = ((xkt_a_ref, val_a_ref, rk_a_ref), (xkt_b_ref, val_b_ref, rk_b_ref))
-    prepare(step, 0, other_ref, gram_hi_ref, gram_lo_ref, ak_ref, *sides[1])
+    sides = ((xkt_ref, val_ref, rk_ref),)
+    unpack(pay_ref, ak_ref, 1)
+    prepare(step, 0, (mine_ref, other_ref), gram_hi_ref, gram_lo_ref, ak_ref, *sides[0])
 
     unpack(pay_ref, aq_ref, 0)
     xq = jnp.concatenate([mine_ref[chip], other_ref[chip]], axis=0)
@@ -347,17 +343,29 @@
 
         lax.fori_loop(0, GROUPS // 3, body, 0)
 
-
-def attend_own(step, safe, pay, mine, other, gram, qk, ready):
+    for copy in copies:
+        copy.wait()
+
+
+def attend_own(step, safe, pay, mine, other, gram, qk, out_weight):
     group = (GROUPS, 8 * TOK, WIDE)
-    held = [in_vmem(v) for v in (pay, mine, other, *gram, qk, *ready)]
+    half = HEADS * HEAD
+    held = [in_vmem(v) for v in (pay, mine, other, *gram, qk)]
+    specs = [SMEM] + [VMEM] * len(held)
+    shapes = [pltpu.VMEM(group, F32), pltpu.VMEM(group, BF), pltpu.VMEM((half, WIDE), BF)] + side_shapes(2 * SIDE)
+    scratch = [pltpu.VMEM((half, WIDE), BF), pltpu.VMEM((8 * TOK, 2 * SIDE), BF)]
+    if step == 0:
+        held.append(in_hbm(out_weight))
+        specs.append(ANY)
+        shapes.append(pltpu.VMEM((half, out_weight.shape[1]), BF))
+        scratch.append(pltpu.SemaphoreType.DMA)
     return pl.pallas_call(
         functools.partial(own_kernel, step),
-        out_shape=[pltpu.VMEM(group, F32), pltpu.VMEM(group, BF)] + side_shapes(),
-        in_specs=[SMEM] + [VMEM] * len(held),
-        out_specs=[VMEM] * 5,
-        scratch_shapes=[pltpu.VMEM((HEADS * HEAD, WIDE), BF), pltpu.VMEM((8 * TOK, 2 * SIDE), BF)],
-        compiler_params=pltpu.CompilerParams(vmem_limit_bytes=32 * 2**20),
+        out_shape=shapes,
+        in_specs=specs,
+        out_specs=[VMEM] * len(shapes),
+        scratch_shapes=scratch,
+        compiler_params=pltpu.CompilerParams(vmem_limit_bytes=14 * 2**20),
         cost_estimate=cost(HEADS * 2 * TOK * WIDE * 4 * SIDE),
         name="attend_own",
     )(safe, *held)
@@ -370,19 +378,19 @@
     other_ref,
     gram_hi_ref,
     gram_lo_ref,
-    ak_ref,
     sum_ref,
     qc_ref,
+    ak_ref,
     xkt_a_ref,
     val_a_ref,
     rk_a_ref,
-    xkt_b_ref,
-    val_b_ref,
-    rk_b_ref,
     xkt_c_ref,
     val_c_ref,
     rk_c_ref,
-    out_w_ref,
+    w_ref,
+    state_ref,
+    in_ref,
+    cond_ref,
     part_ref,
     part_other_ref,
     xkt_d_ref,
@@ -392,19 +400,10 @@
     p_ref,
     s_ref,
     z_ref,
-    w_ref,
-    sem,
 ):
-    core = lax.axis_index("core")
-    copies = []
-    for m in range(CHIPS):
-        begin = pl.multiple_of((2 * m + core) * COLS, COLS)
-        copies.append(pltpu.make_async_copy(out_w_ref.at[pl.ds(begin, COLS)], w_ref.at[pl.ds(m * COLS, COLS)], sem))
-    for copy in copies:
-        copy.start()
-    own = ((xkt_a_ref, val_a_ref, rk_a_ref), (xkt_b_ref, val_b_ref, rk_b_ref))
+    own = ((xkt_a_ref, val_a_ref, rk_a_ref),)
     prev = ((xkt_c_ref, val_c_ref, rk_c_ref), (xkt_d_ref, val_d_ref, rk_d_ref))
-    prepare(step, 1, other_ref, gram_hi_ref, gram_lo_ref, ak_ref, *prev[1])
+    prepare(step, 1, (other_ref,), gram_hi_ref, gram_lo_ref, ak_ref, *prev[1])
     unpack(pay_ref, av_ref, 2)
 
     def settle(g, h, z):
@@ -430,9 +429,9 @@
         def body(g, carry):
             for h in range(4):
                 span = slice(2 * TOK * h, 2 * TOK * (h + 1))
-                for i, (xkt_ref, _, rk_ref) in enumerate(every):
+                for (xkt_ref, _, rk_ref), keys in columns(every):
                     s = dot(qc_ref[g, span], xkt_ref[...]) * rk_ref[g, h : h + 1, :]
-                    s_ref[:, SIDE * i : SIDE * (i + 1)] = jnp.where(alone, -1e30, s) if i > 1 else s
+                    s_ref[:, keys] = jnp.where(alone, -1e30, s) if keys.start else s
                 s = s_ref[...]
                 p_ref[span, :] = jnp.exp2(s - jnp.max(s, axis=1, keepdims=True)).astype(BF)
                 settle(g, h, collect(g, h, every, p_ref))
@@ -448,43 +447,36 @@
         for h in range(1, 4):
             picked = jnp.where(head_of == h, o[128 * h : 128 * (h + 1)], picked)
         outs.append(picked.astype(BF))
-    for copy in copies:
-        copy.wait()
     y = dot(jnp.concatenate(outs, axis=1), w_ref[...])
-    part_ref[...] = y[0:TOK]
+    hidden = dot(state_ref[...].astype(BF), in_ref[...]) + cond_ref[2 * step : 2 * step + 1, :]
+    part_ref[...] = hidden + y[0:TOK]
     part_other_ref[...] = y[TOK:].astype(BF)
 
 
-def attend_prev(step, safe, pay, other, gram, ak, begun, own, ready, out_weight):
-    width = out_weight.shape[1]
-    half = HEADS * HEAD
-    held = [in_vmem(v) for v in (pay, other, *gram, ak, *begun, *own, *ready)]
+def attend_prev(step, safe, pay, other, gram, begun, ready, weights, state, in_weight, cond):
+    width = weights.shape[1]
+    held = [in_vmem(v) for v in (pay, other, *gram, *begun, *ready, weights, state, in_weight, cond)]
     return pl.pallas_call(
         functools.partial(prev_kernel, step),
         out_shape=(pltpu.VMEM((TOK, width), F32), pltpu.VMEM((TOK, width), BF)),
-        in_specs=[SMEM] + [VMEM] * len(held) + [ANY],
+        in_specs=[SMEM] + [VMEM] * len(held),
         out_specs=(VMEM, VMEM),
-        scratch_shapes=side_shapes()
+        scratch_shapes=side_shapes(SIDE)
         + [
-            pltpu.VMEM((half, WIDE), BF),
+            pltpu.VMEM((HEADS * HEAD, WIDE), BF),
             pltpu.VMEM((8 * TOK, 4 * SIDE), BF),
             pltpu.VMEM((2 * TOK, 4 * SIDE), F32),
             pltpu.VMEM((GROUPS, 8 * TOK, WIDE), BF),
-            pltpu.VMEM((half, width), BF),
-            pltpu.SemaphoreType.DMA,
         ],
-        compiler_params=pltpu.CompilerParams(vmem_limit_bytes=40 * 2**20),
+        compiler_params=pltpu.CompilerParams(vmem_limit_bytes=16 * 2**20),
         cost_estimate=cost(HEADS * 2 * TOK * WIDE * 4 * SIDE),
         name="attend_prev",
-    )(safe, *held, out_weight)
-
-
-def finish_kernel(
-    step, sig_ref, state_ref, in_ref, cond_ref, part_ref, got_ref, gain_ref, final_ref, fresh_ref, est_ref, new_ref, *sent
-):
+    )(safe, *held)
+
+
+def finish_kernel(step, sig_ref, state_ref, part_ref, got_ref, gain_ref, final_ref, fresh_ref, est_ref, new_ref, *sent):
     state = state_ref[...]
-    y = dot(state.astype(BF), in_ref[...]) + cond_ref[2 * step : 2 * step + 1, :]
-    y = y + part_ref[...] + got_ref[...].astype(F32)
+    y = part_ref[...] + got_ref[...].astype(F32)
     scale = lax.rsqrt(jnp.mean(y * y, axis=1, keepdims=True) + EPS)
     velocity = dot((y * scale * gain_ref[...]).astype(BF), final_ref[...])
     est_ref[...] = state - sig_ref[2 * step] * velocity
@@ -495,7 +487,7 @@
             sent_ref[chip] = new.astype(BF)
 
 
-def finish(step, sig, state, in_weight, cond, part, got, gain, final_weight, fresh):
+def finish(step, sig, state, part, got, gain, final_weight, fresh):
     out = jax.ShapeDtypeStruct(state.shape, F32)
     shapes = [out, out]
     if step + 1 < STEPS:
@@ -503,11 +495,34 @@
     return pl.pallas_call(
         functools.partial(finish_kernel, step),
         out_shape=shapes,
-        in_specs=[SMEM] + [VMEM] * 8,
+        in_specs=[SMEM] + [VMEM] * 6,
         out_specs=[VMEM] * len(shapes),
-        compiler_params=pltpu.CompilerParams(vmem_limit_bytes=32 * 2**20),
+        compiler_params=pltpu.CompilerParams(vmem_limit_bytes=12 * 2**20),
         name="finish",
-    )(sig, *[in_vmem(v) for v in (state, in_weight, cond, part, got, gain, final_weight, fresh)])
+    )(sig, *[in_vmem(v) for v in (state, part, got, gain, final_weight, fresh)])
+
+
+def leave_kernel(first_ref, second_ref, queue_ref, est_ref, out_ref, sems):
+    pairs = ((first_ref, est_ref.at[0, 0]), (second_ref, est_ref.at[1, 0]), (queue_ref, out_ref.at[0]))
+    copies = [pltpu.make_async_copy(src, dst, sems.at[i]) for i, (src, dst) in enumerate(pairs)]
+    for copy in copies:
+        copy.start()
+    for copy in copies:
+        copy.wait()
+
+
+def leave(first, second, queue):
+    return pl.pallas_call(
+        leave_kernel,
+        out_shape=(
+            jax.ShapeDtypeStruct((STEPS, 1) + first.shape, F32),
+            jax.ShapeDtypeStruct((1,) + queue.shape, F32),
+        ),
+        in_specs=[VMEM] * 3,
+        out_specs=(ANY, ANY),
+        scratch_shapes=[pltpu.SemaphoreType.DMA((3,))],
+        name="leave",
+    )(in_vmem(first), in_vmem(second), in_vmem(queue))
 
 
 def passed_along(x, by):
@@ -560,23 +575,22 @@
     for step in range(STEPS):
         other = swapped(mine)
         before = passed_along(mine, 1)
-        ready = prepared(step, 0, pay, mine, gram)
-        begun = attend_own(step, safe, pay, mine, other, gram, qk, ready)
+        begun = list(attend_own(step, safe, pay, mine, other, gram, qk, out_weight))
+        if step == 0:
+            weights = begun.pop()
         before, *begun = lax.optimization_barrier((before, *begun))
-        ak, own = ready[0], (*ready[1:], *begun[2:])
         before_other = swapped(before)
-        ready = prepared(step, 1, ak, before, gram)
-        part, part_other = attend_prev(step, safe, pay, before_other, gram, ak, begun[:2], own, ready, out_weight)
+        ready = prepared(step, begun[2], before, gram)
+        part, part_other = attend_prev(
+            step, safe, pay, before_other, gram, begun, ready, weights, state, in_weight, cond
+        )
         got = swapped(part_other)
-        estimate, state, *sent = finish(
-            step, sig, state, in_weight, cond, part, got, final_gain[None], final_weight, fresh_noise
-        )
+        estimate, state, *sent = finish(step, sig, state, part, got, final_gain[None], final_weight, fresh_noise)
         results.append(estimate)
         if sent:
             mine = spread(sent[0])
-    results[1] = passed_along(results[1], -1)
-    state = passed_along(state, -2)
-    return (jnp.stack(results)[:, None], state[None])
+    queue = passed_along(state, -2)
+    return leave(results[0], passed_along(results[1], -1), queue)
 
 
 def solution(mesh):

time: 110 us -> 111 us (level)
  waiting for transfers between devices: 16.5 us -> 12.5 us
  Pallas kernels: 48.5 us -> 52 us
  starting transfers between devices: 3.55 us -> 5.71 us
    pallas_call x6 -> x5, Pallas kernels: 8.06 us -> 11.4 us  [the longest x2 9.18 us: attend_own(): pl.pallas_call(functools.partial(own_kernel, step), out_shape=shapes, in_...]
    ppermute x4, waiting for transfers between devices: 11.7 us -> 8.48 us  [passed_along(): lax.ppermute(x, 'frame', [(i, (i + by) % peers) for i in range(peers)])]
    ppermute x4, starting transfers between devices: 3.02 us -> 4.92 us  [passed_along(): lax.ppermute(x, 'frame', [(i, (i + by) % peers) for i in range(peers)])]
  transfers between devices with their start and end apart: 10 -> 10, of which waited for: 8 -> 7; matrix products, arithmetic and copies ran while one was open for 0% -> 0% of each run, Pallas kernels for 7% -> 10%
where the time goes in v6:
time: 111 us; the launch traced here: 110 us
  Pallas kernels  52 us (47%)
  blocking collectives  39.2 us (35%)
  waiting for transfers between devices  12.5 us (11%)
  starting transfers between devices  5.71 us (5%)
    all_to_all x2, blocking collectives, spread(): return lax.all_to_all(x, ('y', 'far'), 0, 0, tiled=True)  39.2 us
    pallas_call x2, Pallas kernels, attend_prev(): pl.pallas_call(functools.partial(prev_kernel, step), out_shape=(pltpu.VME...  34.1 us
    pallas_call x2, Pallas kernels, attend_own(): pl.pallas_call(functools.partial(own_kernel, step), out_shape=shapes, in_...  9.18 us
    ppermute x4, waiting for transfers between devices, passed_along(): lax.ppermute(x, 'frame', [(i, (i + by) % peers) for i in range(peers)])  8.48 us
    ppermute x4, starting transfers between devices, passed_along(): lax.ppermute(x, 'frame', [(i, (i + by) % peers) for i in range(peers)])  4.92 us
    pallas_call x1, Pallas kernels, fold(): pl.pallas_call(fold_kernel, out_shape=(pltpu.VMEM((CHIPS, PAY, FEAT), BF)...  4.51 us
    ppermute x6, waiting for transfers between devices, swapped(): return lax.ppermute(x, 'core', [(0, 1), (1, 0)])  4.07 us
  transfers between devices with their start and end apart: 10, of which 7 were waited for; matrix products, arithmetic and copies ran while one was open for 0% of the time, Pallas kernels for 10%

profile of v6, /device:TPU:0, one launch (start us, length us, event | category | flops | bytes accessed | tf_op | source)
XLA Modules:
  0.0 110.4 jit_solution(9979546583864075802)
XLA Ops:
  0.6 4.5 %fold.1 = (bf16[8,688,128]{2,1,0:T(8,128)(2,1)S(1)}, bf16[256,256]{1,0:T(8,128)(2,1)S(1)}, bf16[256,256]{1,0:T(8,128)(2,1)S(1)}, f32[8,3072]{1,0:T(8,128)S(1)}, ...) custom-call(s32[8]{0:T(128)} %level_hbm.1, s32[48]{0:T(128)} %plan_hbm.1, s32[10]{0:T(128)} %ids_hbm.1, ...), custom_call_target="tpu_custom_call" | custom-call | tf_op jit(solution)/shard_map/fold/pallas_call | solution.py:191
  5.1 28.0 %all_to_all.10.refs_1_.pay_ref = bf16[8,688,128]{2,1,0:T(8,128)(2,1)S(1)} all-to-all(bf16[8,688,128]{2,1,0:T(8,128)(2,1)S(1)} %get-tuple-element.53), channel_id=1, replica_groups=mesh['frame'=8,'y'=4,'far'=2,'core'=2] {'y','far'}, dimensions={0} | all-to-all | bytes 2818048 | tf_op jit(solution)/shard_map/all_to_all | solution.py:538
  33.2 0.1 collective-permute-start.1
  33.3 2.0 %collective-permute-start = (bf16[8,64,128]{2,1,0:T(8,128)(2,1)S(1)}, bf16[8,64,128]{2,1,0:T(8,128)(2,1)S(1)}, u32[]{:S(2)}, u32[]{:S(2)}) collective-permute-start(bf16[8,64,128]{2,1,0:T(8,128)(2,1)S(1)} %slice.4.refs_2_), channel_id=1, source_target_pairs={{0,16},{16,32},{32,48},{48,64},{64,80},{80,96},{96,112},{112,0},{1... | collective-permute-start | bytes 393224 | tf_op jit(solution)/shard_map/ppermute | solution.py:530
  35.2 0.0 collective-permute-done.1.refs_3_
  35.3 0.0 copy-start
  35.3 0.0 copy-start.2
  35.3 6.3 %attend_own.2 = (f32[6,512,256]{2,1,0:T(8,128)S(1)}, bf16[6,512,256]{2,1,0:T(8,128)(2,1)S(1)}, bf16[1536,256]{1,0:T(8,128)(2,1)S(1)}, bf16[256,1024]{1,0:T(8,128...) custom-call(s32[1]{0:T(128)} %get-tuple-element.52.refs_0_.safe_ref, ...), custom_call_target="tpu_custom_call" | custom-call | flops 3221225472 | tf_op jit(solution)/shard_map/attend_own/pallas_call | solution.py:362
  41.5 0.0 collective-permute-done.block_ref
  41.5 0.2 collective-permute-start.2
  41.8 0.8 prepare.2
  42.6 0.4 collective-permute-done.2.other_ref
  43.0 0.0 copy-done
  43.0 0.0 copy-done.2
  43.0 0.0 copy-start.1
  43.0 0.0 copy-start.3
  43.0 0.0 copy-start.4
  43.0 17.1 %attend_prev.2 = (f32[64,3072]{1,0:T(8,128)S(1)}, bf16[64,3072]{1,0:T(8,128)(2,1)S(1)}) custom-call(s32[1]{0:T(128)} %get-tuple-element.52.refs_0_.safe_ref, bf16[8,688,128]{2,1,0:T(8,128)(2,1)S(1)} %all_to_all.10.refs_1_.pay_ref, bf16[8,64,128]{2,1,0:T(8,128)(2,1)S(1)} %collective-permute-done.2.other_ref, ...), custom_call_target="tpu_custom_call" | custom-call | flops 3221225472 | tf_op jit(solution)/shard_map/attend_prev/pallas_call | solution.py:459
  60.1 0.2 collective-permute-start.3
  60.3 1.6 %collective-permute-done.3.got_ref = bf16[64,3072]{1,0:T(8,128)(2,1)S(1)} collective-permute-done((bf16[64,3072]{1,0:T(8,128)(2,1)S(1)}, bf16[64,3072]{1,0:T(8,128)(2,1)S(1)}, u32[]{:S(2)}, u32[]{:S(2)}) %collective-permute-start.3) | collective-permute-done | bytes 393248 | tf_op jit(solution)/shard_map/ppermute | solution.py:534
  61.9 0.0 copy-done.1
  61.9 0.0 copy-done.3
  61.9 0.0 copy-done.4
  61.9 1.0 finish.2
  62.9 11.2 %all_to_all.11.refs_2_ = bf16[8,64,128]{2,1,0:T(8,128)(2,1)S(1)} all-to-all(bf16[8,64,128]{2,1,0:T(8,128)(2,1)S(1)} %get-tuple-element.79), channel_id=1, replica_groups=mesh['frame'=8,'y'=4,'far'=2,'core'=2] {'y','far'}, dimensions={0} | all-to-all | bytes 262144 | tf_op jit(solution)/shard_map/all_to_all | solution.py:538
  74.1 0.0 collective-permute-start.5
  74.1 1.4 %collective-permute-start.4 = (bf16[8,64,128]{2,1,0:T(8,128)(2,1)S(1)}, bf16[8,64,128]{2,1,0:T(8,128)(2,1)S(1)}, u32[]{:S(2)}, u32[]{:S(2)}) collective-permute-start(bf16[8,64,128]{2,1,0:T(8,128)(2,1)S(1)} %all_to_all.11.refs_2_), channel_id=1, source_target_pairs={{0,16},{16,32},{32,48},{48,64},{64,80},{80,96},{96,112},{112,0},{1... | collective-permute-start | bytes 393224 | tf_op jit(solution)/shard_map/ppermute | solution.py:530
  75.5 0.0 collective-permute-done.5.refs_3_
  75.5 2.9 %attend_own.3 = (f32[6,512,256]{2,1,0:T(8,128)S(1)}, bf16[6,512,256]{2,1,0:T(8,128)(2,1)S(1)}, bf16[1536,256]{1,0:T(8,128)(2,1)S(1)}, bf16[256,1024]{1,0:T(8,128...) custom-call(s32[1]{0:T(128)} %get-tuple-element.52.refs_0_.safe_ref, ...), custom_call_target="tpu_custom_call" | custom-call | flops 3221225472 | tf_op jit(solution)/shard_map/attend_own/pallas_call | solution.py:362
  78.4 3.7 %collective-permute-done.4.block_ref = bf16[8,64,128]{2,1,0:T(8,128)(2,1)S(1)} collective-permute-done((bf16[8,64,128]{2,1,0:T(8,128)(2,1)S(1)}, bf16[8,64,128]{2,1,0:T(8,128)(2,1)S(1)}, u32[]{:S(2)}, u32[]{:S(2)}) %collective-permute-start.4) | collective-permute-done | bytes 131104 | tf_op jit(solution)/shard_map/ppermute | solution.py:530
  82.1 0.0 collective-permute-start.6
  82.1 0.8 prepare.3
  82.9 0.5 collective-permute-done.6.other_ref
  83.4 17.0 %attend_prev.3 = (f32[64,3072]{1,0:T(8,128)S(1)}, bf16[64,3072]{1,0:T(8,128)(2,1)S(1)}) custom-call(s32[1]{0:T(128)} %get-tuple-element.52.refs_0_.safe_ref, bf16[8,688,128]{2,1,0:T(8,128)(2,1)S(1)} %all_to_all.10.refs_1_.pay_ref, bf16[8,64,128]{2,1,0:T(8,128)(2,1)S(1)} %collective-permute-done.6.other_ref, ...), custom_call_target="tpu_custom_call" | custom-call | flops 3221225472 | tf_op jit(solution)/shard_map/attend_prev/pallas_call | solution.py:459
  100.5 0.2 collective-permute-start.7
  100.7 1.6 %collective-permute-done.7.got_ref = bf16[64,3072]{1,0:T(8,128)(2,1)S(1)} collective-permute-done((bf16[64,3072]{1,0:T(8,128)(2,1)S(1)}, bf16[64,3072]{1,0:T(8,128)(2,1)S(1)}, u32[]{:S(2)}, u32[]{:S(2)}) %collective-permute-start.7) | collective-permute-done | bytes 393248 | tf_op jit(solution)/shard_map/ppermute | solution.py:534
  102.3 1.0 finish.3
  103.3 0.9 collective-permute-start.8
  104.2 0.6 collective-permute-start.9
  104.8 2.8 %collective-permute-done.8.second_ref = f32[64,128]{1,0:T(8,128)S(1)} collective-permute-done((f32[64,128]{1,0:T(8,128)S(1)}, f32[64,128]{1,0:T(8,128)S(1)}, u32[]{:S(2)}, u32[]{:S(2)}) %collective-permute-start.8) | collective-permute-done | bytes 32800 | tf_op jit(solution)/shard_map/ppermute | solution.py:530
  107.6 2.0 %collective-permute-done.9.queue_ref = f32[64,128]{1,0:T(8,128)S(1)} collective-permute-done((f32[64,128]{1,0:T(8,128)S(1)}, f32[64,128]{1,0:T(8,128)S(1)}, u32[]{:S(2)}, u32[]{:S(2)}) %collective-permute-start.9) | collective-permute-done | bytes 32800 | tf_op jit(solution)/shard_map/ppermute | solution.py:530
  109.6 0.7 leave.1
  (1 shorter events, 0.0 us)
Async XLA Ops:
  33.2 2.1 %collective-permute-start.1 = (bf16[8,64,128]{2,1,0:T(8,128)(2,1)S(1)}, bf16[8,64,128]{2,1,0:T(8,128)(2,1)S(1)}, u32[]{:S(2)}, u32[]{:S(2)}) collective-permute-start(bf16[8,64,128]{2,1,0:T(8,128)(2,1)S(1)} %slice.4.refs_2_), channel_id=1, source_target_pairs={{0,1},{1,0},{2,3},{3,2},{4,5},{5,4},{6,7},{7,6},{8,9},{9,8},{10,11... | collective-permute-start | bytes 393224 | tf_op jit(solution)/shard_map/ppermute | solution.py:534
  33.3 8.3 %collective-permute-start = (bf16[8,64,128]{2,1,0:T(8,128)(2,1)S(1)}, bf16[8,64,128]{2,1,0:T(8,128)(2,1)S(1)}, u32[]{:S(2)}, u32[]{:S(2)}) collective-permute-start(bf16[8,64,128]{2,1,0:T(8,128)(2,1)S(1)} %slice.4.refs_2_), channel_id=1, source_target_pairs={{0,16},{16,32},{32,48},{48,64},{64,80},{80,96},{96,112},{112,0},{1... | collective-permute-start | bytes 393224 | tf_op jit(solution)/shard_map/ppermute | solution.py:530
  35.3 7.7 %copy-start = (bf16[128,3072]{1,0:T(8,128)(2,1)S(1)}, bf16[128,3072]{1,0:T(8,128)(2,1)}, u32[]{:S(2)}) copy-start(bf16[128,3072]{1,0:T(8,128)(2,1)} %in_ref.3) | copy-start | bytes 2359300
  35.3 7.7 %copy-start.2 = (f32[1,64,128]{2,1,0:T(8,128)S(1)}, f32[1,64,128]{2,1,0:T(8,128)}, u32[]{:S(2)}) copy-start(f32[1,64,128]{2,1,0:T(8,128)} %state_hbm.1) | copy-start | bytes 98308
  41.5 1.4 %collective-permute-start.2 = (bf16[8,64,128]{2,1,0:T(8,128)(2,1)S(1)}, bf16[8,64,128]{2,1,0:T(8,128)(2,1)S(1)}, u32[]{:S(2)}, u32[]{:S(2)}) collective-permute-start(bf16[8,64,128]{2,1,0:T(8,128)(2,1)S(1)} %collective-permute-done.block_ref), channel_id=1, source_target_pairs={{0,1},{1,0},{2,3},{3,2},{4,5},{5,4},{6,7},{7,6},{8,9},{9,8},{10,11... | collective-permute-start | bytes 393224 | tf_op jit(solution)/shard_map/ppermute | solution.py:534
  43.0 18.9 %copy-start.1 = (bf16[3072,128]{1,0:T(8,128)(2,1)S(1)}, bf16[3072,128]{1,0:T(8,128)(2,1)}, u32[]{:S(2)}) copy-start(bf16[3072,128]{1,0:T(8,128)(2,1)} %final_ref.3) | copy-start | bytes 2359300
  43.0 18.9 %copy-start.3 = (f32[2,64,128]{2,1,0:T(8,128)S(1)}, f32[2,64,128]{2,1,0:T(8,128)}, u32[]{:S(2)}) copy-start(f32[2,64,128]{2,1,0:T(8,128)} %fresh_ref.3) | copy-start | bytes 196612
  43.0 18.9 %copy-start.4 = (f32[3072]{0:T(1024)S(1)}, f32[3072]{0:T(1024)}, u32[]{:S(2)}) copy-start(f32[3072]{0:T(1024)} %param.25) | copy-start | bytes 36868
  60.1 1.8 %collective-permute-start.3 = (bf16[64,3072]{1,0:T(8,128)(2,1)S(1)}, bf16[64,3072]{1,0:T(8,128)(2,1)S(1)}, u32[]{:S(2)}, u32[]{:S(2)}) collective-permute-start(bf16[64,3072]{1,0:T(8,128)(2,1)S(1)} %get-tuple-element.76), channel_id=1, source_target_pairs={{0,1},{1,0},{2,3},{3,2},{4,5},{5,4},{6,7},{7,6},{8,9},{9,8},{10,11... | collective-permute-start | bytes 1179656 | tf_op jit(solution)/shard_map/ppermute | solution.py:534
  74.1 1.4 %collective-permute-start.5 = (bf16[8,64,128]{2,1,0:T(8,128)(2,1)S(1)}, bf16[8,64,128]{2,1,0:T(8,128)(2,1)S(1)}, u32[]{:S(2)}, u32[]{:S(2)}) collective-permute-start(bf16[8,64,128]{2,1,0:T(8,128)(2,1)S(1)} %all_to_all.11.refs_2_), channel_id=1, source_target_pairs={{0,1},{1,0},{2,3},{3,2},{4,5},{5,4},{6,7},{7,6},{8,9},{9,8},{10,11... | collective-permute-start | bytes 393224 | tf_op jit(solution)/shard_map/ppermute | solution.py:534
  74.1 8.0 %collective-permute-start.4 = (bf16[8,64,128]{2,1,0:T(8,128)(2,1)S(1)}, bf16[8,64,128]{2,1,0:T(8,128)(2,1)S(1)}, u32[]{:S(2)}, u32[]{:S(2)}) collective-permute-start(bf16[8,64,128]{2,1,0:T(8,128)(2,1)S(1)} %all_to_all.11.refs_2_), channel_id=1, source_target_pairs={{0,16},{16,32},{32,48},{48,64},{64,80},{80,96},{96,112},{112,0},{1... | collective-permute-start | bytes 393224 | tf_op jit(solution)/shard_map/ppermute | solution.py:530
  82.1 1.3 %collective-permute-start.6 = (bf16[8,64,128]{2,1,0:T(8,128)(2,1)S(1)}, bf16[8,64,128]{2,1,0:T(8,128)(2,1)S(1)}, u32[]{:S(2)}, u32[]{:S(2)}) collective-permute-start(bf16[8,64,128]{2,1,0:T(8,128)(2,1)S(1)} %collective-permute-done.4.block_ref), channel_id=1, source_target_pairs={{0,1},{1,0},{2,3},{3,2},{4,5},{5,4},{6,7},{7,6},{8,9},{9,8},{10,11... | collective-permute-start | bytes 393224 | tf_op jit(solution)/shard_map/ppermute | solution.py:534
  100.5 1.8 %collective-permute-start.7 = (bf16[64,3072]{1,0:T(8,128)(2,1)S(1)}, bf16[64,3072]{1,0:T(8,128)(2,1)S(1)}, u32[]{:S(2)}, u32[]{:S(2)}) collective-permute-start(bf16[64,3072]{1,0:T(8,128)(2,1)S(1)} %get-tuple-element.97), channel_id=1, source_target_pairs={{0,1},{1,0},{2,3},{3,2},{4,5},{5,4},{6,7},{7,6},{8,9},{9,8},{10,11... | collective-permute-start | bytes 1179656 | tf_op jit(solution)/shard_map/ppermute | solution.py:534
  103.3 4.3 %collective-permute-start.8 = (f32[64,128]{1,0:T(8,128)S(1)}, f32[64,128]{1,0:T(8,128)S(1)}, u32[]{:S(2)}, u32[]{:S(2)}) collective-permute-start(f32[64,128]{1,0:T(8,128)S(1)} %get-tuple-element.98), channel_id=1, source_target_pairs={{0,112},{16,0},{32,16},{48,32},{64,48},{80,64},{96,80},{112,96},{1... | collective-permute-start | bytes 98312 | tf_op jit(solution)/shard_map/ppermute | solution.py:530
  104.2 5.4 %collective-permute-start.9 = (f32[64,128]{1,0:T(8,128)S(1)}, f32[64,128]{1,0:T(8,128)S(1)}, u32[]{:S(2)}, u32[]{:S(2)}) collective-permute-start(f32[64,128]{1,0:T(8,128)S(1)} %get-tuple-element.99), channel_id=1, source_target_pairs={{0,96},{16,112},{32,0},{48,16},{64,32},{80,48},{96,64},{112,80},{1... | collective-permute-start | bytes 98312 | tf_op jit(solution)/shard_map/ppermute | solution.py:530

commit v7 on v6

--- a/solution.py
+++ b/solution.py
@@ -246,6 +246,62 @@
         rk_ref[g] = jnp.concatenate([rk, rk], axis=0)
 
 
+def queries(step, tokens, pay_ref, gram_hi_ref, gram_lo_ref, qk_ref, aq_ref, ak_ref, qc_ref):
+    unpack(pay_ref, aq_ref, 0)
+    xq = jnp.concatenate(tokens, axis=0)
+    row = rows((FEAT, 2 * TOK))
+    mark = jnp.logical_or(row == 2 * step, row == 4 + 2 * step)
+    xqt = jnp.concatenate([jnp.transpose(xq), mark.astype(F32).astype(BF)], axis=0)
+    square = dot(gram_hi_ref[...], xqt) + dot(gram_lo_ref[...], xqt)
+    m_q = jnp.sum(square * xqt.astype(F32), axis=0, keepdims=True) * (1.0 / 3072.0) + EPS
+    head_of = lanes((2 * TOK, WIDE)) // HEAD
+
+    q = dot(aq_ref[...], xqt).reshape(HEADS, HEAD, 2 * TOK)
+    q = q * lax.rsqrt(jnp.sum(q * q, axis=1, keepdims=True) * (1.0 / HEAD) + EPS * m_q[None])
+    q = q.reshape(HEADS * HEAD, 2 * TOK)
+    for g in range(GROUPS):
+        span = slice(g * WIDE, (g + 1) * WIDE)
+        some = jnp.transpose(q[span]) * qk_ref[...]
+        some = jnp.concatenate([jnp.where(head_of == h, some, 0.0) for h in range(4)], axis=0)
+        qc_ref[g] = dot(some.astype(BF), ak_ref[span, :]).astype(BF)
+
+
+def prepare_own_kernel(step, *refs):
+    refs = list(refs)
+    pay_ref, block_ref, gram_hi_ref, gram_lo_ref = refs[:4]
+    del refs[:4]
+    if step == 0:
+        qk_ref, partner_ref, qc_ref, aq_ref = refs.pop(0), refs.pop(0), refs.pop(4), refs.pop()
+    ak_ref, xkt_ref, val_ref, rk_ref = refs
+    unpack(pay_ref, ak_ref, 1)
+    prepare(step, 0, (block_ref,), gram_hi_ref, gram_lo_ref, ak_ref, xkt_ref, val_ref, rk_ref)
+    if step == 0:
+        chip = lax.axis_index(("y", "far"))
+        tokens = (block_ref[chip], partner_ref[...].astype(BF))
+        queries(step, tokens, pay_ref, gram_hi_ref, gram_lo_ref, qk_ref, aq_ref, ak_ref, qc_ref)
+
+
+def prepared_own(step, pay, block, gram, qk, partner):
+    half = HEADS * HEAD
+    held = [in_vmem(v) for v in (pay, block, *gram)]
+    shapes = [pltpu.VMEM((half, WIDE), BF)] + side_shapes(SIDE)
+    scratch = []
+    if step == 0:
+        held += [in_vmem(qk), in_vmem(partner)]
+        shapes.append(pltpu.VMEM((GROUPS, 8 * TOK, WIDE), BF))
+        scratch.append(pltpu.VMEM((half, WIDE), BF))
+    return pl.pallas_call(
+        functools.partial(prepare_own_kernel, step),
+        out_shape=shapes,
+        in_specs=[VMEM] * len(held),
+        out_specs=[VMEM] * len(shapes),
+        scratch_shapes=scratch,
+        compiler_params=pltpu.CompilerParams(vmem_limit_bytes=12 * 2**20),
+        cost_estimate=cost(HEADS * HEAD * WIDE * SIDE, 2 * CHIPS * PAY * FEAT),
+        name="prepare_own",
+    )(*held)
+
+
 def prepare_kernel(step, ak_ref, block_ref, gram_hi_ref, gram_lo_ref, xkt_ref, val_ref, rk_ref):
     prepare(step, 1, (block_ref,), gram_hi_ref, gram_lo_ref, ak_ref, xkt_ref, val_ref, rk_ref)
 
@@ -294,11 +350,12 @@
 
 def own_kernel(step, *refs):
     refs = list(refs)
-    safe_ref, pay_ref, mine_ref, other_ref, gram_hi_ref, gram_lo_ref, qk_ref = refs[:7]
-    del refs[:7]
+    safe_ref, other_ref, gram_hi_ref, gram_lo_ref, ak_ref = refs[:5]
+    sides = (refs[5:8],)
+    del refs[:8]
     copies = []
     if step == 0:
-        out_w_ref, w_ref, sem = refs.pop(0), refs.pop(6), refs.pop()
+        qc_ref, out_w_ref, w_ref, sem = refs.pop(0), refs.pop(0), refs.pop(4), refs.pop()
         core = lax.axis_index("core")
         for m in range(CHIPS):
             begin = pl.multiple_of((2 * m + core) * COLS, COLS)
@@ -307,29 +364,15 @@
             )
         for copy in copies:
             copy.start()
-    sum_ref, qc_ref, ak_ref, xkt_ref, val_ref, rk_ref, aq_ref, p_ref = refs
-    chip = lax.axis_index(("y", "far"))
-    sides = ((xkt_ref, val_ref, rk_ref),)
-    unpack(pay_ref, ak_ref, 1)
-    prepare(step, 0, (mine_ref, other_ref), gram_hi_ref, gram_lo_ref, ak_ref, *sides[0])
-
-    unpack(pay_ref, aq_ref, 0)
-    xq = jnp.concatenate([mine_ref[chip], other_ref[chip]], axis=0)
-    row = rows((FEAT, 2 * TOK))
-    mark = jnp.logical_or(row == 2 * step, row == 4 + 2 * step)
-    xqt = jnp.concatenate([jnp.transpose(xq), mark.astype(F32).astype(BF)], axis=0)
-    square = dot(gram_hi_ref[...], xqt) + dot(gram_lo_ref[...], xqt)
-    m_q = jnp.sum(square * xqt.astype(F32), axis=0, keepdims=True) * (1.0 / 3072.0) + EPS
-    head_of = lanes((2 * TOK, WIDE)) // HEAD
-
-    q = dot(aq_ref[...], xqt).reshape(HEADS, HEAD, 2 * TOK)
-    q = q * lax.rsqrt(jnp.sum(q * q, axis=1, keepdims=True) * (1.0 / HEAD) + EPS * m_q[None])
-    q = q.reshape(HEADS * HEAD, 2 * TOK)
-    for g in range(GROUPS):
-        span = slice(g * WIDE, (g + 1) * WIDE)
-        some = jnp.transpose(q[span]) * qk_ref[...]
-        some = jnp.concatenate([jnp.where(head_of == h, some, 0.0) for h in range(4)], axis=0)
-        qc_ref[g] = dot(some.astype(BF), ak_ref[span, :]).astype(BF)
+    else:
+        pay_ref, mine_ref, qk_ref, qc_ref, aq_ref = refs.pop(0), refs.pop(0), refs.pop(0), refs.pop(4), refs.pop()
+    sum_ref, p_ref = refs.pop(0), refs.pop()
+    sides += (tuple(refs),)
+    prepare(step, 0, (other_ref,), gram_hi_ref, gram_lo_ref, ak_ref, *sides[1])
+    if step > 0:
+        chip = lax.axis_index(("y", "far"))
+        tokens = (mine_ref[chip], other_ref[chip])
+        queries(step, tokens, pay_ref, gram_hi_ref, gram_lo_ref, qk_ref, aq_ref, ak_ref, qc_ref)
 
     @pl.when(safe_ref[0] == 1)
     def _():
@@ -347,22 +390,24 @@
         copy.wait()
 
 
-def attend_own(step, safe, pay, mine, other, gram, qk, out_weight):
+def attend_own(step, safe, pay, mine, other, gram, qk, ready, out_weight):
     group = (GROUPS, 8 * TOK, WIDE)
     half = HEADS * HEAD
-    held = [in_vmem(v) for v in (pay, mine, other, *gram, qk)]
-    specs = [SMEM] + [VMEM] * len(held)
-    shapes = [pltpu.VMEM(group, F32), pltpu.VMEM(group, BF), pltpu.VMEM((half, WIDE), BF)] + side_shapes(2 * SIDE)
-    scratch = [pltpu.VMEM((half, WIDE), BF), pltpu.VMEM((8 * TOK, 2 * SIDE), BF)]
+    held = [in_vmem(v) for v in (other, *gram, *ready)]
+    shapes = [pltpu.VMEM(group, F32)] + side_shapes(SIDE)
+    scratch = [pltpu.VMEM((8 * TOK, 2 * SIDE), BF)]
     if step == 0:
         held.append(in_hbm(out_weight))
-        specs.append(ANY)
         shapes.append(pltpu.VMEM((half, out_weight.shape[1]), BF))
         scratch.append(pltpu.SemaphoreType.DMA)
+    else:
+        held += [in_vmem(v) for v in (pay, mine, qk)]
+        shapes.append(pltpu.VMEM(group, BF))
+        scratch.append(pltpu.VMEM((half, WIDE), BF))
     return pl.pallas_call(
         functools.partial(own_kernel, step),
         out_shape=shapes,
-        in_specs=specs,
+        in_specs=[SMEM] + [VMEM] * (len(held) - 1) + [ANY if step == 0 else VMEM],
         out_specs=[VMEM] * len(shapes),
         scratch_shapes=scratch,
         compiler_params=pltpu.CompilerParams(vmem_limit_bytes=14 * 2**20),
@@ -384,6 +429,9 @@
     xkt_a_ref,
     val_a_ref,
     rk_a_ref,
+    xkt_b_ref,
+    val_b_ref,
+    rk_b_ref,
     xkt_c_ref,
     val_c_ref,
     rk_c_ref,
@@ -401,7 +449,7 @@
     s_ref,
     z_ref,
 ):
-    own = ((xkt_a_ref, val_a_ref, rk_a_ref),)
+    own = ((xkt_a_ref, val_a_ref, rk_a_ref), (xkt_b_ref, val_b_ref, rk_b_ref))
     prev = ((xkt_c_ref, val_c_ref, rk_c_ref), (xkt_d_ref, val_d_ref, rk_d_ref))
     prepare(step, 1, (other_ref,), gram_hi_ref, gram_lo_ref, ak_ref, *prev[1])
     unpack(pay_ref, av_ref, 2)
@@ -431,7 +479,7 @@
                 span = slice(2 * TOK * h, 2 * TOK * (h + 1))
                 for (xkt_ref, _, rk_ref), keys in columns(every):
                     s = dot(qc_ref[g, span], xkt_ref[...]) * rk_ref[g, h : h + 1, :]
-                    s_ref[:, keys] = jnp.where(alone, -1e30, s) if keys.start else s
+                    s_ref[:, keys] = jnp.where(alone, -1e30, s) if keys.start >= 2 * SIDE else s
                 s = s_ref[...]
                 p_ref[span, :] = jnp.exp2(s - jnp.max(s, axis=1, keepdims=True)).astype(BF)
                 settle(g, h, collect(g, h, every, p_ref))
@@ -502,7 +550,7 @@
     )(sig, *[in_vmem(v) for v in (state, part, got, gain, final_weight, fresh)])
 
 
-def leave_kernel(first_ref, second_ref, queue_ref, est_ref, out_ref, sems):
+def leave_kernel(queue_ref, second_ref, first_ref, est_ref, out_ref, sems):
     pairs = ((first_ref, est_ref.at[0, 0]), (second_ref, est_ref.at[1, 0]), (queue_ref, out_ref.at[0]))
     copies = [pltpu.make_async_copy(src, dst, sems.at[i]) for i, (src, dst) in enumerate(pairs)]
     for copy in copies:
@@ -522,7 +570,7 @@
         out_specs=(ANY, ANY),
         scratch_shapes=[pltpu.SemaphoreType.DMA((3,))],
         name="leave",
-    )(in_vmem(first), in_vmem(second), in_vmem(queue))
+    )(in_vmem(queue), in_vmem(second), in_vmem(first))
 
 
 def passed_along(x, by):
@@ -556,6 +604,7 @@
     half = in_weight.shape[1] // 2
     freq = jnp.asarray(np.exp(-math.log(10000.0) * np.arange(half, dtype=np.float32) / half), F32)
     state = latents[0]
+    partner = swapped(state)
     sent, gram_hi, gram_lo, cond, qk, safe, sig = fold(
         level_index,
         plan,
@@ -569,15 +618,20 @@
         latents,
     )
     gram = (gram_hi, gram_lo)
+    sent, partner = lax.optimization_barrier((sent, partner))
     pay = spread(sent)
     mine = pay[:, PAY - TOK :, :]
     results = []
     for step in range(STEPS):
         other = swapped(mine)
         before = passed_along(mine, 1)
-        begun = list(attend_own(step, safe, pay, mine, other, gram, qk, out_weight))
+        ready = list(prepared_own(step, pay, mine, gram, qk, partner))
         if step == 0:
-            weights = begun.pop()
+            sums, *keys, weights = attend_own(step, safe, pay, mine, other, gram, qk, ready, out_weight)
+            queried = ready.pop()
+        else:
+            sums, *keys, queried = attend_own(step, safe, pay, mine, other, gram, qk, ready, out_weight)
+        begun = [sums, queried, *ready, *keys]
         before, *begun = lax.optimization_barrier((before, *begun))
         before_other = swapped(before)
         ready = prepared(step, begun[2], before, gram)

time: 111 us -> 110 us (level)
  waiting for transfers between devices: 12.5 us -> 9.82 us
  starting transfers between devices: 5.71 us -> 7.38 us
    ppermute x4, waiting for transfers between devices: 8.48 us -> 5.78 us  [passed_along(): lax.ppermute(x, 'frame', [(i, (i + by) % peers) for i in range(peers)])]
    pallas_call x0 -> x2, Pallas kernels: none -> 2.58 us  [prepared_own(): pl.pallas_call(functools.partial(prepare_own_kernel, step), out_shape=sha...]
    pallas_call x2, Pallas kernels: 9.18 us -> 7.52 us  [attend_own(): pl.pallas_call(functools.partial(own_kernel, step), out_shape=shapes, in_...]
    ppermute x4, starting transfers between devices: 4.92 us -> 6.49 us  [passed_along(): lax.ppermute(x, 'frame', [(i, (i + by) % peers) for i in range(peers)])]
    ppermute x6 -> x7, waiting for transfers between devices: 4.07 us -> 4.05 us  [swapped(): return lax.ppermute(x, 'core', [(0, 1), (1, 0)])]
  transfers between devices with their start and end apart: 10 -> 11, of which waited for: 7 -> 6; matrix products, arithmetic and copies ran while one was open for 0% -> 0% of each run, Pallas kernels for 10% -> 15%
where the time goes in v7:
time: 110 us
  Pallas kernels  52.2 us (47%)
  blocking collectives  39.3 us (36%)
  waiting for transfers between devices  9.82 us (9%)
  starting transfers between devices  7.38 us (7%)
    all_to_all x2, blocking collectives, spread(): return lax.all_to_all(x, ('y', 'far'), 0, 0, tiled=True)  39.3 us
    pallas_call x2, Pallas kernels, attend_prev(): pl.pallas_call(functools.partial(prev_kernel, step), out_shape=(pltpu.VME...  33.4 us
    pallas_call x2, Pallas kernels, attend_own(): pl.pallas_call(functools.partial(own_kernel, step), out_shape=shapes, in_...  7.52 us
    ppermute x4, starting transfers between devices, passed_along(): lax.ppermute(x, 'frame', [(i, (i + by) % peers) for i in range(peers)])  6.49 us
    ppermute x4, waiting for transfers between devices, passed_along(): lax.ppermute(x, 'frame', [(i, (i + by) % peers) for i in range(peers)])  5.78 us
    pallas_call x1, Pallas kernels, fold(): pl.pallas_call(fold_kernel, out_shape=(pltpu.VMEM((CHIPS, PAY, FEAT), BF)...  4.51 us
    ppermute x7, waiting for transfers between devices, swapped(): return lax.ppermute(x, 'core', [(0, 1), (1, 0)])  4.05 us
    pallas_call x2, Pallas kernels, prepared_own(): pl.pallas_call(functools.partial(prepare_own_kernel, step), out_shape=sha...  2.58 us
  transfers between devices with their start and end apart: 11, of which 6 were waited for; matrix products, arithmetic and copies ran while one was open for 0% of the time, Pallas kernels for 15%

profile of v7, /device:TPU:0, one launch (start us, length us, event | category | flops | bytes accessed | tf_op | source)
XLA Modules:
  0.0 109.7 jit_solution(12643729444137880288)
XLA Ops:
  0.6 0.1 collective-permute-start
  0.7 4.5 %fold.1 = (bf16[8,688,128]{2,1,0:T(8,128)(2,1)S(1)}, bf16[256,256]{1,0:T(8,128)(2,1)S(1)}, bf16[256,256]{1,0:T(8,128)(2,1)S(1)}, f32[8,3072]{1,0:T(8,128)S(1)}, ...) custom-call(s32[8]{0:T(128)} %level_hbm.1, s32[48]{0:T(128)} %plan_hbm.1, s32[10]{0:T(128)} %ids_hbm.1, ...), custom_call_target="tpu_custom_call" | custom-call | tf_op jit(solution)/shard_map/fold/pallas_call | solution.py:191
  5.2 0.0 collective-permute-done.refs_5_
  5.3 28.7 %all_to_all.10.refs_0_.pay_ref.refs_8_ = bf16[8,688,128]{2,1,0:T(8,128)(2,1)S(1)} all-to-all(bf16[8,688,128]{2,1,0:T(8,128)(2,1)S(1)} %get-tuple-element.68), channel_id=1, replica_groups=mesh['frame'=8,'y'=4,'far'=2,'core'=2] {'y','far'}, dimensions={0} | all-to-all | bytes 2818048 | tf_op jit(solution)/shard_map/all_to_all | solution.py:586
  33.9 0.1 collective-permute-start.2
  34.0 2.0 %collective-permute-start.1 = (bf16[8,64,128]{2,1,0:T(8,128)(2,1)S(1)}, bf16[8,64,128]{2,1,0:T(8,128)(2,1)S(1)}, u32[]{:S(2)}, u32[]{:S(2)}) collective-permute-start(bf16[8,64,128]{2,1,0:T(8,128)(2,1)S(1)} %slice.4.refs_1_), channel_id=1, source_target_pairs={{0,16},{16,32},{32,48},{48,64},{64,80},{80,96},{96,112},{112,0},{1... | collective-permute-start | bytes 393224 | tf_op jit(solution)/shard_map/ppermute | solution.py:578
  36.0 1.8 %prepare_own.2 = (bf16[1536,256]{1,0:T(8,128)(2,1)S(1)}, bf16[256,512]{1,0:T(8,128)(2,1)S(1)}, bf16[512,256]{1,0:T(8,128)(2,1)S(1)}, f32[6,8,512]{2,1,0:T(8,128)S(1)}, bf16[6,512,256]{2,1,0:T(8,128)(2,1)S(1)}) custom-call(bf16[8,688,128]{2,1,0:T(8,128)(2,1)S(1)} %all_to_all.10.refs_0_.pay_ref.refs_8_, bf16[8,64,128]{2,1,0:T(8,128)(2,1)S(1)} %slice.4.refs_1_, ...), custom_call_target="tpu_custom_call" | custom-call | flops 402653184 | bytes 1409024 | tf_op jit(solution)/shard_map/prepare_own/pallas_call | solution.py:293
  37.8 0.0 collective-permute-done.2.refs_1_
  37.8 0.0 copy-start
  37.8 0.0 copy-start.2
  37.8 5.1 %attend_own.2 = (f32[6,512,256]{2,1,0:T(8,128)S(1)}, bf16[256,512]{1,0:T(8,128)(2,1)S(1)}, bf16[512,256]{1,0:T(8,128)(2,1)S(1)}, f32[6,8,512]{2,1,0:T(8,128)S(1)}, bf16[1536,3072]{1,0:T(8,128)(2,1)S(1)}) custom-call(s32[1]{0:T(128)} %get-tuple-element.66.refs_0_.safe_ref, bf16[8,64,128]{2,1,0:T(8,128)(2,1)S(1)} %collective-permute-done.2.refs_1_, ...), custom_call_target="tpu_custom_call" | custom-call | flops 3221225472 | tf_op jit(solution)/shard_map/attend_own/pallas_call | solution.py:407
  42.9 0.0 collective-permute-done.1.block_ref
  43.0 0.2 collective-permute-start.3
  43.2 0.8 prepare.2
  44.0 0.4 collective-permute-done.3.other_ref
  44.4 0.0 copy-done
  44.4 0.0 copy-done.2
  44.4 0.0 copy-start.1
  44.4 0.0 copy-start.3
  44.4 0.0 copy-start.4
  44.4 16.6 %attend_prev.2 = (f32[64,3072]{1,0:T(8,128)S(1)}, bf16[64,3072]{1,0:T(8,128)(2,1)S(1)}) custom-call(s32[1]{0:T(128)} %get-tuple-element.66.refs_0_.safe_ref, bf16[8,688,128]{2,1,0:T(8,128)(2,1)S(1)} %all_to_all.10.refs_0_.pay_ref.refs_8_, bf16[8,64,128]{2,1,0:T(8,128)(2,1)S(1)} %collective-permute-done.3.other_ref, ...), custom_call_target="tpu_custom_call" | custom-call | flops 3221225472 | tf_op jit(solution)/shard_map/attend_prev/pallas_call | solution.py:507
  61.1 0.2 collective-permute-start.4
  61.3 1.6 %collective-permute-done.4.got_ref = bf16[64,3072]{1,0:T(8,128)(2,1)S(1)} collective-permute-done((bf16[64,3072]{1,0:T(8,128)(2,1)S(1)}, bf16[64,3072]{1,0:T(8,128)(2,1)S(1)}, u32[]{:S(2)}, u32[]{:S(2)}) %collective-permute-start.4) | collective-permute-done | bytes 393248 | tf_op jit(solution)/shard_map/ppermute | solution.py:582
  62.9 0.0 copy-done.1
  62.9 0.0 copy-done.3
  62.9 0.0 copy-done.4
  62.9 1.0 finish.2
  63.9 10.6 %all_to_all.11.refs_1_.refs_9_ = bf16[8,64,128]{2,1,0:T(8,128)(2,1)S(1)} all-to-all(bf16[8,64,128]{2,1,0:T(8,128)(2,1)S(1)} %get-tuple-element.100), channel_id=1, replica_groups=mesh['frame'=8,'y'=4,'far'=2,'core'=2] {'y','far'}, dimensions={0} | all-to-all | bytes 262144 | tf_op jit(solution)/shard_map/all_to_all | solution.py:586
  74.5 0.0 collective-permute-start.6
  74.5 1.9 %collective-permute-start.5 = (bf16[8,64,128]{2,1,0:T(8,128)(2,1)S(1)}, bf16[8,64,128]{2,1,0:T(8,128)(2,1)S(1)}, u32[]{:S(2)}, u32[]{:S(2)}) collective-permute-start(bf16[8,64,128]{2,1,0:T(8,128)(2,1)S(1)} %all_to_all.11.refs_1_.refs_9_), channel_id=1, source_target_pairs={{0,16},{16,32},{32,48},{48,64},{64,80},{80,96},{96,112},{112,0},{1... | collective-permute-start | bytes 393224 | tf_op jit(solution)/shard_map/ppermute | solution.py:578
  76.4 0.8 prepare_own.3
  77.2 0.0 collective-permute-done.6.refs_1_
  77.2 2.4 %attend_own.3 = (f32[6,512,256]{2,1,0:T(8,128)S(1)}, bf16[256,512]{1,0:T(8,128)(2,1)S(1)}, bf16[512,256]{1,0:T(8,128)(2,1)S(1)}, f32[6,8,512]{2,1,0:T(8,128)S(1)}, bf16[6,512,256]{2,1,0:T(8,128)(2,1)S(1)}) custom-call(s32[1]{0:T(128)} %get-tuple-element.66.refs_0_.safe_ref, bf16[8,64,128]{2,1,0:T(8,128)(2,1)S(1)} %collective-permute-done.6.refs_1_, ...), custom_call_target="tpu_custom_call" | custom-call | flops 3221225472 | tf_op jit(solution)/shard_map/attend_own/pallas_call | solution.py:407
  79.6 2.9 %collective-permute-done.5.block_ref = bf16[8,64,128]{2,1,0:T(8,128)(2,1)S(1)} collective-permute-done((bf16[8,64,128]{2,1,0:T(8,128)(2,1)S(1)}, bf16[8,64,128]{2,1,0:T(8,128)(2,1)S(1)}, u32[]{:S(2)}, u32[]{:S(2)}) %collective-permute-start.5) | collective-permute-done | bytes 131104 | tf_op jit(solution)/shard_map/ppermute | solution.py:578
  82.5 0.0 collective-permute-start.7
  82.5 0.8 prepare.3
  83.3 0.5 collective-permute-done.7.other_ref
  83.8 16.7 %attend_prev.3 = (f32[64,3072]{1,0:T(8,128)S(1)}, bf16[64,3072]{1,0:T(8,128)(2,1)S(1)}) custom-call(s32[1]{0:T(128)} %get-tuple-element.66.refs_0_.safe_ref, bf16[8,688,128]{2,1,0:T(8,128)(2,1)S(1)} %all_to_all.10.refs_0_.pay_ref.refs_8_, bf16[8,64,128]{2,1,0:T(8,128)(2,1)S(1)} %collective-permute-done.7.other_ref, ...), custom_call_target="tpu_custom_call" | custom-call | flops 3221225472 | tf_op jit(solution)/shard_map/attend_prev/pallas_call | solution.py:507
  100.6 0.2 collective-permute-start.8
  100.8 1.6 %collective-permute-done.8.got_ref = bf16[64,3072]{1,0:T(8,128)(2,1)S(1)} collective-permute-done((bf16[64,3072]{1,0:T(8,128)(2,1)S(1)}, bf16[64,3072]{1,0:T(8,128)(2,1)S(1)}, u32[]{:S(2)}, u32[]{:S(2)}) %collective-permute-start.8) | collective-permute-done | bytes 393248 | tf_op jit(solution)/shard_map/ppermute | solution.py:582
  102.4 1.0 finish.3
  103.4 1.6 %collective-permute-start.9 = (f32[64,128]{1,0:T(8,128)S(1)}, f32[64,128]{1,0:T(8,128)S(1)}, u32[]{:S(2)}, u32[]{:S(2)}) collective-permute-start(f32[64,128]{1,0:T(8,128)S(1)} %get-tuple-element.125), channel_id=1, source_target_pairs={{0,96},{16,112},{32,0},{48,16},{64,32},{80,48},{96,64},{112,80},{1... | collective-permute-start | bytes 98312 | tf_op jit(solution)/shard_map/ppermute | solution.py:578
  104.9 1.0 collective-permute-start.10
  105.9 2.9 %collective-permute-done.9.queue_ref = f32[64,128]{1,0:T(8,128)S(1)} collective-permute-done((f32[64,128]{1,0:T(8,128)S(1)}, f32[64,128]{1,0:T(8,128)S(1)}, u32[]{:S(2)}, u32[]{:S(2)}) %collective-permute-start.9) | collective-permute-done | bytes 32800 | tf_op jit(solution)/shard_map/ppermute | solution.py:578
  108.9 0.0 collective-permute-done.10.second_ref
  108.9 0.7 leave.1
  (1 shorter events, 0.0 us)
Async XLA Ops:
  0.6 4.6 %collective-permute-start = (f32[64,128]{1,0:T(8,128)}, f32[64,128]{1,0:T(8,128)S(1)}, u32[]{:S(2)}, u32[]{:S(2)}) collective-permute-start(f32[64,128]{1,0:T(8,128)} %bitcast.4), channel_id=1, source_target_pairs={{0,1},{1,0},{2,3},{3,2},{4,5},{5,4},{6,7},{7,6},{8,9},{9,8},{10,11... | collective-permute-start | bytes 98312 | tf_op jit(solution)/shard_map/ppermute | solution.py:582
  33.9 3.9 %collective-permute-start.2 = (bf16[8,64,128]{2,1,0:T(8,128)(2,1)S(1)}, bf16[8,64,128]{2,1,0:T(8,128)(2,1)S(1)}, u32[]{:S(2)}, u32[]{:S(2)}) collective-permute-start(bf16[8,64,128]{2,1,0:T(8,128)(2,1)S(1)} %slice.4.refs_1_), channel_id=1, source_target_pairs={{0,1},{1,0},{2,3},{3,2},{4,5},{5,4},{6,7},{7,6},{8,9},{9,8},{10,11... | collective-permute-start | bytes 393224 | tf_op jit(solution)/shard_map/ppermute | solution.py:582
  34.0 8.9 %collective-permute-start.1 = (bf16[8,64,128]{2,1,0:T(8,128)(2,1)S(1)}, bf16[8,64,128]{2,1,0:T(8,128)(2,1)S(1)}, u32[]{:S(2)}, u32[]{:S(2)}) collective-permute-start(bf16[8,64,128]{2,1,0:T(8,128)(2,1)S(1)} %slice.4.refs_1_), channel_id=1, source_target_pairs={{0,16},{16,32},{32,48},{48,64},{64,80},{80,96},{96,112},{112,0},{1... | collective-permute-start | bytes 393224 | tf_op jit(solution)/shard_map/ppermute | solution.py:578
  37.8 6.6 %copy-start = (bf16[128,3072]{1,0:T(8,128)(2,1)S(1)}, bf16[128,3072]{1,0:T(8,128)(2,1)}, u32[]{:S(2)}) copy-start(bf16[128,3072]{1,0:T(8,128)(2,1)} %in_ref.3) | copy-start | bytes 2359300
  37.8 6.6 %copy-start.2 = (f32[1,64,128]{2,1,0:T(8,128)S(1)}, f32[1,64,128]{2,1,0:T(8,128)}, u32[]{:S(2)}) copy-start(f32[1,64,128]{2,1,0:T(8,128)} %state_hbm.1) | copy-start | bytes 98308
  43.0 1.4 %collective-permute-start.3 = (bf16[8,64,128]{2,1,0:T(8,128)(2,1)S(1)}, bf16[8,64,128]{2,1,0:T(8,128)(2,1)S(1)}, u32[]{:S(2)}, u32[]{:S(2)}) collective-permute-start(bf16[8,64,128]{2,1,0:T(8,128)(2,1)S(1)} %collective-permute-done.1.block_ref), channel_id=1, source_target_pairs={{0,1},{1,0},{2,3},{3,2},{4,5},{5,4},{6,7},{7,6},{8,9},{9,8},{10,11... | collective-permute-start | bytes 393224 | tf_op jit(solution)/shard_map/ppermute | solution.py:582
  44.4 18.5 %copy-start.1 = (bf16[3072,128]{1,0:T(8,128)(2,1)S(1)}, bf16[3072,128]{1,0:T(8,128)(2,1)}, u32[]{:S(2)}) copy-start(bf16[3072,128]{1,0:T(8,128)(2,1)} %final_ref.3) | copy-start | bytes 2359300
  44.4 18.5 %copy-start.3 = (f32[2,64,128]{2,1,0:T(8,128)S(1)}, f32[2,64,128]{2,1,0:T(8,128)}, u32[]{:S(2)}) copy-start(f32[2,64,128]{2,1,0:T(8,128)} %fresh_ref.3) | copy-start | bytes 196612
  44.4 18.5 %copy-start.4 = (f32[3072]{0:T(1024)S(1)}, f32[3072]{0:T(1024)}, u32[]{:S(2)}) copy-start(f32[3072]{0:T(1024)} %param.25) | copy-start | bytes 36868
  61.1 1.8 %collective-permute-start.4 = (bf16[64,3072]{1,0:T(8,128)(2,1)S(1)}, bf16[64,3072]{1,0:T(8,128)(2,1)S(1)}, u32[]{:S(2)}, u32[]{:S(2)}) collective-permute-start(bf16[64,3072]{1,0:T(8,128)(2,1)S(1)} %get-tuple-element.98), channel_id=1, source_target_pairs={{0,1},{1,0},{2,3},{3,2},{4,5},{5,4},{6,7},{7,6},{8,9},{9,8},{10,11... | collective-permute-start | bytes 1179656 | tf_op jit(solution)/shard_map/ppermute | solution.py:582
  74.5 2.7 %collective-permute-start.6 = (bf16[8,64,128]{2,1,0:T(8,128)(2,1)S(1)}, bf16[8,64,128]{2,1,0:T(8,128)(2,1)S(1)}, u32[]{:S(2)}, u32[]{:S(2)}) collective-permute-start(bf16[8,64,128]{2,1,0:T(8,128)(2,1)S(1)} %all_to_all.11.refs_1_.refs_9_), channel_id=1, source_target_pairs={{0,1},{1,0},{2,3},{3,2},{4,5},{5,4},{6,7},{7,6},{8,9},{9,8},{10,11... | collective-permute-start | bytes 393224 | tf_op jit(solution)/shard_map/ppermute | solution.py:582
  74.5 8.0 %collective-permute-start.5 = (bf16[8,64,128]{2,1,0:T(8,128)(2,1)S(1)}, bf16[8,64,128]{2,1,0:T(8,128)(2,1)S(1)}, u32[]{:S(2)}, u32[]{:S(2)}) collective-permute-start(bf16[8,64,128]{2,1,0:T(8,128)(2,1)S(1)} %all_to_all.11.refs_1_.refs_9_), channel_id=1, source_target_pairs={{0,16},{16,32},{32,48},{48,64},{64,80},{80,96},{96,112},{112,0},{1... | collective-permute-start | bytes 393224 | tf_op jit(solution)/shard_map/ppermute | solution.py:578
  82.5 1.3 %collective-permute-start.7 = (bf16[8,64,128]{2,1,0:T(8,128)(2,1)S(1)}, bf16[8,64,128]{2,1,0:T(8,128)(2,1)S(1)}, u32[]{:S(2)}, u32[]{:S(2)}) collective-permute-start(bf16[8,64,128]{2,1,0:T(8,128)(2,1)S(1)} %collective-permute-done.5.block_ref), channel_id=1, source_target_pairs={{0,1},{1,0},{2,3},{3,2},{4,5},{5,4},{6,7},{7,6},{8,9},{9,8},{10,11... | collective-permute-start | bytes 393224 | tf_op jit(solution)/shard_map/ppermute | solution.py:582
  100.6 1.8 %collective-permute-start.8 = (bf16[64,3072]{1,0:T(8,128)(2,1)S(1)}, bf16[64,3072]{1,0:T(8,128)(2,1)S(1)}, u32[]{:S(2)}, u32[]{:S(2)}) collective-permute-start(bf16[64,3072]{1,0:T(8,128)(2,1)S(1)} %get-tuple-element.124), channel_id=1, source_target_pairs={{0,1},{1,0},{2,3},{3,2},{4,5},{5,4},{6,7},{7,6},{8,9},{9,8},{10,11... | collective-permute-start | bytes 1179656 | tf_op jit(solution)/shard_map/ppermute | solution.py:582
  103.4 5.5 %collective-permute-start.9 = (f32[64,128]{1,0:T(8,128)S(1)}, f32[64,128]{1,0:T(8,128)S(1)}, u32[]{:S(2)}, u32[]{:S(2)}) collective-permute-start(f32[64,128]{1,0:T(8,128)S(1)} %get-tuple-element.125), channel_id=1, source_target_pairs={{0,96},{16,112},{32,0},{48,16},{64,32},{80,48},{96,64},{112,80},{1... | collective-permute-start | bytes 98312 | tf_op jit(solution)/shard_map/ppermute | solution.py:578
  104.9 3.9 %collective-permute-start.10 = (f32[64,128]{1,0:T(8,128)S(1)}, f32[64,128]{1,0:T(8,128)S(1)}, u32[]{:S(2)}, u32[]{:S(2)}) collective-permute-start(f32[64,128]{1,0:T(8,128)S(1)} %get-tuple-element.126), channel_id=1, source_target_pairs={{0,112},{16,0},{32,16},{48,32},{64,48},{80,64},{96,80},{112,96},{1... | collective-permute-start | bytes 98312 | tf_op jit(solution)/shard_map/ppermute | solution.py:578

commit v8 on v7

--- a/solution.py
+++ b/solution.py
@@ -302,8 +302,25 @@
     )(*held)
 
 
-def prepare_kernel(step, ak_ref, block_ref, gram_hi_ref, gram_lo_ref, xkt_ref, val_ref, rk_ref):
+def prepare_kernel(
+    step,
+    ak_ref,
+    block_ref,
+    gram_hi_ref,
+    gram_lo_ref,
+    pay_ref,
+    state_ref,
+    in_ref,
+    cond_ref,
+    xkt_ref,
+    val_ref,
+    rk_ref,
+    av_ref,
+    hidden_ref,
+):
     prepare(step, 1, (block_ref,), gram_hi_ref, gram_lo_ref, ak_ref, xkt_ref, val_ref, rk_ref)
+    unpack(pay_ref, av_ref, 2)
+    hidden_ref[...] = dot(state_ref[...].astype(BF), in_ref[...]) + cond_ref[2 * step : 2 * step + 1, :]
 
 
 def side_shapes(count):
@@ -314,16 +331,19 @@
     ]
 
 
-def prepared(step, ak, block, gram):
+def prepared(step, ak, block, gram, pay, state, in_weight, cond):
+    held = [in_vmem(v) for v in (ak, block, *gram, pay, state, in_weight, cond)]
+    shapes = side_shapes(SIDE)
+    shapes += [pltpu.VMEM((HEADS * HEAD, WIDE), BF), pltpu.VMEM((TOK, in_weight.shape[1]), F32)]
     return pl.pallas_call(
         functools.partial(prepare_kernel, step),
-        out_shape=side_shapes(SIDE),
-        in_specs=[VMEM] * 4,
-        out_specs=[VMEM] * 3,
+        out_shape=shapes,
+        in_specs=[VMEM] * len(held),
+        out_specs=[VMEM] * len(shapes),
         compiler_params=pltpu.CompilerParams(vmem_limit_bytes=10 * 2**20),
         cost_estimate=cost(HEADS * HEAD * WIDE * SIDE),
         name="prepare",
-    )(*[in_vmem(v) for v in (ak, block, *gram)])
+    )(*held)
 
 
 def columns(sides):
@@ -419,7 +439,6 @@
 def prev_kernel(
     step,
     safe_ref,
-    pay_ref,
     other_ref,
     gram_hi_ref,
     gram_lo_ref,
@@ -435,16 +454,14 @@
     xkt_c_ref,
     val_c_ref,
     rk_c_ref,
+    av_ref,
+    hidden_ref,
     w_ref,
-    state_ref,
-    in_ref,
-    cond_ref,
     part_ref,
     part_other_ref,
     xkt_d_ref,
     val_d_ref,
     rk_d_ref,
-    av_ref,
     p_ref,
     s_ref,
     z_ref,
@@ -452,7 +469,6 @@
     own = ((xkt_a_ref, val_a_ref, rk_a_ref), (xkt_b_ref, val_b_ref, rk_b_ref))
     prev = ((xkt_c_ref, val_c_ref, rk_c_ref), (xkt_d_ref, val_d_ref, rk_d_ref))
     prepare(step, 1, (other_ref,), gram_hi_ref, gram_lo_ref, ak_ref, *prev[1])
-    unpack(pay_ref, av_ref, 2)
 
     def settle(g, h, z):
         z_ref[g, 2 * TOK * h : 2 * TOK * (h + 1)] = (z * (1.0 / z[:, ONE : ONE + 1])).astype(BF)
@@ -496,14 +512,13 @@
             picked = jnp.where(head_of == h, o[128 * h : 128 * (h + 1)], picked)
         outs.append(picked.astype(BF))
     y = dot(jnp.concatenate(outs, axis=1), w_ref[...])
-    hidden = dot(state_ref[...].astype(BF), in_ref[...]) + cond_ref[2 * step : 2 * step + 1, :]
-    part_ref[...] = hidden + y[0:TOK]
+    part_ref[...] = hidden_ref[...] + y[0:TOK]
     part_other_ref[...] = y[TOK:].astype(BF)
 
 
-def attend_prev(step, safe, pay, other, gram, begun, ready, weights, state, in_weight, cond):
+def attend_prev(step, safe, other, gram, begun, ready, weights):
     width = weights.shape[1]
-    held = [in_vmem(v) for v in (pay, other, *gram, *begun, *ready, weights, state, in_weight, cond)]
+    held = [in_vmem(v) for v in (other, *gram, *begun, *ready, weights)]
     return pl.pallas_call(
         functools.partial(prev_kernel, step),
         out_shape=(pltpu.VMEM((TOK, width), F32), pltpu.VMEM((TOK, width), BF)),
@@ -511,7 +526,6 @@
         out_specs=(VMEM, VMEM),
         scratch_shapes=side_shapes(SIDE)
         + [
-            pltpu.VMEM((HEADS * HEAD, WIDE), BF),
             pltpu.VMEM((8 * TOK, 4 * SIDE), BF),
             pltpu.VMEM((2 * TOK, 4 * SIDE), F32),
             pltpu.VMEM((GROUPS, 8 * TOK, WIDE), BF),
@@ -634,10 +648,8 @@
         begun = [sums, queried, *ready, *keys]
         before, *begun = lax.optimization_barrier((before, *begun))
         before_other = swapped(before)
-        ready = prepared(step, begun[2], before, gram)
-        part, part_other = attend_prev(
-            step, safe, pay, before_other, gram, begun, ready, weights, state, in_weight, cond
-        )
+        ready = prepared(step, begun[2], before, gram, pay, state, in_weight, cond)
+        part, part_other = attend_prev(step, safe, before_other, gram, begun, ready, weights)
         got = swapped(part_other)
         estimate, state, *sent = finish(step, sig, state, part, got, final_gain[None], final_weight, fresh_noise)
         results.append(estimate)

time: 110 us -> 109 us (level)
  no operation moved by 1% of the time
where the time goes in v8:
time: 109 us
  Pallas kernels  52 us (48%)
  blocking collectives  39.3 us (36%)
  waiting for transfers between devices  9.56 us (9%)
  starting transfers between devices  7.39 us (7%)
    all_to_all x2, blocking collectives, spread(): return lax.all_to_all(x, ('y', 'far'), 0, 0, tiled=True)  39.3 us
    pallas_call x2, Pallas kernels, attend_prev(): pl.pallas_call(functools.partial(prev_kernel, step), out_shape=(pltpu.VME...  32.9 us
    pallas_call x2, Pallas kernels, attend_own(): pl.pallas_call(functools.partial(own_kernel, step), out_shape=shapes, in_...  7.52 us
    ppermute x4, starting transfers between devices, passed_along(): lax.ppermute(x, 'frame', [(i, (i + by) % peers) for i in range(peers)])  6.49 us
    ppermute x4, waiting for transfers between devices, passed_along(): lax.ppermute(x, 'frame', [(i, (i + by) % peers) for i in range(peers)])  5.76 us
    pallas_call x1, Pallas kernels, fold(): pl.pallas_call(fold_kernel, out_shape=(pltpu.VMEM((CHIPS, PAY, FEAT), BF)...  4.51 us
    ppermute x7, waiting for transfers between devices, swapped(): return lax.ppermute(x, 'core', [(0, 1), (1, 0)])  3.8 us
    pallas_call x2, Pallas kernels, prepared_own(): pl.pallas_call(functools.partial(prepare_own_kernel, step), out_shape=sha...  2.59 us
  transfers between devices with their start and end apart: 11, of which 6 were waited for; matrix products, arithmetic and copies ran while one was open for 0% of the time, Pallas kernels for 15%

profile of v8, /device:TPU:0, one launch (start us, length us, event | category | flops | bytes accessed | tf_op | source)
XLA Modules:
  0.0 109.2 jit_solution(11349204103743042581)
XLA Ops:
  0.6 0.1 collective-permute-start
  0.7 4.5 %fold.1 = (bf16[8,688,128]{2,1,0:T(8,128)(2,1)S(1)}, bf16[256,256]{1,0:T(8,128)(2,1)S(1)}, bf16[256,256]{1,0:T(8,128)(2,1)S(1)}, f32[8,3072]{1,0:T(8,128)S(1)}, ...) custom-call(s32[8]{0:T(128)} %level_hbm.1, s32[48]{0:T(128)} %plan_hbm.1, s32[10]{0:T(128)} %ids_hbm.1, ...), custom_call_target="tpu_custom_call" | custom-call | tf_op jit(solution)/shard_map/fold/pallas_call | solution.py:191
  5.2 0.0 collective-permute-done.refs_5_
  5.3 28.7 %all_to_all.10.refs_0_.pay_ref.refs_8_ = bf16[8,688,128]{2,1,0:T(8,128)(2,1)S(1)} all-to-all(bf16[8,688,128]{2,1,0:T(8,128)(2,1)S(1)} %get-tuple-element.72), channel_id=1, replica_groups=mesh['frame'=8,'y'=4,'far'=2,'core'=2] {'y','far'}, dimensions={0} | all-to-all | bytes 2818048 | tf_op jit(solution)/shard_map/all_to_all | solution.py:600
  33.9 0.1 collective-permute-start.2
  34.0 2.0 %collective-permute-start.1 = (bf16[8,64,128]{2,1,0:T(8,128)(2,1)S(1)}, bf16[8,64,128]{2,1,0:T(8,128)(2,1)S(1)}, u32[]{:S(2)}, u32[]{:S(2)}) collective-permute-start(bf16[8,64,128]{2,1,0:T(8,128)(2,1)S(1)} %slice.4.refs_1_), channel_id=1, source_target_pairs={{0,16},{16,32},{32,48},{48,64},{64,80},{80,96},{96,112},{112,0},{1... | collective-permute-start | bytes 393224 | tf_op jit(solution)/shard_map/ppermute | solution.py:592
  36.0 1.8 %prepare_own.2 = (bf16[1536,256]{1,0:T(8,128)(2,1)S(1)}, bf16[256,512]{1,0:T(8,128)(2,1)S(1)}, bf16[512,256]{1,0:T(8,128)(2,1)S(1)}, f32[6,8,512]{2,1,0:T(8,128)S(1)}, bf16[6,512,256]{2,1,0:T(8,128)(2,1)S(1)}) custom-call(bf16[8,688,128]{2,1,0:T(8,128)(2,1)S(1)} %all_to_all.10.refs_0_.pay_ref.refs_8_, bf16[8,64,128]{2,1,0:T(8,128)(2,1)S(1)} %slice.4.refs_1_, ...), custom_call_target="tpu_custom_call" | custom-call | flops 402653184 | bytes 1409024 | tf_op jit(solution)/shard_map/prepare_own/pallas_call | solution.py:293
  37.8 0.0 collective-permute-done.2.refs_1_
  37.8 0.0 copy-start
  37.8 0.0 copy-start.2
  37.8 5.1 %attend_own.2 = (f32[6,512,256]{2,1,0:T(8,128)S(1)}, bf16[256,512]{1,0:T(8,128)(2,1)S(1)}, bf16[512,256]{1,0:T(8,128)(2,1)S(1)}, f32[6,8,512]{2,1,0:T(8,128)S(1)}, bf16[1536,3072]{1,0:T(8,128)(2,1)S(1)}) custom-call(s32[1]{0:T(128)} %get-tuple-element.70.refs_0_.safe_ref, bf16[8,64,128]{2,1,0:T(8,128)(2,1)S(1)} %collective-permute-done.2.refs_1_, ...), custom_call_target="tpu_custom_call" | custom-call | flops 3221225472 | tf_op jit(solution)/shard_map/attend_own/pallas_call | solution.py:427
  42.9 0.0 collective-permute-done.1.block_ref
  42.9 0.2 collective-permute-start.3
  43.2 0.0 copy-done
  43.2 0.0 copy-done.2
  43.2 0.9 prepare.2
  44.1 0.2 collective-permute-done.3.other_ref
  44.4 0.0 copy-start.1
  44.4 0.0 copy-start.3
  44.4 0.0 copy-start.4
  44.4 16.5 %attend_prev.2 = (f32[64,3072]{1,0:T(8,128)S(1)}, bf16[64,3072]{1,0:T(8,128)(2,1)S(1)}) custom-call(s32[1]{0:T(128)} %get-tuple-element.70.refs_0_.safe_ref, bf16[8,64,128]{2,1,0:T(8,128)(2,1)S(1)} %collective-permute-done.3.other_ref, bf16[256,256]{1,0:T(8,128)(2,1)S(1)} %get-tuple-element.73.refs_2_.gram_hi_ref, ...), custom_call_target="tpu_custom_call" | custom-call | flops 3221225472 | tf_op jit(solution)/shard_map/attend_prev/pallas_call | solution.py:522
  60.9 0.2 collective-permute-start.4
  61.2 1.6 %collective-permute-done.4.got_ref = bf16[64,3072]{1,0:T(8,128)(2,1)S(1)} collective-permute-done((bf16[64,3072]{1,0:T(8,128)(2,1)S(1)}, bf16[64,3072]{1,0:T(8,128)(2,1)S(1)}, u32[]{:S(2)}, u32[]{:S(2)}) %collective-permute-start.4) | collective-permute-done | bytes 393248 | tf_op jit(solution)/shard_map/ppermute | solution.py:596
  62.7 0.0 copy-done.1
  62.7 0.0 copy-done.3
  62.7 0.0 copy-done.4
  62.7 1.0 finish.2
  63.7 10.6 %all_to_all.11.refs_1_.refs_9_ = bf16[8,64,128]{2,1,0:T(8,128)(2,1)S(1)} all-to-all(bf16[8,64,128]{2,1,0:T(8,128)(2,1)S(1)} %get-tuple-element.106), channel_id=1, replica_groups=mesh['frame'=8,'y'=4,'far'=2,'core'=2] {'y','far'}, dimensions={0} | all-to-all | bytes 262144 | tf_op jit(solution)/shard_map/all_to_all | solution.py:600
  74.3 0.0 collective-permute-start.6
  74.3 1.9 %collective-permute-start.5 = (bf16[8,64,128]{2,1,0:T(8,128)(2,1)S(1)}, bf16[8,64,128]{2,1,0:T(8,128)(2,1)S(1)}, u32[]{:S(2)}, u32[]{:S(2)}) collective-permute-start(bf16[8,64,128]{2,1,0:T(8,128)(2,1)S(1)} %all_to_all.11.refs_1_.refs_9_), channel_id=1, source_target_pairs={{0,16},{16,32},{32,48},{48,64},{64,80},{80,96},{96,112},{112,0},{1... | collective-permute-start | bytes 393224 | tf_op jit(solution)/shard_map/ppermute | solution.py:592
  76.3 0.8 prepare_own.3
  77.1 0.0 collective-permute-done.6.refs_1_
  77.1 2.4 %attend_own.3 = (f32[6,512,256]{2,1,0:T(8,128)S(1)}, bf16[256,512]{1,0:T(8,128)(2,1)S(1)}, bf16[512,256]{1,0:T(8,128)(2,1)S(1)}, f32[6,8,512]{2,1,0:T(8,128)S(1)}, bf16[6,512,256]{2,1,0:T(8,128)(2,1)S(1)}) custom-call(s32[1]{0:T(128)} %get-tuple-element.70.refs_0_.safe_ref, bf16[8,64,128]{2,1,0:T(8,128)(2,1)S(1)} %collective-permute-done.6.refs_1_, ...), custom_call_target="tpu_custom_call" | custom-call | flops 3221225472 | tf_op jit(solution)/shard_map/attend_own/pallas_call | solution.py:427
  79.5 2.8 %collective-permute-done.5.block_ref = bf16[8,64,128]{2,1,0:T(8,128)(2,1)S(1)} collective-permute-done((bf16[8,64,128]{2,1,0:T(8,128)(2,1)S(1)}, bf16[8,64,128]{2,1,0:T(8,128)(2,1)S(1)}, u32[]{:S(2)}, u32[]{:S(2)}) %collective-permute-start.5) | collective-permute-done | bytes 131104 | tf_op jit(solution)/shard_map/ppermute | solution.py:592
  82.4 0.0 collective-permute-start.7
  82.4 0.9 prepare.3
  83.3 0.4 collective-permute-done.7.other_ref
  83.7 16.4 %attend_prev.3 = (f32[64,3072]{1,0:T(8,128)S(1)}, bf16[64,3072]{1,0:T(8,128)(2,1)S(1)}) custom-call(s32[1]{0:T(128)} %get-tuple-element.70.refs_0_.safe_ref, bf16[8,64,128]{2,1,0:T(8,128)(2,1)S(1)} %collective-permute-done.7.other_ref, bf16[256,256]{1,0:T(8,128)(2,1)S(1)} %get-tuple-element.73.refs_2_.gram_hi_ref, ...), custom_call_target="tpu_custom_call" | custom-call | flops 3221225472 | tf_op jit(solution)/shard_map/attend_prev/pallas_call | solution.py:522
  100.1 0.2 collective-permute-start.8
  100.3 1.6 %collective-permute-done.8.got_ref = bf16[64,3072]{1,0:T(8,128)(2,1)S(1)} collective-permute-done((bf16[64,3072]{1,0:T(8,128)(2,1)S(1)}, bf16[64,3072]{1,0:T(8,128)(2,1)S(1)}, u32[]{:S(2)}, u32[]{:S(2)}) %collective-permute-start.8) | collective-permute-done | bytes 393248 | tf_op jit(solution)/shard_map/ppermute | solution.py:596
  101.9 1.0 finish.3
  102.9 1.6 %collective-permute-start.9 = (f32[64,128]{1,0:T(8,128)S(1)}, f32[64,128]{1,0:T(8,128)S(1)}, u32[]{:S(2)}, u32[]{:S(2)}) collective-permute-start(f32[64,128]{1,0:T(8,128)S(1)} %get-tuple-element.133), channel_id=1, source_target_pairs={{0,96},{16,112},{32,0},{48,16},{64,32},{80,48},{96,64},{112,80},{1... | collective-permute-start | bytes 98312 | tf_op jit(solution)/shard_map/ppermute | solution.py:592
  104.4 1.0 collective-permute-start.10
  105.4 2.9 %collective-permute-done.9.queue_ref = f32[64,128]{1,0:T(8,128)S(1)} collective-permute-done((f32[64,128]{1,0:T(8,128)S(1)}, f32[64,128]{1,0:T(8,128)S(1)}, u32[]{:S(2)}, u32[]{:S(2)}) %collective-permute-start.9) | collective-permute-done | bytes 32800 | tf_op jit(solution)/shard_map/ppermute | solution.py:592
  108.4 0.0 collective-permute-done.10.second_ref
  108.4 0.7 leave.1
  (1 shorter events, 0.0 us)
Async XLA Ops:
  0.6 4.6 %collective-permute-start = (f32[64,128]{1,0:T(8,128)}, f32[64,128]{1,0:T(8,128)S(1)}, u32[]{:S(2)}, u32[]{:S(2)}) collective-permute-start(f32[64,128]{1,0:T(8,128)} %bitcast.4), channel_id=1, source_target_pairs={{0,1},{1,0},{2,3},{3,2},{4,5},{5,4},{6,7},{7,6},{8,9},{9,8},{10,11... | collective-permute-start | bytes 98312 | tf_op jit(solution)/shard_map/ppermute | solution.py:596
  33.9 3.9 %collective-permute-start.2 = (bf16[8,64,128]{2,1,0:T(8,128)(2,1)S(1)}, bf16[8,64,128]{2,1,0:T(8,128)(2,1)S(1)}, u32[]{:S(2)}, u32[]{:S(2)}) collective-permute-start(bf16[8,64,128]{2,1,0:T(8,128)(2,1)S(1)} %slice.4.refs_1_), channel_id=1, source_target_pairs={{0,1},{1,0},{2,3},{3,2},{4,5},{5,4},{6,7},{7,6},{8,9},{9,8},{10,11... | collective-permute-start | bytes 393224 | tf_op jit(solution)/shard_map/ppermute | solution.py:596
  34.0 8.9 %collective-permute-start.1 = (bf16[8,64,128]{2,1,0:T(8,128)(2,1)S(1)}, bf16[8,64,128]{2,1,0:T(8,128)(2,1)S(1)}, u32[]{:S(2)}, u32[]{:S(2)}) collective-permute-start(bf16[8,64,128]{2,1,0:T(8,128)(2,1)S(1)} %slice.4.refs_1_), channel_id=1, source_target_pairs={{0,16},{16,32},{32,48},{48,64},{64,80},{80,96},{96,112},{112,0},{1... | collective-permute-start | bytes 393224 | tf_op jit(solution)/shard_map/ppermute | solution.py:592
  37.8 5.4 %copy-start = (bf16[128,3072]{1,0:T(8,128)(2,1)S(1)}, bf16[128,3072]{1,0:T(8,128)(2,1)}, u32[]{:S(2)}) copy-start(bf16[128,3072]{1,0:T(8,128)(2,1)} %in_ref.3) | copy-start | bytes 2359300
  37.8 5.4 %copy-start.2 = (f32[1,64,128]{2,1,0:T(8,128)S(1)}, f32[1,64,128]{2,1,0:T(8,128)}, u32[]{:S(2)}) copy-start(f32[1,64,128]{2,1,0:T(8,128)} %state_hbm.1) | copy-start | bytes 98308
  42.9 1.4 %collective-permute-start.3 = (bf16[8,64,128]{2,1,0:T(8,128)(2,1)S(1)}, bf16[8,64,128]{2,1,0:T(8,128)(2,1)S(1)}, u32[]{:S(2)}, u32[]{:S(2)}) collective-permute-start(bf16[8,64,128]{2,1,0:T(8,128)(2,1)S(1)} %collective-permute-done.1.block_ref), channel_id=1, source_target_pairs={{0,1},{1,0},{2,3},{3,2},{4,5},{5,4},{6,7},{7,6},{8,9},{9,8},{10,11... | collective-permute-start | bytes 393224 | tf_op jit(solution)/shard_map/ppermute | solution.py:596
  44.4 18.4 %copy-start.1 = (bf16[3072,128]{1,0:T(8,128)(2,1)S(1)}, bf16[3072,128]{1,0:T(8,128)(2,1)}, u32[]{:S(2)}) copy-start(bf16[3072,128]{1,0:T(8,128)(2,1)} %final_ref.3) | copy-start | bytes 2359300
  44.4 18.4 %copy-start.3 = (f32[2,64,128]{2,1,0:T(8,128)S(1)}, f32[2,64,128]{2,1,0:T(8,128)}, u32[]{:S(2)}) copy-start(f32[2,64,128]{2,1,0:T(8,128)} %fresh_ref.3) | copy-start | bytes 196612
  44.4 18.4 %copy-start.4 = (f32[3072]{0:T(1024)S(1)}, f32[3072]{0:T(1024)}, u32[]{:S(2)}) copy-start(f32[3072]{0:T(1024)} %param.25) | copy-start | bytes 36868
  60.9 1.8 %collective-permute-start.4 = (bf16[64,3072]{1,0:T(8,128)(2,1)S(1)}, bf16[64,3072]{1,0:T(8,128)(2,1)S(1)}, u32[]{:S(2)}, u32[]{:S(2)}) collective-permute-start(bf16[64,3072]{1,0:T(8,128)(2,1)S(1)} %get-tuple-element.104), channel_id=1, source_target_pairs={{0,1},{1,0},{2,3},{3,2},{4,5},{5,4},{6,7},{7,6},{8,9},{9,8},{10,11... | collective-permute-start | bytes 1179656 | tf_op jit(solution)/shard_map/ppermute | solution.py:596
  74.3 2.7 %collective-permute-start.6 = (bf16[8,64,128]{2,1,0:T(8,128)(2,1)S(1)}, bf16[8,64,128]{2,1,0:T(8,128)(2,1)S(1)}, u32[]{:S(2)}, u32[]{:S(2)}) collective-permute-start(bf16[8,64,128]{2,1,0:T(8,128)(2,1)S(1)} %all_to_all.11.refs_1_.refs_9_), channel_id=1, source_target_pairs={{0,1},{1,0},{2,3},{3,2},{4,5},{5,4},{6,7},{7,6},{8,9},{9,8},{10,11... | collective-permute-start | bytes 393224 | tf_op jit(solution)/shard_map/ppermute | solution.py:596
  74.3 8.0 %collective-permute-start.5 = (bf16[8,64,128]{2,1,0:T(8,128)(2,1)S(1)}, bf16[8,64,128]{2,1,0:T(8,128)(2,1)S(1)}, u32[]{:S(2)}, u32[]{:S(2)}) collective-permute-start(bf16[8,64,128]{2,1,0:T(8,128)(2,1)S(1)} %all_to_all.11.refs_1_.refs_9_), channel_id=1, source_target_pairs={{0,16},{16,32},{32,48},{48,64},{64,80},{80,96},{96,112},{112,0},{1... | collective-permute-start | bytes 393224 | tf_op jit(solution)/shard_map/ppermute | solution.py:592
  82.4 1.3 %collective-permute-start.7 = (bf16[8,64,128]{2,1,0:T(8,128)(2,1)S(1)}, bf16[8,64,128]{2,1,0:T(8,128)(2,1)S(1)}, u32[]{:S(2)}, u32[]{:S(2)}) collective-permute-start(bf16[8,64,128]{2,1,0:T(8,128)(2,1)S(1)} %collective-permute-done.5.block_ref), channel_id=1, source_target_pairs={{0,1},{1,0},{2,3},{3,2},{4,5},{5,4},{6,7},{7,6},{8,9},{9,8},{10,11... | collective-permute-start | bytes 393224 | tf_op jit(solution)/shard_map/ppermute | solution.py:596
  100.1 1.8 %collective-permute-start.8 = (bf16[64,3072]{1,0:T(8,128)(2,1)S(1)}, bf16[64,3072]{1,0:T(8,128)(2,1)S(1)}, u32[]{:S(2)}, u32[]{:S(2)}) collective-permute-start(bf16[64,3072]{1,0:T(8,128)(2,1)S(1)} %get-tuple-element.132), channel_id=1, source_target_pairs={{0,1},{1,0},{2,3},{3,2},{4,5},{5,4},{6,7},{7,6},{8,9},{9,8},{10,11... | collective-permute-start | bytes 1179656 | tf_op jit(solution)/shard_map/ppermute | solution.py:596
  102.9 5.5 %collective-permute-start.9 = (f32[64,128]{1,0:T(8,128)S(1)}, f32[64,128]{1,0:T(8,128)S(1)}, u32[]{:S(2)}, u32[]{:S(2)}) collective-permute-start(f32[64,128]{1,0:T(8,128)S(1)} %get-tuple-element.133), channel_id=1, source_target_pairs={{0,96},{16,112},{32,0},{48,16},{64,32},{80,48},{96,64},{112,80},{1... | collective-permute-start | bytes 98312 | tf_op jit(solution)/shard_map/ppermute | solution.py:592
  104.4 3.9 %collective-permute-start.10 = (f32[64,128]{1,0:T(8,128)S(1)}, f32[64,128]{1,0:T(8,128)S(1)}, u32[]{:S(2)}, u32[]{:S(2)}) collective-permute-start(f32[64,128]{1,0:T(8,128)S(1)} %get-tuple-element.134), channel_id=1, source_target_pairs={{0,112},{16,0},{32,16},{48,32},{64,48},{80,64},{96,80},{112,96},{1... | collective-permute-start | bytes 98312 | tf_op jit(solution)/shard_map/ppermute | solution.py:592

commit v9 on v8

--- a/solution.py
+++ b/solution.py
@@ -44,6 +44,11 @@
 def halves(x):
     high = x.astype(BF)
     return high, (x - high.astype(F32)).astype(BF)
+
+
+def stacked_halves(x):
+    high = x.astype(BF).astype(F32)
+    return jnp.concatenate([high, x - high], axis=0).astype(BF)
 
 
 def in_vmem(x):
@@ -152,8 +157,7 @@
     none = jnp.zeros((112, embed.shape[1]), BF)
     gain = gain_ref[...]
     emb = (embed.astype(F32) * gain).astype(BF)
-    cg_hi, cg_lo = halves(cond * gain)
-    right = jnp.concatenate([emb, jnp.concatenate([cg_hi, cg_lo], axis=0), none], axis=0)
+    right = jnp.concatenate([emb, stacked_halves(cond * gain), none], axis=0)
     copies[5].wait()
     full = dot_t(w_ref[...].reshape(3 * COLS, embed.shape[1]), right)
     mat = full[:, 0:FEAT].astype(BF)
@@ -173,8 +177,7 @@
         pay_ref[chip, 3 * COLS : 3 * COLS + PACK] = packed
         pay_ref[chip, PAY - TOK : PAY] = x
 
-    c_hi, c_lo = halves(cond)
-    left = jnp.concatenate([embed, jnp.concatenate([c_hi, c_lo], axis=0)], axis=0)
+    left = jnp.concatenate([embed, stacked_halves(cond)], axis=0)
     gram = dot_t(left, jnp.concatenate([left, none], axis=0))
     gram = jnp.concatenate([gram, jnp.zeros((112, WIDE), F32)], axis=0)
     lane, row = lanes(gram.shape), rows(gram.shape)

time: 109 us -> 109 us (level)
  no operation moved by 1% of the time
where the time goes in v9:
time: 109 us
  Pallas kernels  52 us (48%)
  blocking collectives  39.3 us (36%)
  waiting for transfers between devices  9.55 us (9%)
  starting transfers between devices  7.39 us (7%)
    all_to_all x2, blocking collectives, spread(): return lax.all_to_all(x, ('y', 'far'), 0, 0, tiled=True)  39.3 us
    pallas_call x2, Pallas kernels, attend_prev(): pl.pallas_call(functools.partial(prev_kernel, step), out_shape=(pltpu.VME...  32.9 us
    pallas_call x2, Pallas kernels, attend_own(): pl.pallas_call(functools.partial(own_kernel, step), out_shape=shapes, in_...  7.52 us
    ppermute x4, starting transfers between devices, passed_along(): lax.ppermute(x, 'frame', [(i, (i + by) % peers) for i in range(peers)])  6.5 us
    ppermute x4, waiting for transfers between devices, passed_along(): lax.ppermute(x, 'frame', [(i, (i + by) % peers) for i in range(peers)])  5.75 us
    pallas_call x1, Pallas kernels, fold(): pl.pallas_call(fold_kernel, out_shape=(pltpu.VMEM((CHIPS, PAY, FEAT), BF)...  4.5 us
    ppermute x7, waiting for transfers between devices, swapped(): return lax.ppermute(x, 'core', [(0, 1), (1, 0)])  3.8 us
    pallas_call x2, Pallas kernels, prepared_own(): pl.pallas_call(functools.partial(prepare_own_kernel, step), out_shape=sha...  2.6 us
  transfers between devices with their start and end apart: 11, of which 6 were waited for; matrix products, arithmetic and copies ran while one was open for 0% of the time, Pallas kernels for 15%

profile of v9, /device:TPU:0, one launch (start us, length us, event | category | flops | bytes accessed | tf_op | source)
XLA Modules:
  0.0 109.2 jit_solution(10518898813478205879)
XLA Ops:
  0.6 0.1 collective-permute-start
  0.7 4.5 %fold.1 = (bf16[8,688,128]{2,1,0:T(8,128)(2,1)S(1)}, bf16[256,256]{1,0:T(8,128)(2,1)S(1)}, bf16[256,256]{1,0:T(8,128)(2,1)S(1)}, f32[8,3072]{1,0:T(8,128)S(1)}, ...) custom-call(s32[8]{0:T(128)} %level_hbm.1, s32[48]{0:T(128)} %plan_hbm.1, s32[10]{0:T(128)} %ids_hbm.1, ...), custom_call_target="tpu_custom_call" | custom-call | tf_op jit(solution)/shard_map/fold/pallas_call | solution.py:194
  5.2 0.0 collective-permute-done.refs_5_
  5.2 28.7 %all_to_all.10.refs_0_.pay_ref.refs_8_ = bf16[8,688,128]{2,1,0:T(8,128)(2,1)S(1)} all-to-all(bf16[8,688,128]{2,1,0:T(8,128)(2,1)S(1)} %get-tuple-element.72), channel_id=1, replica_groups=mesh['frame'=8,'y'=4,'far'=2,'core'=2] {'y','far'}, dimensions={0} | all-to-all | bytes 2818048 | tf_op jit(solution)/shard_map/all_to_all | solution.py:603
  33.9 0.1 collective-permute-start.2
  34.0 2.0 %collective-permute-start.1 = (bf16[8,64,128]{2,1,0:T(8,128)(2,1)S(1)}, bf16[8,64,128]{2,1,0:T(8,128)(2,1)S(1)}, u32[]{:S(2)}, u32[]{:S(2)}) collective-permute-start(bf16[8,64,128]{2,1,0:T(8,128)(2,1)S(1)} %slice.4.refs_1_), channel_id=1, source_target_pairs={{0,16},{16,32},{32,48},{48,64},{64,80},{80,96},{96,112},{112,0},{1... | collective-permute-start | bytes 393224 | tf_op jit(solution)/shard_map/ppermute | solution.py:595
  36.0 1.8 %prepare_own.2 = (bf16[1536,256]{1,0:T(8,128)(2,1)S(1)}, bf16[256,512]{1,0:T(8,128)(2,1)S(1)}, bf16[512,256]{1,0:T(8,128)(2,1)S(1)}, f32[6,8,512]{2,1,0:T(8,128)S(1)}, bf16[6,512,256]{2,1,0:T(8,128)(2,1)S(1)}) custom-call(bf16[8,688,128]{2,1,0:T(8,128)(2,1)S(1)} %all_to_all.10.refs_0_.pay_ref.refs_8_, bf16[8,64,128]{2,1,0:T(8,128)(2,1)S(1)} %slice.4.refs_1_, ...), custom_call_target="tpu_custom_call" | custom-call | flops 402653184 | bytes 1409024 | tf_op jit(solution)/shard_map/prepare_own/pallas_call | solution.py:296
  37.8 0.0 collective-permute-done.2.refs_1_
  37.8 0.0 copy-start
  37.8 0.0 copy-start.2
  37.8 5.1 %attend_own.2 = (f32[6,512,256]{2,1,0:T(8,128)S(1)}, bf16[256,512]{1,0:T(8,128)(2,1)S(1)}, bf16[512,256]{1,0:T(8,128)(2,1)S(1)}, f32[6,8,512]{2,1,0:T(8,128)S(1)}, bf16[1536,3072]{1,0:T(8,128)(2,1)S(1)}) custom-call(s32[1]{0:T(128)} %get-tuple-element.70.refs_0_.safe_ref, bf16[8,64,128]{2,1,0:T(8,128)(2,1)S(1)} %collective-permute-done.2.refs_1_, ...), custom_call_target="tpu_custom_call" | custom-call | flops 3221225472 | tf_op jit(solution)/shard_map/attend_own/pallas_call | solution.py:430
  42.9 0.0 collective-permute-done.1.block_ref
  43.0 0.2 collective-permute-start.3
  43.2 0.0 copy-done
  43.2 0.0 copy-done.2
  43.2 0.9 prepare.2
  44.1 0.2 collective-permute-done.3.other_ref
  44.4 0.0 copy-start.1
  44.4 0.0 copy-start.3
  44.4 0.0 copy-start.4
  44.4 16.5 %attend_prev.2 = (f32[64,3072]{1,0:T(8,128)S(1)}, bf16[64,3072]{1,0:T(8,128)(2,1)S(1)}) custom-call(s32[1]{0:T(128)} %get-tuple-element.70.refs_0_.safe_ref, bf16[8,64,128]{2,1,0:T(8,128)(2,1)S(1)} %collective-permute-done.3.other_ref, bf16[256,256]{1,0:T(8,128)(2,1)S(1)} %get-tuple-element.73.refs_2_.gram_hi_ref, ...), custom_call_target="tpu_custom_call" | custom-call | flops 3221225472 | tf_op jit(solution)/shard_map/attend_prev/pallas_call | solution.py:525
  60.9 0.2 collective-permute-start.4
  61.2 1.6 %collective-permute-done.4.got_ref = bf16[64,3072]{1,0:T(8,128)(2,1)S(1)} collective-permute-done((bf16[64,3072]{1,0:T(8,128)(2,1)S(1)}, bf16[64,3072]{1,0:T(8,128)(2,1)S(1)}, u32[]{:S(2)}, u32[]{:S(2)}) %collective-permute-start.4) | collective-permute-done | bytes 393248 | tf_op jit(solution)/shard_map/ppermute | solution.py:599
  62.7 0.0 copy-done.1
  62.7 0.0 copy-done.3
  62.7 0.0 copy-done.4
  62.7 1.0 finish.2
  63.7 10.6 %all_to_all.11.refs_1_.refs_9_ = bf16[8,64,128]{2,1,0:T(8,128)(2,1)S(1)} all-to-all(bf16[8,64,128]{2,1,0:T(8,128)(2,1)S(1)} %get-tuple-element.106), channel_id=1, replica_groups=mesh['frame'=8,'y'=4,'far'=2,'core'=2] {'y','far'}, dimensions={0} | all-to-all | bytes 262144 | tf_op jit(solution)/shard_map/all_to_all | solution.py:603
  74.3 0.0 collective-permute-start.6
  74.3 1.9 %collective-permute-start.5 = (bf16[8,64,128]{2,1,0:T(8,128)(2,1)S(1)}, bf16[8,64,128]{2,1,0:T(8,128)(2,1)S(1)}, u32[]{:S(2)}, u32[]{:S(2)}) collective-permute-start(bf16[8,64,128]{2,1,0:T(8,128)(2,1)S(1)} %all_to_all.11.refs_1_.refs_9_), channel_id=1, source_target_pairs={{0,16},{16,32},{32,48},{48,64},{64,80},{80,96},{96,112},{112,0},{1... | collective-permute-start | bytes 393224 | tf_op jit(solution)/shard_map/ppermute | solution.py:595
  76.2 0.8 prepare_own.3
  77.1 0.0 collective-permute-done.6.refs_1_
  77.1 2.4 %attend_own.3 = (f32[6,512,256]{2,1,0:T(8,128)S(1)}, bf16[256,512]{1,0:T(8,128)(2,1)S(1)}, bf16[512,256]{1,0:T(8,128)(2,1)S(1)}, f32[6,8,512]{2,1,0:T(8,128)S(1)}, bf16[6,512,256]{2,1,0:T(8,128)(2,1)S(1)}) custom-call(s32[1]{0:T(128)} %get-tuple-element.70.refs_0_.safe_ref, bf16[8,64,128]{2,1,0:T(8,128)(2,1)S(1)} %collective-permute-done.6.refs_1_, ...), custom_call_target="tpu_custom_call" | custom-call | flops 3221225472 | tf_op jit(solution)/shard_map/attend_own/pallas_call | solution.py:430
  79.5 2.8 %collective-permute-done.5.block_ref = bf16[8,64,128]{2,1,0:T(8,128)(2,1)S(1)} collective-permute-done((bf16[8,64,128]{2,1,0:T(8,128)(2,1)S(1)}, bf16[8,64,128]{2,1,0:T(8,128)(2,1)S(1)}, u32[]{:S(2)}, u32[]{:S(2)}) %collective-permute-start.5) | collective-permute-done | bytes 131104 | tf_op jit(solution)/shard_map/ppermute | solution.py:595
  82.3 0.0 collective-permute-start.7
  82.3 0.9 prepare.3
  83.3 0.4 collective-permute-done.7.other_ref
  83.7 16.4 %attend_prev.3 = (f32[64,3072]{1,0:T(8,128)S(1)}, bf16[64,3072]{1,0:T(8,128)(2,1)S(1)}) custom-call(s32[1]{0:T(128)} %get-tuple-element.70.refs_0_.safe_ref, bf16[8,64,128]{2,1,0:T(8,128)(2,1)S(1)} %collective-permute-done.7.other_ref, bf16[256,256]{1,0:T(8,128)(2,1)S(1)} %get-tuple-element.73.refs_2_.gram_hi_ref, ...), custom_call_target="tpu_custom_call" | custom-call | flops 3221225472 | tf_op jit(solution)/shard_map/attend_prev/pallas_call | solution.py:525
  100.1 0.2 collective-permute-start.8
  100.3 1.6 %collective-permute-done.8.got_ref = bf16[64,3072]{1,0:T(8,128)(2,1)S(1)} collective-permute-done((bf16[64,3072]{1,0:T(8,128)(2,1)S(1)}, bf16[64,3072]{1,0:T(8,128)(2,1)S(1)}, u32[]{:S(2)}, u32[]{:S(2)}) %collective-permute-start.8) | collective-permute-done | bytes 393248 | tf_op jit(solution)/shard_map/ppermute | solution.py:599
  101.9 1.0 finish.3
  102.9 1.6 %collective-permute-start.9 = (f32[64,128]{1,0:T(8,128)S(1)}, f32[64,128]{1,0:T(8,128)S(1)}, u32[]{:S(2)}, u32[]{:S(2)}) collective-permute-start(f32[64,128]{1,0:T(8,128)S(1)} %get-tuple-element.133), channel_id=1, source_target_pairs={{0,96},{16,112},{32,0},{48,16},{64,32},{80,48},{96,64},{112,80},{1... | collective-permute-start | bytes 98312 | tf_op jit(solution)/shard_map/ppermute | solution.py:595
  104.4 1.0 collective-permute-start.10
  105.4 2.9 %collective-permute-done.9.queue_ref = f32[64,128]{1,0:T(8,128)S(1)} collective-permute-done((f32[64,128]{1,0:T(8,128)S(1)}, f32[64,128]{1,0:T(8,128)S(1)}, u32[]{:S(2)}, u32[]{:S(2)}) %collective-permute-start.9) | collective-permute-done | bytes 32800 | tf_op jit(solution)/shard_map/ppermute | solution.py:595
  108.3 0.0 collective-permute-done.10.second_ref
  108.4 0.7 leave.1
  (1 shorter events, 0.0 us)
Async XLA Ops:
  0.6 4.6 %collective-permute-start = (f32[64,128]{1,0:T(8,128)}, f32[64,128]{1,0:T(8,128)S(1)}, u32[]{:S(2)}, u32[]{:S(2)}) collective-permute-start(f32[64,128]{1,0:T(8,128)} %bitcast.4), channel_id=1, source_target_pairs={{0,1},{1,0},{2,3},{3,2},{4,5},{5,4},{6,7},{7,6},{8,9},{9,8},{10,11... | collective-permute-start | bytes 98312 | tf_op jit(solution)/shard_map/ppermute | solution.py:599
  33.9 3.9 %collective-permute-start.2 = (bf16[8,64,128]{2,1,0:T(8,128)(2,1)S(1)}, bf16[8,64,128]{2,1,0:T(8,128)(2,1)S(1)}, u32[]{:S(2)}, u32[]{:S(2)}) collective-permute-start(bf16[8,64,128]{2,1,0:T(8,128)(2,1)S(1)} %slice.4.refs_1_), channel_id=1, source_target_pairs={{0,1},{1,0},{2,3},{3,2},{4,5},{5,4},{6,7},{7,6},{8,9},{9,8},{10,11... | collective-permute-start | bytes 393224 | tf_op jit(solution)/shard_map/ppermute | solution.py:599
  34.0 8.9 %collective-permute-start.1 = (bf16[8,64,128]{2,1,0:T(8,128)(2,1)S(1)}, bf16[8,64,128]{2,1,0:T(8,128)(2,1)S(1)}, u32[]{:S(2)}, u32[]{:S(2)}) collective-permute-start(bf16[8,64,128]{2,1,0:T(8,128)(2,1)S(1)} %slice.4.refs_1_), channel_id=1, source_target_pairs={{0,16},{16,32},{32,48},{48,64},{64,80},{80,96},{96,112},{112,0},{1... | collective-permute-start | bytes 393224 | tf_op jit(solution)/shard_map/ppermute | solution.py:595
  37.8 5.4 %copy-start = (bf16[128,3072]{1,0:T(8,128)(2,1)S(1)}, bf16[128,3072]{1,0:T(8,128)(2,1)}, u32[]{:S(2)}) copy-start(bf16[128,3072]{1,0:T(8,128)(2,1)} %in_ref.3) | copy-start | bytes 2359300
  37.8 5.4 %copy-start.2 = (f32[1,64,128]{2,1,0:T(8,128)S(1)}, f32[1,64,128]{2,1,0:T(8,128)}, u32[]{:S(2)}) copy-start(f32[1,64,128]{2,1,0:T(8,128)} %state_hbm.1) | copy-start | bytes 98308
  43.0 1.4 %collective-permute-start.3 = (bf16[8,64,128]{2,1,0:T(8,128)(2,1)S(1)}, bf16[8,64,128]{2,1,0:T(8,128)(2,1)S(1)}, u32[]{:S(2)}, u32[]{:S(2)}) collective-permute-start(bf16[8,64,128]{2,1,0:T(8,128)(2,1)S(1)} %collective-permute-done.1.block_ref), channel_id=1, source_target_pairs={{0,1},{1,0},{2,3},{3,2},{4,5},{5,4},{6,7},{7,6},{8,9},{9,8},{10,11... | collective-permute-start | bytes 393224 | tf_op jit(solution)/shard_map/ppermute | solution.py:599
  44.4 18.3 %copy-start.1 = (bf16[3072,128]{1,0:T(8,128)(2,1)S(1)}, bf16[3072,128]{1,0:T(8,128)(2,1)}, u32[]{:S(2)}) copy-start(bf16[3072,128]{1,0:T(8,128)(2,1)} %final_ref.3) | copy-start | bytes 2359300
  44.4 18.3 %copy-start.3 = (f32[2,64,128]{2,1,0:T(8,128)S(1)}, f32[2,64,128]{2,1,0:T(8,128)}, u32[]{:S(2)}) copy-start(f32[2,64,128]{2,1,0:T(8,128)} %fresh_ref.3) | copy-start | bytes 196612
  44.4 18.3 %copy-start.4 = (f32[3072]{0:T(1024)S(1)}, f32[3072]{0:T(1024)}, u32[]{:S(2)}) copy-start(f32[3072]{0:T(1024)} %param.25) | copy-start | bytes 36868
  60.9 1.8 %collective-permute-start.4 = (bf16[64,3072]{1,0:T(8,128)(2,1)S(1)}, bf16[64,3072]{1,0:T(8,128)(2,1)S(1)}, u32[]{:S(2)}, u32[]{:S(2)}) collective-permute-start(bf16[64,3072]{1,0:T(8,128)(2,1)S(1)} %get-tuple-element.104), channel_id=1, source_target_pairs={{0,1},{1,0},{2,3},{3,2},{4,5},{5,4},{6,7},{7,6},{8,9},{9,8},{10,11... | collective-permute-start | bytes 1179656 | tf_op jit(solution)/shard_map/ppermute | solution.py:599
  74.3 2.7 %collective-permute-start.6 = (bf16[8,64,128]{2,1,0:T(8,128)(2,1)S(1)}, bf16[8,64,128]{2,1,0:T(8,128)(2,1)S(1)}, u32[]{:S(2)}, u32[]{:S(2)}) collective-permute-start(bf16[8,64,128]{2,1,0:T(8,128)(2,1)S(1)} %all_to_all.11.refs_1_.refs_9_), channel_id=1, source_target_pairs={{0,1},{1,0},{2,3},{3,2},{4,5},{5,4},{6,7},{7,6},{8,9},{9,8},{10,11... | collective-permute-start | bytes 393224 | tf_op jit(solution)/shard_map/ppermute | solution.py:599
  74.3 8.0 %collective-permute-start.5 = (bf16[8,64,128]{2,1,0:T(8,128)(2,1)S(1)}, bf16[8,64,128]{2,1,0:T(8,128)(2,1)S(1)}, u32[]{:S(2)}, u32[]{:S(2)}) collective-permute-start(bf16[8,64,128]{2,1,0:T(8,128)(2,1)S(1)} %all_to_all.11.refs_1_.refs_9_), channel_id=1, source_target_pairs={{0,16},{16,32},{32,48},{48,64},{64,80},{80,96},{96,112},{112,0},{1... | collective-permute-start | bytes 393224 | tf_op jit(solution)/shard_map/ppermute | solution.py:595
  82.3 1.3 %collective-permute-start.7 = (bf16[8,64,128]{2,1,0:T(8,128)(2,1)S(1)}, bf16[8,64,128]{2,1,0:T(8,128)(2,1)S(1)}, u32[]{:S(2)}, u32[]{:S(2)}) collective-permute-start(bf16[8,64,128]{2,1,0:T(8,128)(2,1)S(1)} %collective-permute-done.5.block_ref), channel_id=1, source_target_pairs={{0,1},{1,0},{2,3},{3,2},{4,5},{5,4},{6,7},{7,6},{8,9},{9,8},{10,11... | collective-permute-start | bytes 393224 | tf_op jit(solution)/shard_map/ppermute | solution.py:599
  100.1 1.8 %collective-permute-start.8 = (bf16[64,3072]{1,0:T(8,128)(2,1)S(1)}, bf16[64,3072]{1,0:T(8,128)(2,1)S(1)}, u32[]{:S(2)}, u32[]{:S(2)}) collective-permute-start(bf16[64,3072]{1,0:T(8,128)(2,1)S(1)} %get-tuple-element.132), channel_id=1, source_target_pairs={{0,1},{1,0},{2,3},{3,2},{4,5},{5,4},{6,7},{7,6},{8,9},{9,8},{10,11... | collective-permute-start | bytes 1179656 | tf_op jit(solution)/shard_map/ppermute | solution.py:599
  102.9 5.5 %collective-permute-start.9 = (f32[64,128]{1,0:T(8,128)S(1)}, f32[64,128]{1,0:T(8,128)S(1)}, u32[]{:S(2)}, u32[]{:S(2)}) collective-permute-start(f32[64,128]{1,0:T(8,128)S(1)} %get-tuple-element.133), channel_id=1, source_target_pairs={{0,96},{16,112},{32,0},{48,16},{64,32},{80,48},{96,64},{112,80},{1... | collective-permute-start | bytes 98312 | tf_op jit(solution)/shard_map/ppermute | solution.py:595
  104.4 3.9 %collective-permute-start.10 = (f32[64,128]{1,0:T(8,128)S(1)}, f32[64,128]{1,0:T(8,128)S(1)}, u32[]{:S(2)}, u32[]{:S(2)}) collective-permute-start(f32[64,128]{1,0:T(8,128)S(1)} %get-tuple-element.134), channel_id=1, source_target_pairs={{0,112},{16,0},{32,16},{48,32},{64,48},{80,64},{96,80},{112,96},{1... | collective-permute-start | bytes 98312 | tf_op jit(solution)/shard_map/ppermute | solution.py:595
